TPU v7x, 32 devices: a whole 2x2x4 slice. The times are simulated.
32 devices in a mesh: macro: 8 (over z, y), pool: 4 (over x, core).
Axes of the slice: x: 2, y: 2, z: 4, core: 2. Of those that a mesh axis runs over, the one named last changes fastest.
Arguments:
- history: float32 [729, 16384], P(None, ('macro', 'pool')), may hold values from -6 to 6
- yield_flags: int32 [729, 16384], P(None, ('macro', 'pool')), may hold values 0 or 1
- strain: float32 [6, 16384], P(None, ('macro', 'pool')), may hold values from -6 to 6
- qp_to_rve: int32 [32, 512], P(('macro', 'pool')), may hold values from 0 to 511, each once within a row
- new_owner: int32 [16384, 1], P(('macro', 'pool')), may hold values from 0 to 31; in each aligned block of 512 rows (0 to 511, 512 to 1023, ...) at most 32 rows name the same one
- stiffness: float32 [9, 9, 81, 81], replicated, as said below
- pattern: int32 [9, 9], replicated, may hold values from 0 to 1, as said below
- coupling: float32 [3, 6, 729], replicated, as said below
- plastic_dir: float32 [3, 729], replicated, may hold values from -6 to 6
Outputs:
- new_history: float32 [729, 32768], P(None, ('macro', 'pool'))
- stress: float32 [6, 16384], P(None, ('macro', 'pool'))
Inputs may be any that keep to these rules, and one draw needn't show every extreme that they name: `new_owner`: among the rows of one device no owner is named more than 32 times, a bound that some block reaches. `qp_to_rve`: each row is a permutation of 0 to 511. `pattern`: Symmetric, with ones on the diagonal. stiffness[a, b] is the transpose of stiffness[b, a]; diagonal entries of diagonal blocks lie in 0.5 to 1.5, all others in 0 to 0.032. `coupling`: entries lie in -5.7 to 6.3.
All inputs are finite; a program needn't handle non-finite values. No bound on the sum of `yield_flags` on one device may be relied on, other than what follows from the above.
Results may differ from a plain program's by a relative error of at most 0.0003.
Values sent between devices are 32-bit elements; how exact they have to be, the bound alone decides.
No kernel may reach another device: no remote copies, remote signals or barrier semaphores. Data moves between devices by JAX's collectives and lax.ppermute only.
A program may use at most 128 MiB of HBM per device.

v0:
```python
import functools
import math

import jax
import jax.numpy as jnp
from jax import lax
from jax.experimental import pallas as pl
from jax.experimental.pallas import tpu as pltpu
from jax.sharding import PartitionSpec as P

ITERS = 3
LANES = 128
PLANES = 4
PATTERN = 32

NN = (((1,), (0,)), ((), ()))
NT = (((1,), (1,)), ((), ()))
TN = (((0,), (0,)), ((), ()))


def up(value, unit):
    return -(-value // unit) * unit


def dot(a, b, dims=NN):
    return lax.dot_general(a, b, dims, preferred_element_type=jnp.float32)


def halves(x):
    hi = x.astype(jnp.bfloat16)
    lo = (x - hi.astype(jnp.float32)).astype(jnp.bfloat16)
    return hi, lo


def whereabouts(devices):
    me = lax.axis_index("macro") * lax.axis_size("pool") + lax.axis_index("pool")
    lanes = devices // PLANES
    return me, me // lanes, me % lanes, lanes


def hot(row, count):
    rows = lax.broadcasted_iota(jnp.int32, (count, row.shape[1]), 0)
    return jnp.where(rows == row, 1.0, 0.0).astype(jnp.bfloat16)


def pack_kernel(coupling, plastic, strain, owner, qp, pattern, small):
    top = 0
    for c in range(coupling.shape[0]):
        small[top:top + coupling.shape[1], :] = coupling[c]
        top += coupling.shape[1]
    for part in (plastic, strain, owner, qp):
        small[top:top + part.shape[0], 0:part.shape[1]] = part[...].astype(jnp.float32)
        top += part.shape[0]
    count = pattern.shape[0]
    for a in range(count):
        for b in range(count):
            couples = jnp.full((1, LANES), pattern[a, b].astype(jnp.float32))
            small[PATTERN + a * count + b:PATTERN + a * count + b + 1, 0:LANES] = couples


def prep_kernel(devices, per_peer, comps, voigt, *refs):
    sources, outs, (kfull, pad), local, sem = refs[:4], refs[4:13], refs[13:15], refs[15:19], refs[19]
    khi, klo, hist_s, weight_s, strain_s, place_s, qp_s, cstack, pdir = outs
    small, stiff, hist, flag = local
    copies = [
        pltpu.make_async_copy(source, target, sem.at[i])
        for i, (source, target) in enumerate(zip(sources, local))
    ]
    for copy in copies:
        copy.start()
    nodes, columns = hist.shape
    nb, blk = stiff.shape[0], stiff.shape[2]
    at_plastic = comps * voigt
    at_strain = at_plastic + comps
    at_owner = at_strain + voigt
    copies[0].wait()

    me, plane, lane, lanes = whereabouts(devices)
    owner = small[at_owner:at_owner + 1, 0:columns].astype(jnp.int32)
    apart = owner // lanes ^ plane
    target = owner % lanes
    away = target ^ lane
    hopping = (away % 2 * 2 + jnp.where(apart == 2, 0, 1)) * (lanes // 2) + away // 2
    staying = jnp.where(apart == 3, 2, 3) * lanes + target
    key = jnp.where((apart == 2) | (apart == 1), hopping, staying)
    key_ids = lax.broadcasted_iota(jnp.int32, (devices, columns), 0)
    mine = jnp.where(key_ids == key, 1.0, 0.0)
    earlier = jnp.where(
        lax.broadcasted_iota(jnp.int32, (columns, columns), 0)
        < lax.broadcasted_iota(jnp.int32, (columns, columns), 1), 1.0, 0.0
    ).astype(jnp.bfloat16)
    before = dot(mine.astype(jnp.bfloat16), earlier)
    rank = jnp.sum(before * mine, axis=0, keepdims=True)
    tally = jnp.sum(mine, axis=1, keepdims=True)
    ahead = jnp.where(key_ids < key, tally, 0.0)
    position = (rank + jnp.sum(ahead, axis=0, keepdims=True)).astype(jnp.int32)

    order = hot(position, columns)
    pad[...] = jnp.zeros_like(pad)
    pad[0:1, :] = key.astype(jnp.float32)
    pad[1:2, :] = rank
    placed = dot(pad[...].astype(jnp.bfloat16), order, NT)
    place_s[...] = jnp.broadcast_to(
        (placed[0:1, :] * per_peer + placed[1:2, :]).astype(jnp.int32), place_s.shape
    )

    pad[0:1, :] = (position // 256).astype(jnp.float32)
    pad[1:2, :] = (position % 256).astype(jnp.float32)
    found = dot(pad[...].astype(jnp.bfloat16), hot(small[at_owner + 1:at_owner + 2, 0:columns].astype(jnp.int32), columns))
    at = (found[0:1, :] * 256.0 + found[1:2, :]).astype(jnp.int32)
    qp_s[...] = jnp.broadcast_to(at, qp_s.shape)
    pad[...] = jnp.zeros_like(pad)
    pad[0:voigt, :] = small[at_strain:at_owner, 0:columns]
    hi, lo = halves(pad[...])
    serves = hot(at, columns)
    strain_s[...] = dot(hi, serves, NT) + dot(lo, serves, NT)

    kfull[...] = jnp.zeros_like(kfull)
    copies[1].wait()
    for a in range(nb):
        for b in range(nb):
            kfull[a * blk:(a + 1) * blk, b * blk:(b + 1) * blk] = (
                stiff[a, b] * small[PATTERN + a * nb + b:PATTERN + a * nb + b + 1, 0:blk]
            )
    k = kfull[...]
    kh = k.astype(jnp.bfloat16)
    khi[...] = kh
    klo[...] = (k - kh.astype(jnp.float32)).astype(jnp.bfloat16)

    copies[2].wait()
    copies[3].wait()
    hi, lo = halves(hist[...])
    hist_s[...] = jnp.zeros_like(hist_s)
    hist_s[0:nodes, :] = dot(hi, order, NT) + dot(lo, order, NT)
    h = hist_s[...]
    weight_s[...] = jnp.zeros_like(weight_s)
    weight_s[0:nodes, :] = dot(flag[...].astype(jnp.float32).astype(jnp.bfloat16), order, NT)
    weight_s[...] = weight_s[...] * h * h / (1.0 + h * h)

    cstack[...] = jnp.zeros_like(cstack)
    for c in range(comps):
        cpl = small[c * voigt:(c + 1) * voigt, :]
        hi = cpl.astype(jnp.bfloat16).astype(jnp.float32)
        cstack[c, 0:voigt, 0:nodes] = hi
        cstack[c, 8:8 + voigt, 0:nodes] = hi
        cstack[c, 16:16 + voigt, 0:nodes] = cpl - hi
    pdir[...] = jnp.zeros_like(pdir)
    for c in range(comps):
        spread = jnp.broadcast_to(small[at_plastic + c:at_plastic + c + 1, :], (LANES, nodes))
        pdir[c, 0:nodes, :] = jnp.transpose(spread)


def row_blocks(rows, span):
    pieces = 4 * span // LANES
    cuts = [rows // 16 * i // pieces * 16 for i in range(pieces + 1)]
    return [slice(top, end) for top, end in zip(cuts, cuts[1:])]


def sweep(rows, comps, span):
    for r in row_blocks(rows, span):
        for c in range(comps):
            yield r, slice(c * span, (c + 1) * span), c


def fold(x):
    return jnp.sum(x.reshape(x.shape[0] // 8, 8, x.shape[1]), axis=0)


def total(parts):
    return jnp.sum(parts, axis=0, keepdims=True)


def solve_kernel(scale, first, earlier, khi, klo, hist, weight, strain, cstack, pdir, place, *refs):
    earlier_updated, refs = refs[:earlier], refs[earlier:]
    updated, stress, blocks = refs[0], refs[1], refs[2:-5]
    field, resid, image, solved, split = refs[-5:]
    rows, span = hist.shape
    comps = pdir.shape[0]
    wide = comps * span
    zero = jnp.zeros((8, span), jnp.float32)

    def flow(c, r):
        return jnp.concatenate([pdir[c, r, :]] * (span // LANES), axis=1)

    def keep(r, c, x):
        split[r, c * span:(c + 1) * span], split[r, wide + c * span:wide + (c + 1) * span] = (
            halves(x)
        )

    s = strain[...]
    s_hi = s.astype(jnp.bfloat16).astype(jnp.float32)
    s3 = jnp.concatenate([s_hi, s - s_hi, s_hi, jnp.zeros_like(s)], axis=0).astype(jnp.bfloat16)
    split[rows:, :] = jnp.zeros((split.shape[0] - rows, 2 * wide), jnp.bfloat16)
    for c in range(comps):
        image[:, c * span:(c + 1) * span] = dot(cstack[c].astype(jnp.bfloat16), s3, TN)
    parts = zero
    for r, l, c in sweep(rows, comps, span):
        d = image[r, l] - weight[r, :] * hist[r, :] * flow(c, r)
        resid[r, l] = d
        field[r, l] = d
        keep(r, c, d)
        parts = parts + fold(d * d)
    norm = total(parts)
    solved[...] = jnp.zeros_like(solved)

    def step_length(norm):
        parts = zero
        for r in row_blocks(rows, span):
            both = dot(khi[r, :], split[...])
            low = dot(klo[r, :], split[:, 0:wide])
            tangent = 1.5 - weight[r, :]
            for c in range(comps):
                l = slice(c * span, (c + 1) * span)
                d = field[r, l]
                q = both[:, l] + both[:, wide + c * span:wide + (c + 1) * span] + low[:, l]
                q = q + tangent * d
                image[r, l] = q
                parts = parts + fold(d * q)
        return norm / jnp.maximum(total(parts), 1.0)

    def step(_, norm):
        alpha = step_length(norm)
        parts = zero
        for r, l, c in sweep(rows, comps, span):
            solved[r, l] = solved[r, l] + alpha * field[r, l]
            left = resid[r, l] - alpha * image[r, l]
            resid[r, l] = left
            parts = parts + fold(left * left)
        following = total(parts)
        beta = following / jnp.maximum(norm, 1.0)
        for r, l, c in sweep(rows, comps, span):
            d = resid[r, l] + beta * field[r, l]
            field[r, l] = d
            keep(r, c, d)
        return following

    alpha = step_length(lax.fori_loop(0, ITERS - 1, step, norm))
    for r, l, c in sweep(rows, comps, span):
        x = solved[r, l] + alpha * field[r, l]
        pushed = flow(c, r) * x
        image[r, 0:span] = pushed if c == 0 else image[r, 0:span] + pushed
        keep(r, c, (1.5 - weight[r, :]) * x)
    updated[...] = hist[...] + weight[...] * image[:, 0:span]
    top, count = 0, sum(block.shape[0] for block in blocks)
    sent = placed_rows(first, count, place, [*earlier_updated, updated])
    for block in blocks:
        put(block, 0, sent[top:top + block.shape[0]])
        top += block.shape[0]
    out = s
    for c in range(comps):
        cpl = cstack[c].astype(jnp.bfloat16)
        main = dot(cpl, split[0:rows, c * span:(c + 1) * span])
        minor = dot(cpl, split[0:rows, wide + c * span:wide + (c + 1) * span])
        out = out + scale * (main[0:8] + main[16:24] + minor[0:8])
    stress[...] = out


def placed_rows(first, count, place, sources):
    width = sum(source.shape[1] for source in sources)
    placing = hot(place[0:1, 0:width] - first, count)
    sums, left = 0.0, 0
    for source in sources:
        hi, lo = halves(source[...])
        cut = placing[:, left:left + source.shape[1]]
        sums = sums + (dot(cut, hi, NT) + dot(cut, lo, NT))
        left += source.shape[1]
    return sums


def put(block, top, rows):
    height, filled = rows.shape
    block[pl.ds(top, height), 0:filled] = rows
    rest = jnp.zeros((height, block.shape[1] - filled), jnp.float32)
    block[pl.ds(top, height), filled:] = rest


def ship_kernel(devices, first, chunks, place, at, *refs):
    updated, stress, (pair, out) = refs[:chunks], refs[chunks:2 * chunks], refs[2 * chunks:]
    me, plane, lane, lanes = whereabouts(devices)
    group = pair.shape[0] // 2
    rows = placed_rows(first, 2 * group, place, updated)
    put(pair, pl.multiple_of((1 - plane // 2) * group, group), rows[0:group])
    put(pair, pl.multiple_of(plane // 2 * group, group), rows[group:])
    hi, lo = halves(jnp.concatenate([ref[...] for ref in stress], axis=1))
    serves = hot(at[0:1, :], hi.shape[1])
    out[...] = (dot(hi, serves) + dot(lo, serves))[0:out.shape[0], :]


def join_kernel(cap, *refs):
    landed, blocks = refs[:3], refs[3:]
    for i, block in enumerate(blocks):
        for k, rows in enumerate(landed):
            block[k * cap:(k + 1) * cap, :] = rows[i * cap:(i + 1) * cap, :]


def land(tile, out, stage, sem, slot, at):
    nodes = out.shape[0]
    stage[slot] = jnp.transpose(tile)[0:nodes, :]
    columns = pl.multiple_of(at * LANES, LANES)
    copy = pltpu.make_async_copy(stage.at[slot], out.at[:, pl.ds(columns, LANES)], sem.at[slot])
    copy.start()
    return copy


def land_group(block, count, plane, out, stage, sem, slot):
    height = block.shape[0] // count
    copies = []
    for part in range(count):
        tile = block[part * height:(part + 1) * height, :]
        copies.append(land(tile, out, stage, sem, slot + part, plane * count + part))
    return copies


def land_kernel(devices, cap, pair, *refs):
    blocks, (out, stage, sem, gather) = refs[:-4], refs[-4:]
    me, plane, lane, lanes = whereabouts(devices)
    group = pair.shape[0] // 2
    copies = []
    for part in range(2):
        source = jnp.where(plane // 2 == part, plane, plane ^ 3)
        block = pair.at[part * group:(part + 1) * group, :]
        copies += land_group(block, 2, source, out, stage, sem, 2 * part)
    for i, apart in enumerate((2, 1)):
        for k in range(lanes):
            at = pl.multiple_of((lane ^ k) * cap, cap)
            if i == 1 and k % 2 == 1:
                gather[i, pl.ds(at, cap), :] = blocks[lanes // 2 + k // 2][...]
            else:
                top = (2 * (k % 2) + i) * cap
                gather[i, pl.ds(at, cap), :] = blocks[k // 2][top:top + cap, :]
        copies += land_group(gather.at[i], 2, plane ^ apart, out, stage, sem, 4 + 2 * i)
    for copy in copies:
        copy.wait()


def params(mib=24):
    return pltpu.CompilerParams(vmem_limit_bytes=mib * 2**20)


def shards(
    history, yield_flags, strain, qp_to_rve, new_owner, stiffness, pattern, coupling, plastic_dir
):
    devices = lax.axis_size(("macro", "pool"))
    nodes, columns = history.shape
    comps, voigt = coupling.shape[0], coupling.shape[1]
    per_peer = 2 * columns // devices
    rows = up(nodes, 32)
    deep = up(nodes, 256)
    f32, bf16, i32 = jnp.float32, jnp.bfloat16, jnp.int32
    vmem = pl.BlockSpec(memory_space=pltpu.VMEM)
    small_inputs = (coupling, plastic_dir, strain, new_owner.reshape(1, columns), qp_to_rve, pattern)
    small = pl.pallas_call(
        pack_kernel,
        out_shape=jax.ShapeDtypeStruct((up(PATTERN + pattern.size, 8), nodes), f32),
        in_specs=[vmem] * 5 + [pl.BlockSpec(memory_space=pltpu.SMEM)],
        out_specs=vmem,
        compiler_params=params(60),
    )(*small_inputs)
    inputs = (small, stiffness, history, yield_flags)
    khi, klo, hist_s, weight_s, strain_s, place_s, qp_s, cstack, pdir = pl.pallas_call(
        functools.partial(prep_kernel, devices, per_peer, comps, voigt),
        out_shape=(
            jax.ShapeDtypeStruct((rows, deep), bf16),
            jax.ShapeDtypeStruct((rows, deep), bf16),
            jax.ShapeDtypeStruct((rows, columns), f32),
            jax.ShapeDtypeStruct((rows, columns), f32),
            jax.ShapeDtypeStruct((8, columns), f32),
            jax.ShapeDtypeStruct((8, columns), i32),
            jax.ShapeDtypeStruct((8, columns), i32),
            jax.ShapeDtypeStruct((comps, 32, rows), f32),
            jax.ShapeDtypeStruct((comps, rows, LANES), f32),
        ),
        in_specs=[pl.BlockSpec(memory_space=pltpu.HBM)] * 4,
        out_specs=[vmem] * 9,
        scratch_shapes=[pltpu.VMEM((rows, deep), f32), pltpu.VMEM((8, columns), f32)]
        + [pltpu.VMEM(x.shape, x.dtype) for x in inputs]
        + [pltpu.SemaphoreType.DMA((4,))],
        compiler_params=params(46),
    )(*inputs)

    lanes = devices // PLANES
    half = lanes // 2
    group = lanes * per_peer
    block = lambda height: jax.ShapeDtypeStruct((height, deep), f32)
    whole = lambda shape: pl.BlockSpec(shape, lambda i: (0,) * len(shape))
    updated, stress_s, ready = [], [], []
    left = 0
    for span in (LANES,) * (columns // LANES):
        part = lambda height: pl.BlockSpec((height, span), lambda i, at=left // span: (0, at))
        wide = comps * span
        outs = [block(LANES)] if len(updated) < 3 else [block(per_peer)] * half
        done = pl.pallas_call(
            functools.partial(solve_kernel, 1.0 / math.sqrt(comps * nodes), left, len(updated)),
            grid=(1,),
            out_shape=(
                jax.ShapeDtypeStruct((rows, span), f32),
                jax.ShapeDtypeStruct((8, span), f32),
                *outs,
            ),
            in_specs=[whole((rows, deep)), whole((rows, deep)), part(rows), part(rows), part(8),
                      whole((comps, 32, rows)), whole((comps, rows, LANES)), whole((8, columns))]
            + [whole(u.shape) for u in updated],
            out_specs=[whole((rows, span)), whole((8, span))] + [whole(o.shape) for o in outs],
            scratch_shapes=[pltpu.VMEM((rows, wide), f32) for _ in range(4)]
            + [pltpu.VMEM((deep, 2 * wide), bf16)],
            compiler_params=params(),
            cost_estimate=pl.CostEstimate(
                flops=18 * rows * deep * wide, bytes_accessed=2**20, transcendentals=0
            ),
        )(khi, klo, hist_s, weight_s, strain_s, cstack, pdir, place_s, *updated)
        updated.append(done[0])
        stress_s.append(done[1])
        ready.append(done[2:])
        left += span
    pair, stress_out = pl.pallas_call(
        functools.partial(ship_kernel, devices, 2 * group, len(updated)),
        out_shape=(block(2 * group), jax.ShapeDtypeStruct((voigt, columns), f32)),
        in_specs=[vmem] * (2 + 2 * len(updated)),
        out_specs=[vmem] * 2,
        compiler_params=params(),
        cost_estimate=pl.CostEstimate(
            flops=4 * rows * columns * columns, bytes_accessed=2**20, transcendentals=0
        ),
    )(place_s, qp_s, *updated, *stress_s)

    axes = ("macro", "pool")

    def hop(sent, mask):
        return lax.ppermute(sent, axes, [(s, s ^ mask) for s in range(devices)])

    pair, *straight = lax.optimization_barrier((pair, *ready[-1]))
    planes = [list(range(z * lanes, (z + 1) * lanes)) for z in range(PLANES)]
    pair = lax.all_to_all(
        pair.reshape(2 * lanes, per_peer, deep), axes, split_axis=0, concat_axis=0, tiled=True,
        axis_index_groups=[planes[0] + planes[3], planes[1] + planes[2]],
    ).reshape(2 * group, deep)
    hops = (2 * lanes, lanes, 2 * lanes + 1)
    landed = []
    for (sent,), mask in zip(ready, hops):
        landed.append(hop(sent, mask))
        landed[-2:] = lax.optimization_barrier(tuple(landed[-2:]))
    joined = pl.pallas_call(
        functools.partial(join_kernel, per_peer),
        out_shape=(block(3 * per_peer),) * half,
        in_specs=[vmem] * 3,
        out_specs=[vmem] * half,
        compiler_params=params(),
        cost_estimate=pl.CostEstimate(flops=2**40, bytes_accessed=2**20, transcendentals=0),
    )(*landed)
    joined = [sent if i == 0 else hop(sent, 2 * i) for i, sent in enumerate(joined)]
    direct = [hop(sent, lanes + 2 * i + 1) for i, sent in enumerate(straight)]
    new_history = pl.pallas_call(
        functools.partial(land_kernel, devices, per_peer),
        out_shape=jax.ShapeDtypeStruct((nodes, devices * per_peer), f32),
        in_specs=[vmem] * (1 + 2 * half),
        out_specs=pl.BlockSpec(memory_space=pl.ANY),
        scratch_shapes=[pltpu.VMEM((8, nodes, LANES), f32), pltpu.SemaphoreType.DMA((8,)),
                        pltpu.VMEM((2, group, deep), f32)],
        compiler_params=params(),
    )(pair, *joined, *direct)
    return (new_history, stress_out)


def solution(mesh):
    return jax.shard_map(
        shards,
        mesh=mesh,
        in_specs=(
            P(None, ("macro", "pool")),
            P(None, ("macro", "pool")),
            P(None, ("macro", "pool")),
            P(("macro", "pool"), None),
            P(("macro", "pool"), None),
            P(),
            P(),
            P(),
            P(),
        ),
        out_specs=(P(None, ("macro", "pool")), P(None, ("macro", "pool"))),
        check_vma=False,
    )
```

profile of v0, /device:TPU:0, one launch (start us, length us, event | category | flops | bytes accessed | tf_op | source)
XLA Modules:
  0.0 98.3 jit_solution(5987846286910314447)
XLA Ops:
  0.6 1.7 %shard_map.104.refs_0_ = f32[120,729]{1,0:T(8,128)} custom-call(f32[3,6,729]{2,1,0:T(8,128)} %coupling.1, f32[3,729]{1,0:T(4,128)} %plastic.1, f32[6,512]{1,0:T(8,128)} %strain.1, s32[1,512]{1,0:T(1,128)} %bitcast.3, s32[1,512]{1,0:T(1,128)} %qp.1, s32[9,9]{1,0:T(8,128)} %pattern.1), custom_call_target="tpu_custom_call" | custom-call | tf_op jit(solution)/shard_map/pallas_call | solution.py:352
  2.4 1.0 %copy-done = f32[120,729]{1,0:T(8,128)S(1)} copy-done((f32[120,729]{1,0:T(8,128)S(1)}, f32[120,729]{1,0:T(8,128)}, u32[]{:S(2)}) %copy-start) | copy-done | bytes 349944
  3.3 4.7 %shard_map.105 = (bf16[736,768]{1,0:T(8,128)(2,1)S(1)}, bf16[736,768]{1,0:T(8,128)(2,1)S(1)}, f32[736,512]{1,0:T(8,128)S(1)}, f32[736,512]{1,0:T(8,128)S(1)}, f3...) custom-call(f32[120,729]{1,0:T(8,128)S(1)} %copy-done, ...), custom_call_target="tpu_custom_call" | custom-call | tf_op jit(solution)/shard_map/pallas_call | solution.py:360
  8.1 8.0 %shard_map.106 = (f32[736,128]{1,0:T(8,128)S(1)}, f32[8,128]{1,0:T(8,128)S(1)}, f32[128,768]{1,0:T(8,128)S(1)}) custom-call(bf16[736,768]{1,0:T(8,128)(2,1)S(1)} %get-tuple-element.43.khi, bf16[736,768]{1,0:T(8,128)(2,1)S(1)} %get-tuple-element.44.klo, f32[736,512]{1,0:T(8,128)S(1)} %get-tuple-element.45.hist, f32[736,512]{1,0:T(8,128)S(1)} %get-tuple-element.46.weight, ...), custom_call_target="tpu_custom_call" | custom-call | flops 3906994176 | bytes 1048576 | tf_op jit(solution)/shard_map/pallas_call | solution.py:392
  16.1 4.1 %collective-permute-start = (f32[128,768]{1,0:T(8,128)S(1)}, f32[128,768]{1,0:T(8,128)S(1)}, u32[]{:S(2)}, u32[]{:S(2)}) collective-permute-start(f32[128,768]{1,0:T(8,128)S(1)} %get-tuple-element.64), channel_id=1, source_target_pairs={{0,16},{1,17},{2,18},{3,19},{4,20},{5,21},{6,22},{7,23},{8,24},{9,... | collective-permute-start | bytes 1179656 | tf_op jit(solution)/shard_map/ppermute | solution.py:429
  20.2 8.4 %shard_map.107 = (f32[736,128]{1,0:T(8,128)S(1)}, f32[8,128]{1,0:T(8,128)S(1)}, f32[128,768]{1,0:T(8,128)S(1)}) custom-call(bf16[736,768]{1,0:T(8,128)(2,1)S(1)} %get-tuple-element.43.khi, bf16[736,768]{1,0:T(8,128)(2,1)S(1)} %get-tuple-element.44.klo, f32[736,512]{1,0:T(8,128)S(1)} %get-tuple-element.45.hist, f32[736,512]{1,0:T(8,128)S(1)} %get-tuple-element.46.weight, ...), custom_call_target="tpu_custom_call" | custom-call | flops 3906994176 | bytes 1048576 | tf_op jit(solution)/shard_map/pallas_call | solution.py:392
  28.7 1.6 %collective-permute-start.1 = (f32[128,768]{1,0:T(8,128)S(1)}, f32[128,768]{1,0:T(8,128)S(1)}, u32[]{:S(2)}, u32[]{:S(2)}) collective-permute-start(f32[128,768]{1,0:T(8,128)S(1)} %get-tuple-element.65), channel_id=1, source_target_pairs={{0,8},{1,9},{2,10},{3,11},{4,12},{5,13},{6,14},{7,15},{8,0},{9,1},... | collective-permute-start | bytes 1179656 | tf_op jit(solution)/shard_map/ppermute | solution.py:429
  30.3 8.4 %shard_map.108 = (f32[736,128]{1,0:T(8,128)S(1)}, f32[8,128]{1,0:T(8,128)S(1)}, f32[128,768]{1,0:T(8,128)S(1)}) custom-call(bf16[736,768]{1,0:T(8,128)(2,1)S(1)} %get-tuple-element.43.khi, bf16[736,768]{1,0:T(8,128)(2,1)S(1)} %get-tuple-element.44.klo, f32[736,512]{1,0:T(8,128)S(1)} %get-tuple-element.45.hist, f32[736,512]{1,0:T(8,128)S(1)} %get-tuple-element.46.weight, ...), custom_call_target="tpu_custom_call" | custom-call | flops 3906994176 | bytes 1048576 | tf_op jit(solution)/shard_map/pallas_call | solution.py:392
  38.7 8.7 %shard_map.109 = (f32[736,128]{1,0:T(8,128)S(1)}, f32[8,128]{1,0:T(8,128)S(1)}, f32[32,768]{1,0:T(8,128)S(1)}, f32[32,768]{1,0:T(8,128)S(1)}, f32[32,768]{1,0:T(8,128)S(1)}, /*index=5*/f32[32,768]{1,0:T(8,128)S(1)}) custom-call(bf16[736,768]{1,0:T(8,128)(2,1)S(1)} %get-tuple-element.43.khi, bf16[736,768]{1,0:T(8,128)(2,1)S(1)} %get-tuple-element.44.klo, ...), custom_call_target="tpu_custom_call" | custom-call | flops 3906994176 | bytes 1048576 | tf_op jit(solution)/shard_map/pallas_call | solution.py:392
  47.5 3.1 %shard_map.110 = (f32[512,768]{1,0:T(8,128)}, f32[6,512]{1,0:T(8,128)}) custom-call(s32[8,512]{1,0:T(8,128)S(1)} %get-tuple-element.41.place, s32[8,512]{1,0:T(8,128)S(1)} %get-tuple-element.42.at, f32[736,128]{1,0:T(8,128)S(1)} %get-tuple-element.50.refs_0_, f32[736,128]{1,0:T(8,128)S(1)} %get-tuple-element.51.refs_1_, ...), custom_call_target="tpu_custom_call" | custom-call | flops 771751936 | bytes 1048576 | tf_op jit(solution)/shard_map/pallas_call | solution.py:415
  50.6 5.8 %all-to-all-start = ((f32[16,32,768]{2,1,0:T(8,128)}), f32[16,32,768]{2,1,0:T(8,128)}, u32[]{:S(2)}, u32[]{:S(2)}) async-start(f32[16,32,768]{2,1,0:T(8,128)} %bitcast.1), calls=%async_computation | async-start | bytes 3145728 | tf_op jit(solution)/shard_map/all_to_all | solution.py:433
  56.4 2.4 %collective-permute-done.2.refs_2_ = f32[128,768]{1,0:T(8,128)S(1)} collective-permute-done((f32[128,768]{1,0:T(8,128)S(1)}, f32[128,768]{1,0:T(8,128)S(1)}, u32[]{:S(2)}, u32[]{:S(2)}) %collective-permute-start.2) | collective-permute-done | bytes 393248 | tf_op jit(solution)/shard_map/ppermute | solution.py:429
  58.9 1.6 %collective-permute-start.3 = (f32[96,768]{1,0:T(8,128)S(1)}, f32[96,768]{1,0:T(8,128)S(1)}, u32[]{:S(2)}, u32[]{:S(2)}) collective-permute-start(f32[96,768]{1,0:T(8,128)S(1)} %get-tuple-element.72), channel_id=1, source_target_pairs={{0,2},{1,3},{2,0},{3,1},{4,6},{5,7},{6,4},{7,5},{8,10},{9,11},{10,... | collective-permute-start | bytes 884744 | tf_op jit(solution)/shard_map/ppermute | solution.py:429
  60.4 1.5 %collective-permute-start.4 = (f32[96,768]{1,0:T(8,128)S(1)}, f32[96,768]{1,0:T(8,128)S(1)}, u32[]{:S(2)}, u32[]{:S(2)}) collective-permute-start(f32[96,768]{1,0:T(8,128)S(1)} %get-tuple-element.73), channel_id=1, source_target_pairs={{0,4},{1,5},{2,6},{3,7},{4,0},{5,1},{6,2},{7,3},{8,12},{9,13},{10,... | collective-permute-start | bytes 884744 | tf_op jit(solution)/shard_map/ppermute | solution.py:429
  62.0 0.5 collective-permute-start.5
  62.4 2.7 %collective-permute-start.7 = (f32[32,768]{1,0:T(8,128)S(1)}, f32[32,768]{1,0:T(8,128)S(1)}, u32[]{:S(2)}, u32[]{:S(2)}) collective-permute-start(f32[32,768]{1,0:T(8,128)S(1)} %get-tuple-element.76), channel_id=1, source_target_pairs={{0,11},{1,10},{2,9},{3,8},{4,15},{5,14},{6,13},{7,12},{8,3},{9,2},... | collective-permute-start | bytes 294920 | tf_op jit(solution)/shard_map/ppermute | solution.py:429
  65.1 15.3 %collective-permute-done.6.refs_4_ = f32[32,768]{1,0:T(8,128)S(1)} collective-permute-done((f32[32,768]{1,0:T(8,128)S(1)}, f32[32,768]{1,0:T(8,128)S(1)}, u32[]{:S(2)}, u32[]{:S(2)}) %collective-permute-start.6) | collective-permute-done | bytes 98336 | tf_op jit(solution)/shard_map/ppermute | solution.py:429
  80.4 1.4 %collective-permute-start.8 = (f32[32,768]{1,0:T(8,128)S(1)}, f32[32,768]{1,0:T(8,128)S(1)}, u32[]{:S(2)}, u32[]{:S(2)}) collective-permute-start(f32[32,768]{1,0:T(8,128)S(1)} %get-tuple-element.77), channel_id=1, source_target_pairs={{0,13},{1,12},{2,15},{3,14},{4,9},{5,8},{6,11},{7,10},{8,5},{9,4},... | collective-permute-start | bytes 294920 | tf_op jit(solution)/shard_map/ppermute | solution.py:429
  81.8 1.6 %collective-permute-done.7.refs_5_ = f32[32,768]{1,0:T(8,128)S(1)} collective-permute-done((f32[32,768]{1,0:T(8,128)S(1)}, f32[32,768]{1,0:T(8,128)S(1)}, u32[]{:S(2)}, u32[]{:S(2)}) %collective-permute-start.7) | collective-permute-done | bytes 98336 | tf_op jit(solution)/shard_map/ppermute | solution.py:429
  83.4 1.6 %collective-permute-start.9 = (f32[32,768]{1,0:T(8,128)S(1)}, f32[32,768]{1,0:T(8,128)S(1)}, u32[]{:S(2)}, u32[]{:S(2)}) collective-permute-start(f32[32,768]{1,0:T(8,128)S(1)} %get-tuple-element.78), channel_id=1, source_target_pairs={{0,15},{1,14},{2,13},{3,12},{4,11},{5,10},{6,9},{7,8},{8,7},{9,6},... | collective-permute-start | bytes 294920 | tf_op jit(solution)/shard_map/ppermute | solution.py:429
  85.1 1.6 %collective-permute-done.8.refs_6_ = f32[32,768]{1,0:T(8,128)S(1)} collective-permute-done((f32[32,768]{1,0:T(8,128)S(1)}, f32[32,768]{1,0:T(8,128)S(1)}, u32[]{:S(2)}, u32[]{:S(2)}) %collective-permute-start.8) | collective-permute-done | bytes 98336 | tf_op jit(solution)/shard_map/ppermute | solution.py:429
  86.7 3.6 %collective-permute-done.9.refs_7_ = f32[32,768]{1,0:T(8,128)S(1)} collective-permute-done((f32[32,768]{1,0:T(8,128)S(1)}, f32[32,768]{1,0:T(8,128)S(1)}, u32[]{:S(2)}, u32[]{:S(2)}) %collective-permute-start.9) | collective-permute-done | bytes 98336 | tf_op jit(solution)/shard_map/ppermute | solution.py:429
  90.3 4.5 %collective-permute-done.5.refs_3_ = f32[96,768]{1,0:T(8,128)S(1)} collective-permute-done((f32[96,768]{1,0:T(8,128)S(1)}, f32[96,768]{1,0:T(8,128)S(1)}, u32[]{:S(2)}, u32[]{:S(2)}) %collective-permute-start.5) | collective-permute-done | bytes 294944 | tf_op jit(solution)/shard_map/ppermute | solution.py:429
  94.8 3.3 %shard_map.112 = f32[729,1024]{1,0:T(8,128)} custom-call(f32[512,768]{1,0:T(8,128)} %bitcast.2.pair, f32[96,768]{1,0:T(8,128)S(1)} %get-tuple-element.71.refs_0_, f32[96,768]{1,0:T(8,128)S(1)} %collective-permute-done.3.refs_1_, f32[96,768]{1,0:T(8,128)S(1)} %collective-permute-done.4.refs_2_, f32[96,768]{1,0:T(8,128)S(1)} %collective-permute-done.5.refs_3_, ...), custom_call_target="tpu_custom_call" | custom-call | tf_op jit(solution)/shard_map/pallas_call | solution.py:452
  (9 shorter events, 0.2 us)
Async XLA Ops:
  2.4 1.0 %copy-start = (f32[120,729]{1,0:T(8,128)S(1)}, f32[120,729]{1,0:T(8,128)}, u32[]{:S(2)}) copy-start(f32[120,729]{1,0:T(8,128)} %shard_map.104.refs_0_) | copy-start | bytes 1049764
  16.1 40.3 %collective-permute-start = (f32[128,768]{1,0:T(8,128)S(1)}, f32[128,768]{1,0:T(8,128)S(1)}, u32[]{:S(2)}, u32[]{:S(2)}) collective-permute-start(f32[128,768]{1,0:T(8,128)S(1)} %get-tuple-element.64), channel_id=1, source_target_pairs={{0,16},{1,17},{2,18},{3,19},{4,20},{5,21},{6,22},{7,23},{8,24},{9,... | collective-permute-start | bytes 1179656 | tf_op jit(solution)/shard_map/ppermute | solution.py:429
  28.7 27.7 %collective-permute-start.1 = (f32[128,768]{1,0:T(8,128)S(1)}, f32[128,768]{1,0:T(8,128)S(1)}, u32[]{:S(2)}, u32[]{:S(2)}) collective-permute-start(f32[128,768]{1,0:T(8,128)S(1)} %get-tuple-element.65), channel_id=1, source_target_pairs={{0,8},{1,9},{2,10},{3,11},{4,12},{5,13},{6,14},{7,15},{8,0},{9,1},... | collective-permute-start | bytes 1179656 | tf_op jit(solution)/shard_map/ppermute | solution.py:429
  38.7 20.1 %collective-permute-start.2 = (f32[128,768]{1,0:T(8,128)S(1)}, f32[128,768]{1,0:T(8,128)S(1)}, u32[]{:S(2)}, u32[]{:S(2)}) collective-permute-start(f32[128,768]{1,0:T(8,128)S(1)} %get-tuple-element.68), channel_id=1, source_target_pairs={{0,17},{1,16},{2,19},{3,18},{4,21},{5,20},{6,23},{7,22},{8,25},{9,... | collective-permute-start | bytes 1179656 | tf_op jit(solution)/shard_map/ppermute | solution.py:429
  50.6 44.3 %all-to-all-start = ((f32[16,32,768]{2,1,0:T(8,128)}), f32[16,32,768]{2,1,0:T(8,128)}, u32[]{:S(2)}, u32[]{:S(2)}) async-start(f32[16,32,768]{2,1,0:T(8,128)} %bitcast.1), calls=%async_computation | async-start | bytes 3145728 | tf_op jit(solution)/shard_map/all_to_all | solution.py:433
  58.9 31.4 %collective-permute-start.3 = (f32[96,768]{1,0:T(8,128)S(1)}, f32[96,768]{1,0:T(8,128)S(1)}, u32[]{:S(2)}, u32[]{:S(2)}) collective-permute-start(f32[96,768]{1,0:T(8,128)S(1)} %get-tuple-element.72), channel_id=1, source_target_pairs={{0,2},{1,3},{2,0},{3,1},{4,6},{5,7},{6,4},{7,5},{8,10},{9,11},{10,... | collective-permute-start | bytes 884744 | tf_op jit(solution)/shard_map/ppermute | solution.py:429
  60.4 29.9 %collective-permute-start.4 = (f32[96,768]{1,0:T(8,128)S(1)}, f32[96,768]{1,0:T(8,128)S(1)}, u32[]{:S(2)}, u32[]{:S(2)}) collective-permute-start(f32[96,768]{1,0:T(8,128)S(1)} %get-tuple-element.73), channel_id=1, source_target_pairs={{0,4},{1,5},{2,6},{3,7},{4,0},{5,1},{6,2},{7,3},{8,12},{9,13},{10,... | collective-permute-start | bytes 884744 | tf_op jit(solution)/shard_map/ppermute | solution.py:429
  62.0 32.9 %collective-permute-start.5 = (f32[96,768]{1,0:T(8,128)S(1)}, f32[96,768]{1,0:T(8,128)S(1)}, u32[]{:S(2)}, u32[]{:S(2)}) collective-permute-start(f32[96,768]{1,0:T(8,128)S(1)} %get-tuple-element.74), channel_id=1, source_target_pairs={{0,6},{1,7},{2,4},{3,5},{4,2},{5,3},{6,0},{7,1},{8,14},{9,15},{10,... | collective-permute-start | bytes 884744 | tf_op jit(solution)/shard_map/ppermute | solution.py:429
  62.4 18.0 %collective-permute-start.6 = (f32[32,768]{1,0:T(8,128)S(1)}, f32[32,768]{1,0:T(8,128)S(1)}, u32[]{:S(2)}, u32[]{:S(2)}) collective-permute-start(f32[32,768]{1,0:T(8,128)S(1)} %get-tuple-element.75), channel_id=1, source_target_pairs={{0,9},{1,8},{2,11},{3,10},{4,13},{5,12},{6,15},{7,14},{8,1},{9,0},... | collective-permute-start | bytes 294920 | tf_op jit(solution)/shard_map/ppermute | solution.py:429
  62.4 21.0 %collective-permute-start.7 = (f32[32,768]{1,0:T(8,128)S(1)}, f32[32,768]{1,0:T(8,128)S(1)}, u32[]{:S(2)}, u32[]{:S(2)}) collective-permute-start(f32[32,768]{1,0:T(8,128)S(1)} %get-tuple-element.76), channel_id=1, source_target_pairs={{0,11},{1,10},{2,9},{3,8},{4,15},{5,14},{6,13},{7,12},{8,3},{9,2},... | collective-permute-start | bytes 294920 | tf_op jit(solution)/shard_map/ppermute | solution.py:429
  80.4 6.3 %collective-permute-start.8 = (f32[32,768]{1,0:T(8,128)S(1)}, f32[32,768]{1,0:T(8,128)S(1)}, u32[]{:S(2)}, u32[]{:S(2)}) collective-permute-start(f32[32,768]{1,0:T(8,128)S(1)} %get-tuple-element.77), channel_id=1, source_target_pairs={{0,13},{1,12},{2,15},{3,14},{4,9},{5,8},{6,11},{7,10},{8,5},{9,4},... | collective-permute-start | bytes 294920 | tf_op jit(solution)/shard_map/ppermute | solution.py:429
  83.4 6.9 %collective-permute-start.9 = (f32[32,768]{1,0:T(8,128)S(1)}, f32[32,768]{1,0:T(8,128)S(1)}, u32[]{:S(2)}, u32[]{:S(2)}) collective-permute-start(f32[32,768]{1,0:T(8,128)S(1)} %get-tuple-element.78), channel_id=1, source_target_pairs={{0,15},{1,14},{2,13},{3,12},{4,11},{5,10},{6,9},{7,8},{8,7},{9,6},... | collective-permute-start | bytes 294920 | tf_op jit(solution)/shard_map/ppermute | solution.py:429
where the time goes:
time: 98.6 us; the launch traced here: 98.3 us
  Pallas kernels  46.5 us (47%)
  waiting for transfers between devices  29.1 us (30%)
  starting transfers between devices  20.8 us (21%)
  local copies, waits for them, and re-layouts  0.99 us (1%)
    pallas_call x4, Pallas kernels, shards(): pl.pallas_call(functools.partial(solve_kernel, 1.0 / math.sqrt(comps * no...  33.6 us
    ppermute x10, waiting for transfers between devices, hop(): return lax.ppermute(sent, axes, [(s, s ^ mask) for s in range(devices)])  29.1 us
    ppermute x10, starting transfers between devices, hop(): return lax.ppermute(sent, axes, [(s, s ^ mask) for s in range(devices)])  15 us
    all_to_all x1, starting transfers between devices, shards(): lax.all_to_all(pair.reshape(2 * lanes, per_peer, deep), axes, split_axis=...  5.81 us
    pallas_call x1, Pallas kernels, shards(): pl.pallas_call(functools.partial(prep_kernel, devices, per_peer, comps, v...  4.72 us
    pallas_call x1, Pallas kernels, shards(): pl.pallas_call(functools.partial(land_kernel, devices, per_peer), out_sha...  3.27 us
    pallas_call x1, Pallas kernels, shards(): pl.pallas_call(functools.partial(ship_kernel, devices, 2 * group, len(upd...  3.09 us
  transfers between devices with their start and end apart: 11, of which 6 were waited for; matrix products, arithmetic and copies ran while one was open for 0% of the time, Pallas kernels for 29%

commit v1 on v0

--- a/solution.py
+++ b/solution.py
@@ -12,10 +12,10 @@
 LANES = 128
 PLANES = 4
 PATTERN = 32
+ROOM = 8192
 
 NN = (((1,), (0,)), ((), ()))
 NT = (((1,), (1,)), ((), ()))
-TN = (((0,), (0,)), ((), ()))
 
 
 def up(value, unit):
@@ -43,7 +43,7 @@
     return jnp.where(rows == row, 1.0, 0.0).astype(jnp.bfloat16)
 
 
-def pack_kernel(coupling, plastic, strain, owner, qp, pattern, small):
+def pack_kernel(coupling, plastic, strain, owner, qp, pattern, packed, small, sem):
     top = 0
     for c in range(coupling.shape[0]):
         small[top:top + coupling.shape[1], :] = coupling[c]
@@ -56,15 +56,21 @@
         for b in range(count):
             couples = jnp.full((1, LANES), pattern[a, b].astype(jnp.float32))
             small[PATTERN + a * count + b:PATTERN + a * count + b + 1, 0:LANES] = couples
+    copy = pltpu.make_async_copy(small, packed.at[pl.ds(0, small.shape[0]), :], sem)
+    copy.start()
+    copy.wait()
 
 
 def prep_kernel(devices, per_peer, comps, voigt, *refs):
-    sources, outs, (kfull, pad), local, sem = refs[:4], refs[4:13], refs[13:15], refs[15:19], refs[19]
-    khi, klo, hist_s, weight_s, strain_s, place_s, qp_s, cstack, pdir = outs
+    sources, outs, local = refs[:4], refs[4:14], refs[14:18]
+    kfull, pad, stack, sem = refs[18:]
+    khi, klo, hist_s, weight_s, strain_s, place_s, qp_s, cstack, loads, pdir = outs
     small, stiff, hist, flag = local
     copies = [
         pltpu.make_async_copy(source, target, sem.at[i])
-        for i, (source, target) in enumerate(zip(sources, local))
+        for i, (source, target) in enumerate(
+            zip((sources[0].at[pl.ds(0, local[0].shape[0]), :], *sources[1:]), local)
+        )
     ]
     for copy in copies:
         copy.start()
@@ -137,13 +143,15 @@
     weight_s[0:nodes, :] = dot(flag[...].astype(jnp.float32).astype(jnp.bfloat16), order, NT)
     weight_s[...] = weight_s[...] * h * h / (1.0 + h * h)
 
-    cstack[...] = jnp.zeros_like(cstack)
     for c in range(comps):
         cpl = small[c * voigt:(c + 1) * voigt, :]
         hi = cpl.astype(jnp.bfloat16).astype(jnp.float32)
-        cstack[c, 0:voigt, 0:nodes] = hi
-        cstack[c, 8:8 + voigt, 0:nodes] = hi
-        cstack[c, 16:16 + voigt, 0:nodes] = cpl - hi
+        stack[...] = jnp.zeros_like(stack)
+        stack[0:voigt, 0:nodes] = hi
+        stack[8:8 + voigt, 0:nodes] = hi
+        stack[16:16 + voigt, 0:nodes] = cpl - hi
+        cstack[c] = stack[...].astype(jnp.bfloat16)
+        loads[c] = jnp.transpose(stack[...]).astype(jnp.bfloat16)
     pdir[...] = jnp.zeros_like(pdir)
     for c in range(comps):
         spread = jnp.broadcast_to(small[at_plastic + c:at_plastic + c + 1, :], (LANES, nodes))
@@ -170,10 +178,11 @@
     return jnp.sum(parts, axis=0, keepdims=True)
 
 
-def solve_kernel(scale, first, earlier, khi, klo, hist, weight, strain, cstack, pdir, place, *refs):
+def solve_kernel(scale, first, earlier, khi, klo, hist, weight, strain, cstack, loads, pdir, place,
+                 *refs):
     earlier_updated, refs = refs[:earlier], refs[earlier:]
     updated, stress, blocks = refs[0], refs[1], refs[2:-5]
-    field, resid, image, solved, split = refs[-5:]
+    field, resid, image, steps, split = refs[-5:]
     rows, span = hist.shape
     comps = pdir.shape[0]
     wide = comps * span
@@ -192,18 +201,17 @@
     s3 = jnp.concatenate([s_hi, s - s_hi, s_hi, jnp.zeros_like(s)], axis=0).astype(jnp.bfloat16)
     split[rows:, :] = jnp.zeros((split.shape[0] - rows, 2 * wide), jnp.bfloat16)
     for c in range(comps):
-        image[:, c * span:(c + 1) * span] = dot(cstack[c].astype(jnp.bfloat16), s3, TN)
+        image[:, c * span:(c + 1) * span] = dot(loads[c], s3)
     parts = zero
     for r, l, c in sweep(rows, comps, span):
         d = image[r, l] - weight[r, :] * hist[r, :] * flow(c, r)
         resid[r, l] = d
-        field[r, l] = d
+        field[0, r, l] = d
         keep(r, c, d)
         parts = parts + fold(d * d)
     norm = total(parts)
-    solved[...] = jnp.zeros_like(solved)
-
-    def step_length(norm):
+
+    def step_length(turn, norm):
         parts = zero
         for r in row_blocks(rows, span):
             both = dot(khi[r, :], split[...])
@@ -211,32 +219,37 @@
             tangent = 1.5 - weight[r, :]
             for c in range(comps):
                 l = slice(c * span, (c + 1) * span)
-                d = field[r, l]
+                d = field[turn, r, l]
                 q = both[:, l] + both[:, wide + c * span:wide + (c + 1) * span] + low[:, l]
                 q = q + tangent * d
                 image[r, l] = q
                 parts = parts + fold(d * q)
         return norm / jnp.maximum(total(parts), 1.0)
 
-    def step(_, norm):
-        alpha = step_length(norm)
+    def step(turn, norm):
+        alpha = step_length(turn, norm)
+        steps[turn] = jnp.broadcast_to(alpha, steps.shape[1:])
         parts = zero
         for r, l, c in sweep(rows, comps, span):
-            solved[r, l] = solved[r, l] + alpha * field[r, l]
             left = resid[r, l] - alpha * image[r, l]
             resid[r, l] = left
             parts = parts + fold(left * left)
         following = total(parts)
         beta = following / jnp.maximum(norm, 1.0)
         for r, l, c in sweep(rows, comps, span):
-            d = resid[r, l] + beta * field[r, l]
-            field[r, l] = d
+            d = resid[r, l] + beta * field[turn, r, l]
+            field[turn + 1, r, l] = d
             keep(r, c, d)
         return following
 
-    alpha = step_length(lax.fori_loop(0, ITERS - 1, step, norm))
+    last = ITERS - 1
+    alpha = step_length(last, lax.fori_loop(0, last, step, norm))
+    alphas = [steps[turn, 0:1, :] for turn in range(last)]
     for r, l, c in sweep(rows, comps, span):
-        x = solved[r, l] + alpha * field[r, l]
+        x = alphas[0] * field[0, r, l]
+        for turn in range(1, last):
+            x = x + alphas[turn] * field[turn, r, l]
+        x = x + alpha * field[last, r, l]
         pushed = flow(c, r) * x
         image[r, 0:span] = pushed if c == 0 else image[r, 0:span] + pushed
         keep(r, c, (1.5 - weight[r, :]) * x)
@@ -248,7 +261,7 @@
         top += block.shape[0]
     out = s
     for c in range(comps):
-        cpl = cstack[c].astype(jnp.bfloat16)
+        cpl = cstack[c]
         main = dot(cpl, split[0:rows, c * span:(c + 1) * span])
         minor = dot(cpl, split[0:rows, wide + c * span:wide + (c + 1) * span])
         out = out + scale * (main[0:8] + main[16:24] + minor[0:8])
@@ -349,15 +362,17 @@
     f32, bf16, i32 = jnp.float32, jnp.bfloat16, jnp.int32
     vmem = pl.BlockSpec(memory_space=pltpu.VMEM)
     small_inputs = (coupling, plastic_dir, strain, new_owner.reshape(1, columns), qp_to_rve, pattern)
+    small_rows = up(PATTERN + pattern.size, 8)
     small = pl.pallas_call(
         pack_kernel,
-        out_shape=jax.ShapeDtypeStruct((up(PATTERN + pattern.size, 8), nodes), f32),
+        out_shape=jax.ShapeDtypeStruct((ROOM, nodes), f32),
         in_specs=[vmem] * 5 + [pl.BlockSpec(memory_space=pltpu.SMEM)],
-        out_specs=vmem,
+        out_specs=pl.BlockSpec(memory_space=pltpu.HBM),
+        scratch_shapes=[pltpu.VMEM((small_rows, nodes), f32), pltpu.SemaphoreType.DMA],
         compiler_params=params(60),
     )(*small_inputs)
     inputs = (small, stiffness, history, yield_flags)
-    khi, klo, hist_s, weight_s, strain_s, place_s, qp_s, cstack, pdir = pl.pallas_call(
+    khi, klo, hist_s, weight_s, strain_s, place_s, qp_s, cstack, loads, pdir = pl.pallas_call(
         functools.partial(prep_kernel, devices, per_peer, comps, voigt),
         out_shape=(
             jax.ShapeDtypeStruct((rows, deep), bf16),
@@ -367,14 +382,16 @@
             jax.ShapeDtypeStruct((8, columns), f32),
             jax.ShapeDtypeStruct((8, columns), i32),
             jax.ShapeDtypeStruct((8, columns), i32),
-            jax.ShapeDtypeStruct((comps, 32, rows), f32),
+            jax.ShapeDtypeStruct((comps, 32, rows), bf16),
+            jax.ShapeDtypeStruct((comps, rows, 32), bf16),
             jax.ShapeDtypeStruct((comps, rows, LANES), f32),
         ),
         in_specs=[pl.BlockSpec(memory_space=pltpu.HBM)] * 4,
-        out_specs=[vmem] * 9,
-        scratch_shapes=[pltpu.VMEM((rows, deep), f32), pltpu.VMEM((8, columns), f32)]
-        + [pltpu.VMEM(x.shape, x.dtype) for x in inputs]
-        + [pltpu.SemaphoreType.DMA((4,))],
+        out_specs=[vmem] * 10,
+        scratch_shapes=[pltpu.VMEM((small_rows, nodes), f32)]
+        + [pltpu.VMEM(x.shape, x.dtype) for x in inputs[1:]]
+        + [pltpu.VMEM((rows, deep), f32), pltpu.VMEM((8, columns), f32),
+           pltpu.VMEM((32, rows), f32), pltpu.SemaphoreType.DMA((4,))],
         compiler_params=params(46),
     )(*inputs)
 
@@ -398,16 +415,18 @@
                 *outs,
             ),
             in_specs=[whole((rows, deep)), whole((rows, deep)), part(rows), part(rows), part(8),
-                      whole((comps, 32, rows)), whole((comps, rows, LANES)), whole((8, columns))]
+                      whole((comps, 32, rows)), whole((comps, rows, 32)), whole((comps, rows, LANES)),
+                      whole((8, columns))]
             + [whole(u.shape) for u in updated],
             out_specs=[whole((rows, span)), whole((8, span))] + [whole(o.shape) for o in outs],
-            scratch_shapes=[pltpu.VMEM((rows, wide), f32) for _ in range(4)]
-            + [pltpu.VMEM((deep, 2 * wide), bf16)],
+            scratch_shapes=[pltpu.VMEM((ITERS, rows, wide), f32), pltpu.VMEM((rows, wide), f32),
+                            pltpu.VMEM((rows, wide), f32), pltpu.VMEM((ITERS, 8, span), f32),
+                            pltpu.VMEM((deep, 2 * wide), bf16)],
             compiler_params=params(),
             cost_estimate=pl.CostEstimate(
                 flops=18 * rows * deep * wide, bytes_accessed=2**20, transcendentals=0
             ),
-        )(khi, klo, hist_s, weight_s, strain_s, cstack, pdir, place_s, *updated)
+        )(khi, klo, hist_s, weight_s, strain_s, cstack, loads, pdir, place_s, *updated)
         updated.append(done[0])
         stress_s.append(done[1])
         ready.append(done[2:])

time: 98.6 us -> 96 us (0.974)
  Pallas kernels: 46.5 us -> 44.9 us
  local copies, waits for them, and re-layouts: 0.99 us -> 0 us
    pallas_call x4, Pallas kernels: 33.6 us -> 32.1 us  [shards(): pl.pallas_call(functools.partial(solve_kernel, 1.0 / math.sqrt(comps * no...]
    unnamed x2 -> x0, local copies, waits for them, and re-layouts: 0.99 us -> none
where the time goes in v1:
time: 96 us; the launch traced here: 95.8 us
  Pallas kernels  44.9 us (47%)
  waiting for transfers between devices  29.1 us (30%)
  starting transfers between devices  20.8 us (22%)
    pallas_call x4, Pallas kernels, shards(): pl.pallas_call(functools.partial(solve_kernel, 1.0 / math.sqrt(comps * no...  32.1 us
    ppermute x10, waiting for transfers between devices, hop(): return lax.ppermute(sent, axes, [(s, s ^ mask) for s in range(devices)])  29.1 us
    ppermute x10, starting transfers between devices, hop(): return lax.ppermute(sent, axes, [(s, s ^ mask) for s in range(devices)])  15 us
    all_to_all x1, starting transfers between devices, shards(): lax.all_to_all(pair.reshape(2 * lanes, per_peer, deep), axes, split_axis=...  5.8 us
    pallas_call x1, Pallas kernels, shards(): pl.pallas_call(functools.partial(prep_kernel, devices, per_peer, comps, v...  4.68 us
    pallas_call x1, Pallas kernels, shards(): pl.pallas_call(functools.partial(land_kernel, devices, per_peer), out_sha...  3.27 us
    pallas_call x1, Pallas kernels, shards(): pl.pallas_call(functools.partial(ship_kernel, devices, 2 * group, len(upd...  3.09 us
  transfers between devices with their start and end apart: 11, of which 6 were waited for; matrix products, arithmetic and copies ran while one was open for 0% of the time, Pallas kernels for 29%

profile of v1, /device:TPU:0, one launch (start us, length us, event | category | flops | bytes accessed | tf_op | source)
XLA Modules:
  0.0 95.8 jit_solution(1506354806627901606)
XLA Ops:
  0.6 1.8 %shard_map.104.refs_0_ = f32[8192,729]{1,0:T(8,128)} custom-call(f32[3,6,729]{2,1,0:T(8,128)} %coupling.1, f32[3,729]{1,0:T(4,128)} %plastic.1, f32[6,512]{1,0:T(8,128)} %strain.1, s32[1,512]{1,0:T(1,128)} %bitcast.3, s32[1,512]{1,0:T(1,128)} %qp.1, s32[9,9]{1,0:T(8,128)} %pattern.1), custom_call_target="tpu_custom_call" | custom-call | tf_op jit(solution)/shard_map/pallas_call | solution.py:366
  2.4 4.7 %shard_map.105 = (bf16[736,768]{1,0:T(8,128)(2,1)S(1)}, bf16[736,768]{1,0:T(8,128)(2,1)S(1)}, f32[736,512]{1,0:T(8,128)S(1)}, f32[736,512]{1,0:T(8,128)S(1)}, f3...) custom-call(f32[8192,729]{1,0:T(8,128)} %shard_map.104.refs_0_, ...), custom_call_target="tpu_custom_call" | custom-call | tf_op jit(solution)/shard_map/pallas_call | solution.py:375
  7.1 7.8 %shard_map.106 = (f32[736,128]{1,0:T(8,128)S(1)}, f32[8,128]{1,0:T(8,128)S(1)}, f32[128,768]{1,0:T(8,128)S(1)}) custom-call(bf16[736,768]{1,0:T(8,128)(2,1)S(1)} %get-tuple-element.44.khi, bf16[736,768]{1,0:T(8,128)(2,1)S(1)} %get-tuple-element.45.klo, f32[736,512]{1,0:T(8,128)S(1)} %get-tuple-element.46.hist, f32[736,512]{1,0:T(8,128)S(1)} %get-tuple-element.47.weight, ...), custom_call_target="tpu_custom_call" | custom-call | flops 3906994176 | bytes 1048576 | tf_op jit(solution)/shard_map/pallas_call | solution.py:409
  14.9 4.1 %collective-permute-start = (f32[128,768]{1,0:T(8,128)S(1)}, f32[128,768]{1,0:T(8,128)S(1)}, u32[]{:S(2)}, u32[]{:S(2)}) collective-permute-start(f32[128,768]{1,0:T(8,128)S(1)} %get-tuple-element.66), channel_id=1, source_target_pairs={{0,16},{1,17},{2,18},{3,19},{4,20},{5,21},{6,22},{7,23},{8,24},{9,... | collective-permute-start | bytes 1179656 | tf_op jit(solution)/shard_map/ppermute | solution.py:448
  19.0 7.9 %shard_map.107 = (f32[736,128]{1,0:T(8,128)S(1)}, f32[8,128]{1,0:T(8,128)S(1)}, f32[128,768]{1,0:T(8,128)S(1)}) custom-call(bf16[736,768]{1,0:T(8,128)(2,1)S(1)} %get-tuple-element.44.khi, bf16[736,768]{1,0:T(8,128)(2,1)S(1)} %get-tuple-element.45.klo, f32[736,512]{1,0:T(8,128)S(1)} %get-tuple-element.46.hist, f32[736,512]{1,0:T(8,128)S(1)} %get-tuple-element.47.weight, ...), custom_call_target="tpu_custom_call" | custom-call | flops 3906994176 | bytes 1048576 | tf_op jit(solution)/shard_map/pallas_call | solution.py:409
  26.9 1.6 %collective-permute-start.1 = (f32[128,768]{1,0:T(8,128)S(1)}, f32[128,768]{1,0:T(8,128)S(1)}, u32[]{:S(2)}, u32[]{:S(2)}) collective-permute-start(f32[128,768]{1,0:T(8,128)S(1)} %get-tuple-element.67), channel_id=1, source_target_pairs={{0,8},{1,9},{2,10},{3,11},{4,12},{5,13},{6,14},{7,15},{8,0},{9,1},... | collective-permute-start | bytes 1179656 | tf_op jit(solution)/shard_map/ppermute | solution.py:448
  28.5 8.2 %shard_map.108 = (f32[736,128]{1,0:T(8,128)S(1)}, f32[8,128]{1,0:T(8,128)S(1)}, f32[128,768]{1,0:T(8,128)S(1)}) custom-call(bf16[736,768]{1,0:T(8,128)(2,1)S(1)} %get-tuple-element.44.khi, bf16[736,768]{1,0:T(8,128)(2,1)S(1)} %get-tuple-element.45.klo, f32[736,512]{1,0:T(8,128)S(1)} %get-tuple-element.46.hist, f32[736,512]{1,0:T(8,128)S(1)} %get-tuple-element.47.weight, ...), custom_call_target="tpu_custom_call" | custom-call | flops 3906994176 | bytes 1048576 | tf_op jit(solution)/shard_map/pallas_call | solution.py:409
  36.8 8.1 %shard_map.109 = (f32[736,128]{1,0:T(8,128)S(1)}, f32[8,128]{1,0:T(8,128)S(1)}, f32[32,768]{1,0:T(8,128)S(1)}, f32[32,768]{1,0:T(8,128)S(1)}, f32[32,768]{1,0:T(8,128)S(1)}, /*index=5*/f32[32,768]{1,0:T(8,128)S(1)}) custom-call(bf16[736,768]{1,0:T(8,128)(2,1)S(1)} %get-tuple-element.44.khi, bf16[736,768]{1,0:T(8,128)(2,1)S(1)} %get-tuple-element.45.klo, ...), custom_call_target="tpu_custom_call" | custom-call | flops 3906994176 | bytes 1048576 | tf_op jit(solution)/shard_map/pallas_call | solution.py:409
  44.9 3.1 %shard_map.110 = (f32[512,768]{1,0:T(8,128)}, f32[6,512]{1,0:T(8,128)}) custom-call(s32[8,512]{1,0:T(8,128)S(1)} %get-tuple-element.42.place, s32[8,512]{1,0:T(8,128)S(1)} %get-tuple-element.43.at, f32[736,128]{1,0:T(8,128)S(1)} %get-tuple-element.52.refs_0_, f32[736,128]{1,0:T(8,128)S(1)} %get-tuple-element.53.refs_1_, ...), custom_call_target="tpu_custom_call" | custom-call | flops 771751936 | bytes 1048576 | tf_op jit(solution)/shard_map/pallas_call | solution.py:434
  48.0 5.8 %all-to-all-start = ((f32[16,32,768]{2,1,0:T(8,128)}), f32[16,32,768]{2,1,0:T(8,128)}, u32[]{:S(2)}, u32[]{:S(2)}) async-start(f32[16,32,768]{2,1,0:T(8,128)} %bitcast.1), calls=%async_computation | async-start | bytes 3145728 | tf_op jit(solution)/shard_map/all_to_all | solution.py:452
  53.9 3.0 %collective-permute-done.2.refs_2_ = f32[128,768]{1,0:T(8,128)S(1)} collective-permute-done((f32[128,768]{1,0:T(8,128)S(1)}, f32[128,768]{1,0:T(8,128)S(1)}, u32[]{:S(2)}, u32[]{:S(2)}) %collective-permute-start.2) | collective-permute-done | bytes 393248 | tf_op jit(solution)/shard_map/ppermute | solution.py:448
  56.9 0.1 shard_map.111
  56.9 1.6 %collective-permute-start.3 = (f32[96,768]{1,0:T(8,128)S(1)}, f32[96,768]{1,0:T(8,128)S(1)}, u32[]{:S(2)}, u32[]{:S(2)}) collective-permute-start(f32[96,768]{1,0:T(8,128)S(1)} %get-tuple-element.74), channel_id=1, source_target_pairs={{0,2},{1,3},{2,0},{3,1},{4,6},{5,7},{6,4},{7,5},{8,10},{9,11},{10,... | collective-permute-start | bytes 884744 | tf_op jit(solution)/shard_map/ppermute | solution.py:448
  58.5 1.5 %collective-permute-start.4 = (f32[96,768]{1,0:T(8,128)S(1)}, f32[96,768]{1,0:T(8,128)S(1)}, u32[]{:S(2)}, u32[]{:S(2)}) collective-permute-start(f32[96,768]{1,0:T(8,128)S(1)} %get-tuple-element.75), channel_id=1, source_target_pairs={{0,4},{1,5},{2,6},{3,7},{4,0},{5,1},{6,2},{7,3},{8,12},{9,13},{10,... | collective-permute-start | bytes 884744 | tf_op jit(solution)/shard_map/ppermute | solution.py:448
  60.0 0.5 collective-permute-start.5
  60.5 2.7 %collective-permute-start.7 = (f32[32,768]{1,0:T(8,128)S(1)}, f32[32,768]{1,0:T(8,128)S(1)}, u32[]{:S(2)}, u32[]{:S(2)}) collective-permute-start(f32[32,768]{1,0:T(8,128)S(1)} %get-tuple-element.78), channel_id=1, source_target_pairs={{0,11},{1,10},{2,9},{3,8},{4,15},{5,14},{6,13},{7,12},{8,3},{9,2},... | collective-permute-start | bytes 294920 | tf_op jit(solution)/shard_map/ppermute | solution.py:448
  63.2 14.7 %collective-permute-done.6.refs_4_ = f32[32,768]{1,0:T(8,128)S(1)} collective-permute-done((f32[32,768]{1,0:T(8,128)S(1)}, f32[32,768]{1,0:T(8,128)S(1)}, u32[]{:S(2)}, u32[]{:S(2)}) %collective-permute-start.6) | collective-permute-done | bytes 98336 | tf_op jit(solution)/shard_map/ppermute | solution.py:448
  77.9 1.4 %collective-permute-start.8 = (f32[32,768]{1,0:T(8,128)S(1)}, f32[32,768]{1,0:T(8,128)S(1)}, u32[]{:S(2)}, u32[]{:S(2)}) collective-permute-start(f32[32,768]{1,0:T(8,128)S(1)} %get-tuple-element.79), channel_id=1, source_target_pairs={{0,13},{1,12},{2,15},{3,14},{4,9},{5,8},{6,11},{7,10},{8,5},{9,4},... | collective-permute-start | bytes 294920 | tf_op jit(solution)/shard_map/ppermute | solution.py:448
  79.3 1.6 %collective-permute-done.7.refs_5_ = f32[32,768]{1,0:T(8,128)S(1)} collective-permute-done((f32[32,768]{1,0:T(8,128)S(1)}, f32[32,768]{1,0:T(8,128)S(1)}, u32[]{:S(2)}, u32[]{:S(2)}) %collective-permute-start.7) | collective-permute-done | bytes 98336 | tf_op jit(solution)/shard_map/ppermute | solution.py:448
  80.9 1.6 %collective-permute-start.9 = (f32[32,768]{1,0:T(8,128)S(1)}, f32[32,768]{1,0:T(8,128)S(1)}, u32[]{:S(2)}, u32[]{:S(2)}) collective-permute-start(f32[32,768]{1,0:T(8,128)S(1)} %get-tuple-element.80), channel_id=1, source_target_pairs={{0,15},{1,14},{2,13},{3,12},{4,11},{5,10},{6,9},{7,8},{8,7},{9,6},... | collective-permute-start | bytes 294920 | tf_op jit(solution)/shard_map/ppermute | solution.py:448
  82.5 1.5 %collective-permute-done.8.refs_6_ = f32[32,768]{1,0:T(8,128)S(1)} collective-permute-done((f32[32,768]{1,0:T(8,128)S(1)}, f32[32,768]{1,0:T(8,128)S(1)}, u32[]{:S(2)}, u32[]{:S(2)}) %collective-permute-start.8) | collective-permute-done | bytes 98336 | tf_op jit(solution)/shard_map/ppermute | solution.py:448
  84.0 3.7 %collective-permute-done.9.refs_7_ = f32[32,768]{1,0:T(8,128)S(1)} collective-permute-done((f32[32,768]{1,0:T(8,128)S(1)}, f32[32,768]{1,0:T(8,128)S(1)}, u32[]{:S(2)}, u32[]{:S(2)}) %collective-permute-start.9) | collective-permute-done | bytes 98336 | tf_op jit(solution)/shard_map/ppermute | solution.py:448
  87.8 4.5 %collective-permute-done.5.refs_3_ = f32[96,768]{1,0:T(8,128)S(1)} collective-permute-done((f32[96,768]{1,0:T(8,128)S(1)}, f32[96,768]{1,0:T(8,128)S(1)}, u32[]{:S(2)}, u32[]{:S(2)}) %collective-permute-start.5) | collective-permute-done | bytes 294944 | tf_op jit(solution)/shard_map/ppermute | solution.py:448
  92.3 3.3 %shard_map.112 = f32[729,1024]{1,0:T(8,128)} custom-call(f32[512,768]{1,0:T(8,128)} %bitcast.2.pair, f32[96,768]{1,0:T(8,128)S(1)} %get-tuple-element.73.refs_0_, f32[96,768]{1,0:T(8,128)S(1)} %collective-permute-done.3.refs_1_, f32[96,768]{1,0:T(8,128)S(1)} %collective-permute-done.4.refs_2_, f32[96,768]{1,0:T(8,128)S(1)} %collective-permute-done.5.refs_3_, ...), custom_call_target="tpu_custom_call" | custom-call | tf_op jit(solution)/shard_map/pallas_call | solution.py:471
  (7 shorter events, 0.1 us)
Async XLA Ops:
  14.9 38.9 %collective-permute-start = (f32[128,768]{1,0:T(8,128)S(1)}, f32[128,768]{1,0:T(8,128)S(1)}, u32[]{:S(2)}, u32[]{:S(2)}) collective-permute-start(f32[128,768]{1,0:T(8,128)S(1)} %get-tuple-element.66), channel_id=1, source_target_pairs={{0,16},{1,17},{2,18},{3,19},{4,20},{5,21},{6,22},{7,23},{8,24},{9,... | collective-permute-start | bytes 1179656 | tf_op jit(solution)/shard_map/ppermute | solution.py:448
  26.9 27.0 %collective-permute-start.1 = (f32[128,768]{1,0:T(8,128)S(1)}, f32[128,768]{1,0:T(8,128)S(1)}, u32[]{:S(2)}, u32[]{:S(2)}) collective-permute-start(f32[128,768]{1,0:T(8,128)S(1)} %get-tuple-element.67), channel_id=1, source_target_pairs={{0,8},{1,9},{2,10},{3,11},{4,12},{5,13},{6,14},{7,15},{8,0},{9,1},... | collective-permute-start | bytes 1179656 | tf_op jit(solution)/shard_map/ppermute | solution.py:448
  36.8 20.1 %collective-permute-start.2 = (f32[128,768]{1,0:T(8,128)S(1)}, f32[128,768]{1,0:T(8,128)S(1)}, u32[]{:S(2)}, u32[]{:S(2)}) collective-permute-start(f32[128,768]{1,0:T(8,128)S(1)} %get-tuple-element.70), channel_id=1, source_target_pairs={{0,17},{1,16},{2,19},{3,18},{4,21},{5,20},{6,23},{7,22},{8,25},{9,... | collective-permute-start | bytes 1179656 | tf_op jit(solution)/shard_map/ppermute | solution.py:448
  48.0 44.3 %all-to-all-start = ((f32[16,32,768]{2,1,0:T(8,128)}), f32[16,32,768]{2,1,0:T(8,128)}, u32[]{:S(2)}, u32[]{:S(2)}) async-start(f32[16,32,768]{2,1,0:T(8,128)} %bitcast.1), calls=%async_computation | async-start | bytes 3145728 | tf_op jit(solution)/shard_map/all_to_all | solution.py:452
  56.9 30.8 %collective-permute-start.3 = (f32[96,768]{1,0:T(8,128)S(1)}, f32[96,768]{1,0:T(8,128)S(1)}, u32[]{:S(2)}, u32[]{:S(2)}) collective-permute-start(f32[96,768]{1,0:T(8,128)S(1)} %get-tuple-element.74), channel_id=1, source_target_pairs={{0,2},{1,3},{2,0},{3,1},{4,6},{5,7},{6,4},{7,5},{8,10},{9,11},{10,... | collective-permute-start | bytes 884744 | tf_op jit(solution)/shard_map/ppermute | solution.py:448
  58.5 29.3 %collective-permute-start.4 = (f32[96,768]{1,0:T(8,128)S(1)}, f32[96,768]{1,0:T(8,128)S(1)}, u32[]{:S(2)}, u32[]{:S(2)}) collective-permute-start(f32[96,768]{1,0:T(8,128)S(1)} %get-tuple-element.75), channel_id=1, source_target_pairs={{0,4},{1,5},{2,6},{3,7},{4,0},{5,1},{6,2},{7,3},{8,12},{9,13},{10,... | collective-permute-start | bytes 884744 | tf_op jit(solution)/shard_map/ppermute | solution.py:448
  60.0 32.3 %collective-permute-start.5 = (f32[96,768]{1,0:T(8,128)S(1)}, f32[96,768]{1,0:T(8,128)S(1)}, u32[]{:S(2)}, u32[]{:S(2)}) collective-permute-start(f32[96,768]{1,0:T(8,128)S(1)} %get-tuple-element.76), channel_id=1, source_target_pairs={{0,6},{1,7},{2,4},{3,5},{4,2},{5,3},{6,0},{7,1},{8,14},{9,15},{10,... | collective-permute-start | bytes 884744 | tf_op jit(solution)/shard_map/ppermute | solution.py:448
  60.5 17.4 %collective-permute-start.6 = (f32[32,768]{1,0:T(8,128)S(1)}, f32[32,768]{1,0:T(8,128)S(1)}, u32[]{:S(2)}, u32[]{:S(2)}) collective-permute-start(f32[32,768]{1,0:T(8,128)S(1)} %get-tuple-element.77), channel_id=1, source_target_pairs={{0,9},{1,8},{2,11},{3,10},{4,13},{5,12},{6,15},{7,14},{8,1},{9,0},... | collective-permute-start | bytes 294920 | tf_op jit(solution)/shard_map/ppermute | solution.py:448
  60.5 20.4 %collective-permute-start.7 = (f32[32,768]{1,0:T(8,128)S(1)}, f32[32,768]{1,0:T(8,128)S(1)}, u32[]{:S(2)}, u32[]{:S(2)}) collective-permute-start(f32[32,768]{1,0:T(8,128)S(1)} %get-tuple-element.78), channel_id=1, source_target_pairs={{0,11},{1,10},{2,9},{3,8},{4,15},{5,14},{6,13},{7,12},{8,3},{9,2},... | collective-permute-start | bytes 294920 | tf_op jit(solution)/shard_map/ppermute | solution.py:448
  77.9 6.2 %collective-permute-start.8 = (f32[32,768]{1,0:T(8,128)S(1)}, f32[32,768]{1,0:T(8,128)S(1)}, u32[]{:S(2)}, u32[]{:S(2)}) collective-permute-start(f32[32,768]{1,0:T(8,128)S(1)} %get-tuple-element.79), channel_id=1, source_target_pairs={{0,13},{1,12},{2,15},{3,14},{4,9},{5,8},{6,11},{7,10},{8,5},{9,4},... | collective-permute-start | bytes 294920 | tf_op jit(solution)/shard_map/ppermute | solution.py:448
  80.9 6.9 %collective-permute-start.9 = (f32[32,768]{1,0:T(8,128)S(1)}, f32[32,768]{1,0:T(8,128)S(1)}, u32[]{:S(2)}, u32[]{:S(2)}) collective-permute-start(f32[32,768]{1,0:T(8,128)S(1)} %get-tuple-element.80), channel_id=1, source_target_pairs={{0,15},{1,14},{2,13},{3,12},{4,11},{5,10},{6,9},{7,8},{8,7},{9,6},... | collective-permute-start | bytes 294920 | tf_op jit(solution)/shard_map/ppermute | solution.py:448

commit v2 on v1

--- a/solution.py
+++ b/solution.py
@@ -178,7 +178,7 @@
     return jnp.sum(parts, axis=0, keepdims=True)
 
 
-def solve_kernel(scale, first, earlier, khi, klo, hist, weight, strain, cstack, loads, pdir, place,
+def solve_kernel(scale, cap, nodes, first, earlier, khi, klo, hist, weight, strain, cstack, loads, pdir, place,
                  *refs):
     earlier_updated, refs = refs[:earlier], refs[earlier:]
     updated, stress, blocks = refs[0], refs[1], refs[2:-5]
@@ -254,11 +254,10 @@
         image[r, 0:span] = pushed if c == 0 else image[r, 0:span] + pushed
         keep(r, c, (1.5 - weight[r, :]) * x)
     updated[...] = hist[...] + weight[...] * image[:, 0:span]
-    top, count = 0, sum(block.shape[0] for block in blocks)
-    sent = placed_rows(first, count, place, [*earlier_updated, updated])
-    for block in blocks:
-        put(block, 0, sent[top:top + block.shape[0]])
-        top += block.shape[0]
+    sent = placed_rows(first, LANES, place, [*earlier_updated, updated], split.shape[0])
+    part = LANES // len(blocks)
+    for i, block in enumerate(blocks):
+        put(block, 0, sent[i * part:(i + 1) * part], cap, nodes)
     out = s
     for c in range(comps):
         cpl = cstack[c]
@@ -268,42 +267,88 @@
     stress[...] = out
 
 
-def placed_rows(first, count, place, sources):
+def placed_rows(first, count, place, sources, deep):
     width = sum(source.shape[1] for source in sources)
     placing = hot(place[0:1, 0:width] - first, count)
     sums, left = 0.0, 0
     for source in sources:
-        hi, lo = halves(source[...])
+        rest = jnp.zeros((deep - source.shape[0], source.shape[1]), jnp.float32)
+        hi, lo = halves(jnp.concatenate([source[...], rest], axis=0))
         cut = placing[:, left:left + source.shape[1]]
         sums = sums + (dot(cut, hi, NT) + dot(cut, lo, NT))
         left += source.shape[1]
     return sums
 
 
-def put(block, top, rows):
-    height, filled = rows.shape
-    block[pl.ds(top, height), 0:filled] = rows
-    rest = jnp.zeros((height, block.shape[1] - filled), jnp.float32)
-    block[pl.ds(top, height), filled:] = rest
-
-
-def ship_kernel(devices, first, chunks, place, at, *refs):
+def tight(cap, nodes):
+    return cap % 32 == 0 and LANES // 2 < nodes % LANES <= LANES * 3 // 4
+
+
+def height(cap, nodes):
+    return cap * (nodes // LANES) + (cap // 2 + cap // 4 if tight(cap, nodes) else cap)
+
+
+def put(block, top, rows, cap, nodes):
+    full, half, quarter = nodes // LANES, cap // 2, cap // 4
+
+    def store(at, piece):
+        block[pl.ds(at, piece.shape[0]), :] = piece
+        return at + piece.shape[0]
+
+    for first in range(0, rows.shape[0], cap):
+        for t in range(full):
+            top = store(top, rows[first:first + cap, t * LANES:(t + 1) * LANES])
+        tail = rows[first:first + cap, full * LANES:]
+        if not tight(cap, nodes):
+            top = store(top, tail)
+            continue
+        lane = lax.broadcasted_iota(jnp.int32, (half, LANES), 1)
+        top = store(top, jnp.where(lane < LANES // 2, tail[0:half],
+                                   pltpu.roll(tail[half:], LANES // 2, 1)))
+        lane = lax.broadcasted_iota(jnp.int32, (quarter, LANES), 1) // (LANES // 4)
+        mixed = tail[0:quarter]
+        for g in range(4):
+            moved = pltpu.roll(tail[g * quarter:(g + 1) * quarter], (g + 2) % 4 * (LANES // 4), 1)
+            mixed = jnp.where(lane == g, moved, mixed)
+        top = store(top, mixed)
+
+
+def take(block, top, target, at, cap, nodes):
+    full, half, quarter = nodes // LANES, cap // 2, cap // 4
+    for t in range(full):
+        target[pl.ds(at, cap), t * LANES:(t + 1) * LANES] = block[top + t * cap:top + (t + 1) * cap, :]
+    top = top + full * cap
+    if not tight(cap, nodes):
+        target[pl.ds(at, cap), full * LANES:] = block[top:top + cap, :]
+        return
+    lane = lax.broadcasted_iota(jnp.int32, (quarter, LANES), 1)
+    mixed = block[top + half:top + half + quarter, :]
+    for g in range(4):
+        left = block[top + g % 2 * quarter:top + (g % 2 + 1) * quarter, :]
+        if g >= 2:
+            left = pltpu.roll(left, LANES // 2, 1)
+        right = mixed if g == 2 else pltpu.roll(mixed, (6 - g) % 4 * (LANES // 4), 1)
+        row = pl.multiple_of(at + g * quarter, quarter)
+        target[pl.ds(row, quarter), full * LANES:] = jnp.where(lane < LANES // 2, left, right)
+
+
+def ship_kernel(devices, cap, nodes, first, chunks, place, at, *refs):
     updated, stress, (pair, out) = refs[:chunks], refs[chunks:2 * chunks], refs[2 * chunks:]
     me, plane, lane, lanes = whereabouts(devices)
-    group = pair.shape[0] // 2
-    rows = placed_rows(first, 2 * group, place, updated)
-    put(pair, pl.multiple_of((1 - plane // 2) * group, group), rows[0:group])
-    put(pair, pl.multiple_of(plane // 2 * group, group), rows[group:])
+    group, span = lanes * cap, lanes * height(cap, nodes)
+    rows = placed_rows(first, 2 * group, place, updated, up(nodes, 256))
+    put(pair, pl.multiple_of((1 - plane // 2) * span, 8), rows[0:group], cap, nodes)
+    put(pair, pl.multiple_of(plane // 2 * span, 8), rows[group:], cap, nodes)
     hi, lo = halves(jnp.concatenate([ref[...] for ref in stress], axis=1))
     serves = hot(at[0:1, :], hi.shape[1])
     out[...] = (dot(hi, serves) + dot(lo, serves))[0:out.shape[0], :]
 
 
-def join_kernel(cap, *refs):
+def join_kernel(tall, *refs):
     landed, blocks = refs[:3], refs[3:]
     for i, block in enumerate(blocks):
         for k, rows in enumerate(landed):
-            block[k * cap:(k + 1) * cap, :] = rows[i * cap:(i + 1) * cap, :]
+            block[k * tall:(k + 1) * tall, :] = rows[i * tall:(i + 1) * tall, :]
 
 
 def land(tile, out, stage, sem, slot, at):
@@ -315,33 +360,30 @@
     return copy
 
 
-def land_group(block, count, plane, out, stage, sem, slot):
-    height = block.shape[0] // count
-    copies = []
-    for part in range(count):
-        tile = block[part * height:(part + 1) * height, :]
-        copies.append(land(tile, out, stage, sem, slot + part, plane * count + part))
-    return copies
-
-
 def land_kernel(devices, cap, pair, *refs):
     blocks, (out, stage, sem, gather) = refs[:-4], refs[-4:]
     me, plane, lane, lanes = whereabouts(devices)
-    group = pair.shape[0] // 2
+    nodes, tall = out.shape[0], height(cap, out.shape[0])
+    tiles = lanes * cap // LANES
     copies = []
-    for part in range(2):
-        source = jnp.where(plane // 2 == part, plane, plane ^ 3)
-        block = pair.at[part * group:(part + 1) * group, :]
-        copies += land_group(block, 2, source, out, stage, sem, 2 * part)
-    for i, apart in enumerate((2, 1)):
+    for i in range(4):
+        target = gather.at[i]
         for k in range(lanes):
+            if i < 2:
+                take(pair, (i * lanes + k) * tall, target, k * cap, cap, nodes)
+                continue
             at = pl.multiple_of((lane ^ k) * cap, cap)
-            if i == 1 and k % 2 == 1:
-                gather[i, pl.ds(at, cap), :] = blocks[lanes // 2 + k // 2][...]
+            if i == 3 and k % 2 == 1:
+                take(blocks[lanes // 2 + k // 2], 0, target, at, cap, nodes)
             else:
-                top = (2 * (k % 2) + i) * cap
-                gather[i, pl.ds(at, cap), :] = blocks[k // 2][top:top + cap, :]
-        copies += land_group(gather.at[i], 2, plane ^ apart, out, stage, sem, 4 + 2 * i)
+                take(blocks[k // 2], (2 * (k % 2) + i - 2) * tall, target, at, cap, nodes)
+        if i < 2:
+            source = jnp.where(plane // 2 == i, plane, plane ^ 3)
+        else:
+            source = plane ^ (4 - i)
+        for part in range(tiles):
+            tile = gather[i, part * LANES:(part + 1) * LANES, :]
+            copies.append(land(tile, out, stage, sem, i * tiles + part, source * tiles + part))
     for copy in copies:
         copy.wait()
 
@@ -398,16 +440,19 @@
     lanes = devices // PLANES
     half = lanes // 2
     group = lanes * per_peer
-    block = lambda height: jax.ShapeDtypeStruct((height, deep), f32)
+    tall = height(per_peer, nodes)
+    block = lambda count: jax.ShapeDtypeStruct((count * tall, LANES), f32)
     whole = lambda shape: pl.BlockSpec(shape, lambda i: (0,) * len(shape))
     updated, stress_s, ready = [], [], []
     left = 0
     for span in (LANES,) * (columns // LANES):
         part = lambda height: pl.BlockSpec((height, span), lambda i, at=left // span: (0, at))
         wide = comps * span
-        outs = [block(LANES)] if len(updated) < 3 else [block(per_peer)] * half
+        outs = [block(half)] if len(updated) < 3 else [block(1)] * half
         done = pl.pallas_call(
-            functools.partial(solve_kernel, 1.0 / math.sqrt(comps * nodes), left, len(updated)),
+            functools.partial(
+                solve_kernel, 1.0 / math.sqrt(comps * nodes), per_peer, nodes, left, len(updated)
+            ),
             grid=(1,),
             out_shape=(
                 jax.ShapeDtypeStruct((rows, span), f32),
@@ -432,8 +477,8 @@
         ready.append(done[2:])
         left += span
     pair, stress_out = pl.pallas_call(
-        functools.partial(ship_kernel, devices, 2 * group, len(updated)),
-        out_shape=(block(2 * group), jax.ShapeDtypeStruct((voigt, columns), f32)),
+        functools.partial(ship_kernel, devices, per_peer, nodes, 2 * group, len(updated)),
+        out_shape=(block(2 * lanes), jax.ShapeDtypeStruct((voigt, columns), f32)),
         in_specs=[vmem] * (2 + 2 * len(updated)),
         out_specs=[vmem] * 2,
         compiler_params=params(),
@@ -450,17 +495,17 @@
     pair, *straight = lax.optimization_barrier((pair, *ready[-1]))
     planes = [list(range(z * lanes, (z + 1) * lanes)) for z in range(PLANES)]
     pair = lax.all_to_all(
-        pair.reshape(2 * lanes, per_peer, deep), axes, split_axis=0, concat_axis=0, tiled=True,
+        pair.reshape(2 * lanes, tall, LANES), axes, split_axis=0, concat_axis=0, tiled=True,
         axis_index_groups=[planes[0] + planes[3], planes[1] + planes[2]],
-    ).reshape(2 * group, deep)
+    ).reshape(2 * lanes * tall, LANES)
     hops = (2 * lanes, lanes, 2 * lanes + 1)
     landed = []
     for (sent,), mask in zip(ready, hops):
         landed.append(hop(sent, mask))
         landed[-2:] = lax.optimization_barrier(tuple(landed[-2:]))
     joined = pl.pallas_call(
-        functools.partial(join_kernel, per_peer),
-        out_shape=(block(3 * per_peer),) * half,
+        functools.partial(join_kernel, tall),
+        out_shape=(block(3),) * half,
         in_specs=[vmem] * 3,
         out_specs=[vmem] * half,
         compiler_params=params(),
@@ -474,7 +519,7 @@
         in_specs=[vmem] * (1 + 2 * half),
         out_specs=pl.BlockSpec(memory_space=pl.ANY),
         scratch_shapes=[pltpu.VMEM((8, nodes, LANES), f32), pltpu.SemaphoreType.DMA((8,)),
-                        pltpu.VMEM((2, group, deep), f32)],
+                        pltpu.VMEM((4, group, deep), f32)],
         compiler_params=params(),
     )(pair, *joined, *direct)
     return (new_history, stress_out)

time: 96 us -> 94.8 us (0.987)
  no operation moved by 1% of the time
where the time goes in v2:
time: 94.8 us; the launch traced here: 94.5 us
  Pallas kernels  44.8 us (47%)
  waiting for transfers between devices  28.5 us (30%)
  starting transfers between devices  20.3 us (21%)
    pallas_call x4, Pallas kernels, shards(): pl.pallas_call(functools.partial(solve_kernel, 1.0 / math.sqrt(comps * no...  31.6 us
    ppermute x10, waiting for transfers between devices, hop(): return lax.ppermute(sent, axes, [(s, s ^ mask) for s in range(devices)])  28.5 us
    ppermute x10, starting transfers between devices, hop(): return lax.ppermute(sent, axes, [(s, s ^ mask) for s in range(devices)])  14.4 us
    all_to_all x1, starting transfers between devices, shards(): lax.all_to_all(pair.reshape(2 * lanes, tall, LANES), axes, split_axis=0,...  5.8 us
    pallas_call x1, Pallas kernels, shards(): pl.pallas_call(functools.partial(prep_kernel, devices, per_peer, comps, v...  4.68 us
    pallas_call x1, Pallas kernels, shards(): pl.pallas_call(functools.partial(land_kernel, devices, per_peer), out_sha...  3.56 us
    pallas_call x1, Pallas kernels, shards(): pl.pallas_call(functools.partial(ship_kernel, devices, per_peer, nodes, 2...  3.14 us
  transfers between devices with their start and end apart: 11, of which 6 were waited for; matrix products, arithmetic and copies ran while one was open for 0% of the time, Pallas kernels for 29%

profile of v2, /device:TPU:0, one launch (start us, length us, event | category | flops | bytes accessed | tf_op | source)
XLA Modules:
  0.0 94.5 jit_solution(10353305538964867823)
XLA Ops:
  0.6 1.8 %shard_map.104.refs_0_ = f32[8192,729]{1,0:T(8,128)} custom-call(f32[3,6,729]{2,1,0:T(8,128)} %coupling.1, f32[3,729]{1,0:T(4,128)} %plastic.1, f32[6,512]{1,0:T(8,128)} %strain.1, s32[1,512]{1,0:T(1,128)} %bitcast.3, s32[1,512]{1,0:T(1,128)} %qp.1, s32[9,9]{1,0:T(8,128)} %pattern.1), custom_call_target="tpu_custom_call" | custom-call | tf_op jit(solution)/shard_map/pallas_call | solution.py:408
  2.4 4.7 %shard_map.105 = (bf16[736,768]{1,0:T(8,128)(2,1)S(1)}, bf16[736,768]{1,0:T(8,128)(2,1)S(1)}, f32[736,512]{1,0:T(8,128)S(1)}, f32[736,512]{1,0:T(8,128)S(1)}, f3...) custom-call(f32[8192,729]{1,0:T(8,128)} %shard_map.104.refs_0_, ...), custom_call_target="tpu_custom_call" | custom-call | tf_op jit(solution)/shard_map/pallas_call | solution.py:417
  7.1 7.8 %shard_map.106 = (f32[736,128]{1,0:T(8,128)S(1)}, f32[8,128]{1,0:T(8,128)S(1)}, f32[736,128]{1,0:T(8,128)S(1)}) custom-call(bf16[736,768]{1,0:T(8,128)(2,1)S(1)} %get-tuple-element.44.khi, bf16[736,768]{1,0:T(8,128)(2,1)S(1)} %get-tuple-element.45.klo, f32[736,512]{1,0:T(8,128)S(1)} %get-tuple-element.46.hist, f32[736,512]{1,0:T(8,128)S(1)} %get-tuple-element.47.weight, ...), custom_call_target="tpu_custom_call" | custom-call | flops 3906994176 | bytes 1048576 | tf_op jit(solution)/shard_map/pallas_call | solution.py:452
  14.9 4.1 %collective-permute-start = (f32[736,128]{1,0:T(8,128)S(1)}, f32[736,128]{1,0:T(8,128)S(1)}, u32[]{:S(2)}, u32[]{:S(2)}) collective-permute-start(f32[736,128]{1,0:T(8,128)S(1)} %get-tuple-element.66), channel_id=1, source_target_pairs={{0,16},{1,17},{2,18},{3,19},{4,20},{5,21},{6,22},{7,23},{8,24},{9,... | collective-permute-start | bytes 1130504 | tf_op jit(solution)/shard_map/ppermute | solution.py:493
  19.0 7.8 %shard_map.107 = (f32[736,128]{1,0:T(8,128)S(1)}, f32[8,128]{1,0:T(8,128)S(1)}, f32[736,128]{1,0:T(8,128)S(1)}) custom-call(bf16[736,768]{1,0:T(8,128)(2,1)S(1)} %get-tuple-element.44.khi, bf16[736,768]{1,0:T(8,128)(2,1)S(1)} %get-tuple-element.45.klo, f32[736,512]{1,0:T(8,128)S(1)} %get-tuple-element.46.hist, f32[736,512]{1,0:T(8,128)S(1)} %get-tuple-element.47.weight, ...), custom_call_target="tpu_custom_call" | custom-call | flops 3906994176 | bytes 1048576 | tf_op jit(solution)/shard_map/pallas_call | solution.py:452
  26.8 1.6 %collective-permute-start.1 = (f32[736,128]{1,0:T(8,128)S(1)}, f32[736,128]{1,0:T(8,128)S(1)}, u32[]{:S(2)}, u32[]{:S(2)}) collective-permute-start(f32[736,128]{1,0:T(8,128)S(1)} %get-tuple-element.67), channel_id=1, source_target_pairs={{0,8},{1,9},{2,10},{3,11},{4,12},{5,13},{6,14},{7,15},{8,0},{9,1},... | collective-permute-start | bytes 1130504 | tf_op jit(solution)/shard_map/ppermute | solution.py:493
  28.5 8.1 %shard_map.108 = (f32[736,128]{1,0:T(8,128)S(1)}, f32[8,128]{1,0:T(8,128)S(1)}, f32[736,128]{1,0:T(8,128)S(1)}) custom-call(bf16[736,768]{1,0:T(8,128)(2,1)S(1)} %get-tuple-element.44.khi, bf16[736,768]{1,0:T(8,128)(2,1)S(1)} %get-tuple-element.45.klo, f32[736,512]{1,0:T(8,128)S(1)} %get-tuple-element.46.hist, f32[736,512]{1,0:T(8,128)S(1)} %get-tuple-element.47.weight, ...), custom_call_target="tpu_custom_call" | custom-call | flops 3906994176 | bytes 1048576 | tf_op jit(solution)/shard_map/pallas_call | solution.py:452
  36.6 7.9 %shard_map.109 = (f32[736,128]{1,0:T(8,128)S(1)}, f32[8,128]{1,0:T(8,128)S(1)}, f32[184,128]{1,0:T(8,128)S(1)}, f32[184,128]{1,0:T(8,128)S(1)}, f32[184,128]{1,0:T(8,128)S(1)}, /*index=5*/f32[184,128]{1,0:T(8,128)S(1)}) custom-call(bf16[736,768]{1,0:T(8,128)(2,1)S(1)} %get-tuple-element.44.khi, bf16[736,768]{1,0:T(8,128)(2,1)S(1)} %get-tuple-element.45.klo, ...), custom_call_target="tpu_custom_call" | custom-call | flops 3906994176 | bytes 1048576 | tf_op jit(solution)/shard_map/pallas_call | solution.py:452
  44.6 3.1 %shard_map.110 = (f32[2944,128]{1,0:T(8,128)}, f32[6,512]{1,0:T(8,128)}) custom-call(s32[8,512]{1,0:T(8,128)S(1)} %get-tuple-element.42.place, s32[8,512]{1,0:T(8,128)S(1)} %get-tuple-element.43.at, f32[736,128]{1,0:T(8,128)S(1)} %get-tuple-element.52.refs_0_, f32[736,128]{1,0:T(8,128)S(1)} %get-tuple-element.53.refs_1_, ...), custom_call_target="tpu_custom_call" | custom-call | flops 771751936 | bytes 1048576 | tf_op jit(solution)/shard_map/pallas_call | solution.py:479
  47.7 5.8 %all-to-all-start = ((f32[16,184,128]{2,1,0:T(8,128)}), f32[16,184,128]{2,1,0:T(8,128)}, u32[]{:S(2)}, u32[]{:S(2)}) async-start(f32[16,184,128]{2,1,0:T(8,128)} %bitcast.1), calls=%async_computation | async-start | bytes 3014656 | tf_op jit(solution)/shard_map/all_to_all | solution.py:497
  53.5 2.4 %collective-permute-done.2.refs_2_ = f32[736,128]{1,0:T(8,128)S(1)} collective-permute-done((f32[736,128]{1,0:T(8,128)S(1)}, f32[736,128]{1,0:T(8,128)S(1)}, u32[]{:S(2)}, u32[]{:S(2)}) %collective-permute-start.2) | collective-permute-done | bytes 376864 | tf_op jit(solution)/shard_map/ppermute | solution.py:493
  56.0 0.1 shard_map.111
  56.0 1.6 %collective-permute-start.3 = (f32[552,128]{1,0:T(8,128)S(1)}, f32[552,128]{1,0:T(8,128)S(1)}, u32[]{:S(2)}, u32[]{:S(2)}) collective-permute-start(f32[552,128]{1,0:T(8,128)S(1)} %get-tuple-element.74), channel_id=1, source_target_pairs={{0,2},{1,3},{2,0},{3,1},{4,6},{5,7},{6,4},{7,5},{8,10},{9,11},{10,... | collective-permute-start | bytes 847880 | tf_op jit(solution)/shard_map/ppermute | solution.py:493
  57.6 1.5 %collective-permute-start.4 = (f32[552,128]{1,0:T(8,128)S(1)}, f32[552,128]{1,0:T(8,128)S(1)}, u32[]{:S(2)}, u32[]{:S(2)}) collective-permute-start(f32[552,128]{1,0:T(8,128)S(1)} %get-tuple-element.75), channel_id=1, source_target_pairs={{0,4},{1,5},{2,6},{3,7},{4,0},{5,1},{6,2},{7,3},{8,12},{9,13},{10,... | collective-permute-start | bytes 847880 | tf_op jit(solution)/shard_map/ppermute | solution.py:493
  59.1 0.5 collective-permute-start.5
  59.6 2.7 %collective-permute-start.7 = (f32[184,128]{1,0:T(8,128)S(1)}, f32[184,128]{1,0:T(8,128)S(1)}, u32[]{:S(2)}, u32[]{:S(2)}) collective-permute-start(f32[184,128]{1,0:T(8,128)S(1)} %get-tuple-element.78), channel_id=1, source_target_pairs={{0,11},{1,10},{2,9},{3,8},{4,15},{5,14},{6,13},{7,12},{8,3},{9,2},... | collective-permute-start | bytes 282632 | tf_op jit(solution)/shard_map/ppermute | solution.py:493
  62.3 14.5 %collective-permute-done.6.refs_4_ = f32[184,128]{1,0:T(8,128)S(1)} collective-permute-done((f32[184,128]{1,0:T(8,128)S(1)}, f32[184,128]{1,0:T(8,128)S(1)}, u32[]{:S(2)}, u32[]{:S(2)}) %collective-permute-start.6) | collective-permute-done | bytes 94240 | tf_op jit(solution)/shard_map/ppermute | solution.py:493
  76.8 1.2 %collective-permute-start.8 = (f32[184,128]{1,0:T(8,128)S(1)}, f32[184,128]{1,0:T(8,128)S(1)}, u32[]{:S(2)}, u32[]{:S(2)}) collective-permute-start(f32[184,128]{1,0:T(8,128)S(1)} %get-tuple-element.79), channel_id=1, source_target_pairs={{0,13},{1,12},{2,15},{3,14},{4,9},{5,8},{6,11},{7,10},{8,5},{9,4},... | collective-permute-start | bytes 282632 | tf_op jit(solution)/shard_map/ppermute | solution.py:493
  78.0 1.7 %collective-permute-done.7.refs_5_ = f32[184,128]{1,0:T(8,128)S(1)} collective-permute-done((f32[184,128]{1,0:T(8,128)S(1)}, f32[184,128]{1,0:T(8,128)S(1)}, u32[]{:S(2)}, u32[]{:S(2)}) %collective-permute-start.7) | collective-permute-done | bytes 94240 | tf_op jit(solution)/shard_map/ppermute | solution.py:493
  79.7 1.2 %collective-permute-start.9 = (f32[184,128]{1,0:T(8,128)S(1)}, f32[184,128]{1,0:T(8,128)S(1)}, u32[]{:S(2)}, u32[]{:S(2)}) collective-permute-start(f32[184,128]{1,0:T(8,128)S(1)} %get-tuple-element.80), channel_id=1, source_target_pairs={{0,15},{1,14},{2,13},{3,12},{4,11},{5,10},{6,9},{7,8},{8,7},{9,6},... | collective-permute-start | bytes 282632 | tf_op jit(solution)/shard_map/ppermute | solution.py:493
  80.9 2.4 %collective-permute-done.8.refs_6_ = f32[184,128]{1,0:T(8,128)S(1)} collective-permute-done((f32[184,128]{1,0:T(8,128)S(1)}, f32[184,128]{1,0:T(8,128)S(1)}, u32[]{:S(2)}, u32[]{:S(2)}) %collective-permute-start.8) | collective-permute-done | bytes 94240 | tf_op jit(solution)/shard_map/ppermute | solution.py:493
  83.4 3.2 %collective-permute-done.9.refs_7_ = f32[184,128]{1,0:T(8,128)S(1)} collective-permute-done((f32[184,128]{1,0:T(8,128)S(1)}, f32[184,128]{1,0:T(8,128)S(1)}, u32[]{:S(2)}, u32[]{:S(2)}) %collective-permute-start.9) | collective-permute-done | bytes 94240 | tf_op jit(solution)/shard_map/ppermute | solution.py:493
  86.6 4.2 %collective-permute-done.5.refs_3_ = f32[552,128]{1,0:T(8,128)S(1)} collective-permute-done((f32[552,128]{1,0:T(8,128)S(1)}, f32[552,128]{1,0:T(8,128)S(1)}, u32[]{:S(2)}, u32[]{:S(2)}) %collective-permute-start.5) | collective-permute-done | bytes 282656 | tf_op jit(solution)/shard_map/ppermute | solution.py:493
  90.8 3.6 %shard_map.112 = f32[729,1024]{1,0:T(8,128)} custom-call(f32[2944,128]{1,0:T(8,128)} %bitcast.2.pair, f32[552,128]{1,0:T(8,128)S(1)} %get-tuple-element.73.refs_0_, f32[552,128]{1,0:T(8,128)S(1)} %collective-permute-done.3.refs_1_, f32[552,128]{1,0:T(8,128)S(1)} %collective-permute-done.4.refs_2_, f32[552,128]{1,0:T(8,128)S(1)} %collective-permute-done.5.refs_3_, ...), custom_call_target="tpu_custom_call" | custom-call | tf_op jit(solution)/shard_map/pallas_call | solution.py:516
  (7 shorter events, 0.1 us)
Async XLA Ops:
  14.9 38.6 %collective-permute-start = (f32[736,128]{1,0:T(8,128)S(1)}, f32[736,128]{1,0:T(8,128)S(1)}, u32[]{:S(2)}, u32[]{:S(2)}) collective-permute-start(f32[736,128]{1,0:T(8,128)S(1)} %get-tuple-element.66), channel_id=1, source_target_pairs={{0,16},{1,17},{2,18},{3,19},{4,20},{5,21},{6,22},{7,23},{8,24},{9,... | collective-permute-start | bytes 1130504 | tf_op jit(solution)/shard_map/ppermute | solution.py:493
  26.8 26.7 %collective-permute-start.1 = (f32[736,128]{1,0:T(8,128)S(1)}, f32[736,128]{1,0:T(8,128)S(1)}, u32[]{:S(2)}, u32[]{:S(2)}) collective-permute-start(f32[736,128]{1,0:T(8,128)S(1)} %get-tuple-element.67), channel_id=1, source_target_pairs={{0,8},{1,9},{2,10},{3,11},{4,12},{5,13},{6,14},{7,15},{8,0},{9,1},... | collective-permute-start | bytes 1130504 | tf_op jit(solution)/shard_map/ppermute | solution.py:493
  36.5 19.4 %collective-permute-start.2 = (f32[736,128]{1,0:T(8,128)S(1)}, f32[736,128]{1,0:T(8,128)S(1)}, u32[]{:S(2)}, u32[]{:S(2)}) collective-permute-start(f32[736,128]{1,0:T(8,128)S(1)} %get-tuple-element.70), channel_id=1, source_target_pairs={{0,17},{1,16},{2,19},{3,18},{4,21},{5,20},{6,23},{7,22},{8,25},{9,... | collective-permute-start | bytes 1130504 | tf_op jit(solution)/shard_map/ppermute | solution.py:493
  47.7 43.1 %all-to-all-start = ((f32[16,184,128]{2,1,0:T(8,128)}), f32[16,184,128]{2,1,0:T(8,128)}, u32[]{:S(2)}, u32[]{:S(2)}) async-start(f32[16,184,128]{2,1,0:T(8,128)} %bitcast.1), calls=%async_computation | async-start | bytes 3014656 | tf_op jit(solution)/shard_map/all_to_all | solution.py:497
  56.0 30.5 %collective-permute-start.3 = (f32[552,128]{1,0:T(8,128)S(1)}, f32[552,128]{1,0:T(8,128)S(1)}, u32[]{:S(2)}, u32[]{:S(2)}) collective-permute-start(f32[552,128]{1,0:T(8,128)S(1)} %get-tuple-element.74), channel_id=1, source_target_pairs={{0,2},{1,3},{2,0},{3,1},{4,6},{5,7},{6,4},{7,5},{8,10},{9,11},{10,... | collective-permute-start | bytes 847880 | tf_op jit(solution)/shard_map/ppermute | solution.py:493
  57.6 29.0 %collective-permute-start.4 = (f32[552,128]{1,0:T(8,128)S(1)}, f32[552,128]{1,0:T(8,128)S(1)}, u32[]{:S(2)}, u32[]{:S(2)}) collective-permute-start(f32[552,128]{1,0:T(8,128)S(1)} %get-tuple-element.75), channel_id=1, source_target_pairs={{0,4},{1,5},{2,6},{3,7},{4,0},{5,1},{6,2},{7,3},{8,12},{9,13},{10,... | collective-permute-start | bytes 847880 | tf_op jit(solution)/shard_map/ppermute | solution.py:493
  59.1 31.7 %collective-permute-start.5 = (f32[552,128]{1,0:T(8,128)S(1)}, f32[552,128]{1,0:T(8,128)S(1)}, u32[]{:S(2)}, u32[]{:S(2)}) collective-permute-start(f32[552,128]{1,0:T(8,128)S(1)} %get-tuple-element.76), channel_id=1, source_target_pairs={{0,6},{1,7},{2,4},{3,5},{4,2},{5,3},{6,0},{7,1},{8,14},{9,15},{10,... | collective-permute-start | bytes 847880 | tf_op jit(solution)/shard_map/ppermute | solution.py:493
  59.6 17.2 %collective-permute-start.6 = (f32[184,128]{1,0:T(8,128)S(1)}, f32[184,128]{1,0:T(8,128)S(1)}, u32[]{:S(2)}, u32[]{:S(2)}) collective-permute-start(f32[184,128]{1,0:T(8,128)S(1)} %get-tuple-element.77), channel_id=1, source_target_pairs={{0,9},{1,8},{2,11},{3,10},{4,13},{5,12},{6,15},{7,14},{8,1},{9,0},... | collective-permute-start | bytes 282632 | tf_op jit(solution)/shard_map/ppermute | solution.py:493
  59.6 20.1 %collective-permute-start.7 = (f32[184,128]{1,0:T(8,128)S(1)}, f32[184,128]{1,0:T(8,128)S(1)}, u32[]{:S(2)}, u32[]{:S(2)}) collective-permute-start(f32[184,128]{1,0:T(8,128)S(1)} %get-tuple-element.78), channel_id=1, source_target_pairs={{0,11},{1,10},{2,9},{3,8},{4,15},{5,14},{6,13},{7,12},{8,3},{9,2},... | collective-permute-start | bytes 282632 | tf_op jit(solution)/shard_map/ppermute | solution.py:493
  76.8 6.6 %collective-permute-start.8 = (f32[184,128]{1,0:T(8,128)S(1)}, f32[184,128]{1,0:T(8,128)S(1)}, u32[]{:S(2)}, u32[]{:S(2)}) collective-permute-start(f32[184,128]{1,0:T(8,128)S(1)} %get-tuple-element.79), channel_id=1, source_target_pairs={{0,13},{1,12},{2,15},{3,14},{4,9},{5,8},{6,11},{7,10},{8,5},{9,4},... | collective-permute-start | bytes 282632 | tf_op jit(solution)/shard_map/ppermute | solution.py:493
  79.7 6.9 %collective-permute-start.9 = (f32[184,128]{1,0:T(8,128)S(1)}, f32[184,128]{1,0:T(8,128)S(1)}, u32[]{:S(2)}, u32[]{:S(2)}) collective-permute-start(f32[184,128]{1,0:T(8,128)S(1)} %get-tuple-element.80), channel_id=1, source_target_pairs={{0,15},{1,14},{2,13},{3,12},{4,11},{5,10},{6,9},{7,8},{8,7},{9,6},... | collective-permute-start | bytes 282632 | tf_op jit(solution)/shard_map/ppermute | solution.py:493

commit v3 on v2

--- a/solution.py
+++ b/solution.py
@@ -66,13 +66,13 @@
     kfull, pad, stack, sem = refs[18:]
     khi, klo, hist_s, weight_s, strain_s, place_s, qp_s, cstack, loads, pdir = outs
     small, stiff, hist, flag = local
+    pairs = [(sources[0].at[pl.ds(0, small.shape[0]), :], small), (sources[2], hist), (sources[3], flag)]
+    pairs += [(sources[1].at[a], stiff.at[a]) for a in range(stiff.shape[0])]
     copies = [
         pltpu.make_async_copy(source, target, sem.at[i])
-        for i, (source, target) in enumerate(
-            zip((sources[0].at[pl.ds(0, local[0].shape[0]), :], *sources[1:]), local)
-        )
+        for i, (source, target) in enumerate(pairs)
     ]
-    for copy in copies:
+    for copy in copies[:1] + copies[3:] + copies[1:3]:
         copy.start()
     nodes, columns = hist.shape
     nb, blk = stiff.shape[0], stiff.shape[2]
@@ -122,8 +122,8 @@
     strain_s[...] = dot(hi, serves, NT) + dot(lo, serves, NT)
 
     kfull[...] = jnp.zeros_like(kfull)
-    copies[1].wait()
     for a in range(nb):
+        copies[3 + a].wait()
         for b in range(nb):
             kfull[a * blk:(a + 1) * blk, b * blk:(b + 1) * blk] = (
                 stiff[a, b] * small[PATTERN + a * nb + b:PATTERN + a * nb + b + 1, 0:blk]
@@ -133,8 +133,8 @@
     khi[...] = kh
     klo[...] = (k - kh.astype(jnp.float32)).astype(jnp.bfloat16)
 
+    copies[1].wait()
     copies[2].wait()
-    copies[3].wait()
     hi, lo = halves(hist[...])
     hist_s[...] = jnp.zeros_like(hist_s)
     hist_s[0:nodes, :] = dot(hi, order, NT) + dot(lo, order, NT)
@@ -252,7 +252,10 @@
         x = x + alpha * field[last, r, l]
         pushed = flow(c, r) * x
         image[r, 0:span] = pushed if c == 0 else image[r, 0:span] + pushed
-        keep(r, c, (1.5 - weight[r, :]) * x)
+        lead = 2 * c * span
+        split[r, lead:lead + span], split[r, lead + span:lead + 2 * span] = halves(
+            (1.5 - weight[r, :]) * x
+        )
     updated[...] = hist[...] + weight[...] * image[:, 0:span]
     sent = placed_rows(first, LANES, place, [*earlier_updated, updated], split.shape[0])
     part = LANES // len(blocks)
@@ -261,9 +264,8 @@
     out = s
     for c in range(comps):
         cpl = cstack[c]
-        main = dot(cpl, split[0:rows, c * span:(c + 1) * span])
-        minor = dot(cpl, split[0:rows, wide + c * span:wide + (c + 1) * span])
-        out = out + scale * (main[0:8] + main[16:24] + minor[0:8])
+        both = dot(cpl, split[0:rows, 2 * c * span:2 * (c + 1) * span])
+        out = out + scale * (both[0:8, 0:span] + both[16:24, 0:span] + both[0:8, span:])
     stress[...] = out
 
 
@@ -332,14 +334,18 @@
         target[pl.ds(row, quarter), full * LANES:] = jnp.where(lane < LANES // 2, left, right)
 
 
-def ship_kernel(devices, cap, nodes, first, chunks, place, at, *refs):
-    updated, stress, (pair, out) = refs[:chunks], refs[chunks:2 * chunks], refs[2 * chunks:]
+def ship_kernel(devices, cap, nodes, first, place, *refs):
+    updated, pair = refs[:-1], refs[-1]
     me, plane, lane, lanes = whereabouts(devices)
     group, span = lanes * cap, lanes * height(cap, nodes)
     rows = placed_rows(first, 2 * group, place, updated, up(nodes, 256))
     put(pair, pl.multiple_of((1 - plane // 2) * span, 8), rows[0:group], cap, nodes)
     put(pair, pl.multiple_of(plane // 2 * span, 8), rows[group:], cap, nodes)
-    hi, lo = halves(jnp.concatenate([ref[...] for ref in stress], axis=1))
+
+
+def back_kernel(at, *refs):
+    out = refs[-1]
+    hi, lo = halves(jnp.concatenate([ref[...] for ref in refs[:-1]], axis=1))
     serves = hot(at[0:1, :], hi.shape[1])
     out[...] = (dot(hi, serves) + dot(lo, serves))[0:out.shape[0], :]
 
@@ -433,7 +439,7 @@
         scratch_shapes=[pltpu.VMEM((small_rows, nodes), f32)]
         + [pltpu.VMEM(x.shape, x.dtype) for x in inputs[1:]]
         + [pltpu.VMEM((rows, deep), f32), pltpu.VMEM((8, columns), f32),
-           pltpu.VMEM((32, rows), f32), pltpu.SemaphoreType.DMA((4,))],
+           pltpu.VMEM((32, rows), f32), pltpu.SemaphoreType.DMA((3 + stiffness.shape[0],))],
         compiler_params=params(46),
     )(*inputs)
 
@@ -476,16 +482,16 @@
         stress_s.append(done[1])
         ready.append(done[2:])
         left += span
-    pair, stress_out = pl.pallas_call(
-        functools.partial(ship_kernel, devices, per_peer, nodes, 2 * group, len(updated)),
-        out_shape=(block(2 * lanes), jax.ShapeDtypeStruct((voigt, columns), f32)),
-        in_specs=[vmem] * (2 + 2 * len(updated)),
-        out_specs=[vmem] * 2,
+    pair = pl.pallas_call(
+        functools.partial(ship_kernel, devices, per_peer, nodes, 2 * group),
+        out_shape=block(2 * lanes),
+        in_specs=[vmem] * (1 + len(updated)),
+        out_specs=vmem,
         compiler_params=params(),
         cost_estimate=pl.CostEstimate(
             flops=4 * rows * columns * columns, bytes_accessed=2**20, transcendentals=0
         ),
-    )(place_s, qp_s, *updated, *stress_s)
+    )(place_s, *updated)
 
     axes = ("macro", "pool")
 
@@ -513,6 +519,15 @@
     )(*landed)
     joined = [sent if i == 0 else hop(sent, 2 * i) for i, sent in enumerate(joined)]
     direct = [hop(sent, lanes + 2 * i + 1) for i, sent in enumerate(straight)]
+    *stress_s, joined[0] = lax.optimization_barrier((*stress_s, joined[0]))
+    stress_out = pl.pallas_call(
+        back_kernel,
+        out_shape=jax.ShapeDtypeStruct((voigt, columns), f32),
+        in_specs=[vmem] * (1 + len(stress_s)),
+        out_specs=vmem,
+        compiler_params=params(),
+    )(qp_s, *stress_s)
+    joined[0], stress_out = lax.optimization_barrier((joined[0], stress_out))
     new_history = pl.pallas_call(
         functools.partial(land_kernel, devices, per_peer),
         out_shape=jax.ShapeDtypeStruct((nodes, devices * per_peer), f32),

time: 94.8 us -> 95.4 us (level)
  Pallas kernels: 44.8 us -> 46.4 us
where the time goes in v3:
time: 95.4 us; the launch traced here: 95.1 us
  Pallas kernels  46.4 us (49%)
  waiting for transfers between devices  27.6 us (29%)
  starting transfers between devices  20.3 us (21%)
    pallas_call x4, Pallas kernels, shards(): pl.pallas_call(functools.partial(solve_kernel, 1.0 / math.sqrt(comps * no...  31.5 us
    ppermute x10, waiting for transfers between devices, hop(): return lax.ppermute(sent, axes, [(s, s ^ mask) for s in range(devices)])  27.6 us
    ppermute x10, starting transfers between devices, hop(): return lax.ppermute(sent, axes, [(s, s ^ mask) for s in range(devices)])  14.5 us
    all_to_all x1, starting transfers between devices, shards(): lax.all_to_all(pair.reshape(2 * lanes, tall, LANES), axes, split_axis=0,...  5.82 us
    pallas_call x1, Pallas kernels, shards(): pl.pallas_call(functools.partial(prep_kernel, devices, per_peer, comps, v...  5.57 us
    pallas_call x1, Pallas kernels, shards(): pl.pallas_call(functools.partial(land_kernel, devices, per_peer), out_sha...  3.56 us
    pallas_call x1, Pallas kernels, shards(): pl.pallas_call(functools.partial(ship_kernel, devices, per_peer, nodes, 2...  3.02 us
  transfers between devices with their start and end apart: 11, of which 6 were waited for; matrix products, arithmetic and copies ran while one was open for 0% of the time, Pallas kernels for 29%

profile of v3, /device:TPU:0, one launch (start us, length us, event | category | flops | bytes accessed | tf_op | source)
XLA Modules:
  0.0 95.1 jit_solution(5789518818151169039)
XLA Ops:
  0.6 1.7 %shard_map.104.refs_0_ = f32[8192,729]{1,0:T(8,128)} custom-call(f32[3,6,729]{2,1,0:T(8,128)} %coupling.1, f32[3,729]{1,0:T(4,128)} %plastic.1, f32[6,512]{1,0:T(8,128)} %strain.1, s32[1,512]{1,0:T(1,128)} %bitcast.3, s32[1,512]{1,0:T(1,128)} %qp.1, s32[9,9]{1,0:T(8,128)} %pattern.1), custom_call_target="tpu_custom_call" | custom-call | tf_op jit(solution)/shard_map/pallas_call | solution.py:414
  2.4 5.6 %shard_map.105 = (bf16[736,768]{1,0:T(8,128)(2,1)S(1)}, bf16[736,768]{1,0:T(8,128)(2,1)S(1)}, f32[736,512]{1,0:T(8,128)S(1)}, f32[736,512]{1,0:T(8,128)S(1)}, f3...) custom-call(f32[8192,729]{1,0:T(8,128)} %shard_map.104.refs_0_, ...), custom_call_target="tpu_custom_call" | custom-call | tf_op jit(solution)/shard_map/pallas_call | solution.py:423
  7.9 7.8 %shard_map.106 = (f32[736,128]{1,0:T(8,128)S(1)}, f32[8,128]{1,0:T(8,128)S(1)}, f32[736,128]{1,0:T(8,128)S(1)}) custom-call(bf16[736,768]{1,0:T(8,128)(2,1)S(1)} %get-tuple-element.48.khi, bf16[736,768]{1,0:T(8,128)(2,1)S(1)} %get-tuple-element.49.klo, f32[736,512]{1,0:T(8,128)S(1)} %get-tuple-element.50.hist, f32[736,512]{1,0:T(8,128)S(1)} %get-tuple-element.51.weight, ...), custom_call_target="tpu_custom_call" | custom-call | flops 3906994176 | bytes 1048576 | tf_op jit(solution)/shard_map/pallas_call | solution.py:458
  15.7 4.1 %collective-permute-start = (f32[736,128]{1,0:T(8,128)S(1)}, f32[736,128]{1,0:T(8,128)S(1)}, u32[]{:S(2)}, u32[]{:S(2)}) collective-permute-start(f32[736,128]{1,0:T(8,128)S(1)} %get-tuple-element.69), channel_id=1, source_target_pairs={{0,16},{1,17},{2,18},{3,19},{4,20},{5,21},{6,22},{7,23},{8,24},{9,... | collective-permute-start | bytes 1130504 | tf_op jit(solution)/shard_map/ppermute | solution.py:499
  19.8 7.8 %shard_map.107 = (f32[736,128]{1,0:T(8,128)S(1)}, f32[8,128]{1,0:T(8,128)S(1)}, f32[736,128]{1,0:T(8,128)S(1)}) custom-call(bf16[736,768]{1,0:T(8,128)(2,1)S(1)} %get-tuple-element.48.khi, bf16[736,768]{1,0:T(8,128)(2,1)S(1)} %get-tuple-element.49.klo, f32[736,512]{1,0:T(8,128)S(1)} %get-tuple-element.50.hist, f32[736,512]{1,0:T(8,128)S(1)} %get-tuple-element.51.weight, ...), custom_call_target="tpu_custom_call" | custom-call | flops 3906994176 | bytes 1048576 | tf_op jit(solution)/shard_map/pallas_call | solution.py:458
  27.6 1.6 %collective-permute-start.1 = (f32[736,128]{1,0:T(8,128)S(1)}, f32[736,128]{1,0:T(8,128)S(1)}, u32[]{:S(2)}, u32[]{:S(2)}) collective-permute-start(f32[736,128]{1,0:T(8,128)S(1)} %get-tuple-element.70), channel_id=1, source_target_pairs={{0,8},{1,9},{2,10},{3,11},{4,12},{5,13},{6,14},{7,15},{8,0},{9,1},... | collective-permute-start | bytes 1130504 | tf_op jit(solution)/shard_map/ppermute | solution.py:499
  29.3 8.1 %shard_map.108 = (f32[736,128]{1,0:T(8,128)S(1)}, f32[8,128]{1,0:T(8,128)S(1)}, f32[736,128]{1,0:T(8,128)S(1)}) custom-call(bf16[736,768]{1,0:T(8,128)(2,1)S(1)} %get-tuple-element.48.khi, bf16[736,768]{1,0:T(8,128)(2,1)S(1)} %get-tuple-element.49.klo, f32[736,512]{1,0:T(8,128)S(1)} %get-tuple-element.50.hist, f32[736,512]{1,0:T(8,128)S(1)} %get-tuple-element.51.weight, ...), custom_call_target="tpu_custom_call" | custom-call | flops 3906994176 | bytes 1048576 | tf_op jit(solution)/shard_map/pallas_call | solution.py:458
  37.4 7.9 %shard_map.109 = (f32[736,128]{1,0:T(8,128)S(1)}, f32[8,128]{1,0:T(8,128)S(1)}, f32[184,128]{1,0:T(8,128)S(1)}, f32[184,128]{1,0:T(8,128)S(1)}, f32[184,128]{1,0:T(8,128)S(1)}, /*index=5*/f32[184,128]{1,0:T(8,128)S(1)}) custom-call(bf16[736,768]{1,0:T(8,128)(2,1)S(1)} %get-tuple-element.48.khi, bf16[736,768]{1,0:T(8,128)(2,1)S(1)} %get-tuple-element.49.klo, ...), custom_call_target="tpu_custom_call" | custom-call | flops 3906994176 | bytes 1048576 | tf_op jit(solution)/shard_map/pallas_call | solution.py:458
  45.3 3.0 %shard_map.110 = f32[2944,128]{1,0:T(8,128)} custom-call(s32[8,512]{1,0:T(8,128)S(1)} %get-tuple-element.47.place, f32[736,128]{1,0:T(8,128)S(1)} %get-tuple-element.56.refs_0_, f32[736,128]{1,0:T(8,128)S(1)} %get-tuple-element.57.refs_1_, f32[736,128]{1,0:T(8,128)S(1)} %get-tuple-element.58.refs_2_, f32[736,128]{1,0:T(8,128)S(1)} %get-tuple-element.59.refs_3_), custom_call_target="tpu_custom_call" | custom-call | flops 771751936 | bytes 1048576 | tf_op jit(solution)/shard_map/pallas_call | solution.py:485
  48.3 5.8 %all-to-all-start = ((f32[16,184,128]{2,1,0:T(8,128)}), f32[16,184,128]{2,1,0:T(8,128)}, u32[]{:S(2)}, u32[]{:S(2)}) async-start(f32[16,184,128]{2,1,0:T(8,128)} %bitcast.1), calls=%async_computation | async-start | bytes 3014656 | tf_op jit(solution)/shard_map/all_to_all | solution.py:503
  54.2 2.7 %collective-permute-done.2.refs_2_ = f32[736,128]{1,0:T(8,128)S(1)} collective-permute-done((f32[736,128]{1,0:T(8,128)S(1)}, f32[736,128]{1,0:T(8,128)S(1)}, u32[]{:S(2)}, u32[]{:S(2)}) %collective-permute-start.2) | collective-permute-done | bytes 376864 | tf_op jit(solution)/shard_map/ppermute | solution.py:499
  56.9 1.5 %collective-permute-start.3 = (f32[552,128]{1,0:T(8,128)S(1)}, f32[552,128]{1,0:T(8,128)S(1)}, u32[]{:S(2)}, u32[]{:S(2)}) collective-permute-start(f32[552,128]{1,0:T(8,128)S(1)} %get-tuple-element.84), channel_id=1, source_target_pairs={{0,2},{1,3},{2,0},{3,1},{4,6},{5,7},{6,4},{7,5},{8,10},{9,11},{10,... | collective-permute-start | bytes 847880 | tf_op jit(solution)/shard_map/ppermute | solution.py:499
  58.4 1.5 %collective-permute-start.4 = (f32[552,128]{1,0:T(8,128)S(1)}, f32[552,128]{1,0:T(8,128)S(1)}, u32[]{:S(2)}, u32[]{:S(2)}) collective-permute-start(f32[552,128]{1,0:T(8,128)S(1)} %get-tuple-element.85), channel_id=1, source_target_pairs={{0,4},{1,5},{2,6},{3,7},{4,0},{5,1},{6,2},{7,3},{8,12},{9,13},{10,... | collective-permute-start | bytes 847880 | tf_op jit(solution)/shard_map/ppermute | solution.py:499
  60.0 0.5 collective-permute-start.5
  60.4 2.7 %collective-permute-start.7 = (f32[184,128]{1,0:T(8,128)S(1)}, f32[184,128]{1,0:T(8,128)S(1)}, u32[]{:S(2)}, u32[]{:S(2)}) collective-permute-start(f32[184,128]{1,0:T(8,128)S(1)} %get-tuple-element.88), channel_id=1, source_target_pairs={{0,11},{1,10},{2,9},{3,8},{4,15},{5,14},{6,13},{7,12},{8,3},{9,2},... | collective-permute-start | bytes 282632 | tf_op jit(solution)/shard_map/ppermute | solution.py:499
  63.1 14.3 %collective-permute-done.6.refs_4_ = f32[184,128]{1,0:T(8,128)S(1)} collective-permute-done((f32[184,128]{1,0:T(8,128)S(1)}, f32[184,128]{1,0:T(8,128)S(1)}, u32[]{:S(2)}, u32[]{:S(2)}) %collective-permute-start.6) | collective-permute-done | bytes 94240 | tf_op jit(solution)/shard_map/ppermute | solution.py:499
  77.4 1.2 %collective-permute-start.8 = (f32[184,128]{1,0:T(8,128)S(1)}, f32[184,128]{1,0:T(8,128)S(1)}, u32[]{:S(2)}, u32[]{:S(2)}) collective-permute-start(f32[184,128]{1,0:T(8,128)S(1)} %get-tuple-element.89), channel_id=1, source_target_pairs={{0,13},{1,12},{2,15},{3,14},{4,9},{5,8},{6,11},{7,10},{8,5},{9,4},... | collective-permute-start | bytes 282632 | tf_op jit(solution)/shard_map/ppermute | solution.py:499
  78.6 1.7 %collective-permute-done.7.refs_5_ = f32[184,128]{1,0:T(8,128)S(1)} collective-permute-done((f32[184,128]{1,0:T(8,128)S(1)}, f32[184,128]{1,0:T(8,128)S(1)}, u32[]{:S(2)}, u32[]{:S(2)}) %collective-permute-start.7) | collective-permute-done | bytes 94240 | tf_op jit(solution)/shard_map/ppermute | solution.py:499
  80.3 1.3 %collective-permute-start.9 = (f32[184,128]{1,0:T(8,128)S(1)}, f32[184,128]{1,0:T(8,128)S(1)}, u32[]{:S(2)}, u32[]{:S(2)}) collective-permute-start(f32[184,128]{1,0:T(8,128)S(1)} %get-tuple-element.90), channel_id=1, source_target_pairs={{0,15},{1,14},{2,13},{3,12},{4,11},{5,10},{6,9},{7,8},{8,7},{9,6},... | collective-permute-start | bytes 282632 | tf_op jit(solution)/shard_map/ppermute | solution.py:499
  81.6 0.9 shard_map.112
  82.5 1.1 %collective-permute-done.8.refs_6_ = f32[184,128]{1,0:T(8,128)S(1)} collective-permute-done((f32[184,128]{1,0:T(8,128)S(1)}, f32[184,128]{1,0:T(8,128)S(1)}, u32[]{:S(2)}, u32[]{:S(2)}) %collective-permute-start.8) | collective-permute-done | bytes 94240 | tf_op jit(solution)/shard_map/ppermute | solution.py:499
  83.6 3.5 %collective-permute-done.9.refs_7_ = f32[184,128]{1,0:T(8,128)S(1)} collective-permute-done((f32[184,128]{1,0:T(8,128)S(1)}, f32[184,128]{1,0:T(8,128)S(1)}, u32[]{:S(2)}, u32[]{:S(2)}) %collective-permute-start.9) | collective-permute-done | bytes 94240 | tf_op jit(solution)/shard_map/ppermute | solution.py:499
  87.2 4.2 %collective-permute-done.5.refs_3_ = f32[552,128]{1,0:T(8,128)S(1)} collective-permute-done((f32[552,128]{1,0:T(8,128)S(1)}, f32[552,128]{1,0:T(8,128)S(1)}, u32[]{:S(2)}, u32[]{:S(2)}) %collective-permute-start.5) | collective-permute-done | bytes 282656 | tf_op jit(solution)/shard_map/ppermute | solution.py:499
  91.4 3.6 %shard_map.113 = f32[729,1024]{1,0:T(8,128)} custom-call(f32[2944,128]{1,0:T(8,128)} %bitcast.2.pair, f32[552,128]{1,0:T(8,128)S(1)} %get-tuple-element.83.refs_0_, f32[552,128]{1,0:T(8,128)S(1)} %collective-permute-done.3.refs_1_, f32[552,128]{1,0:T(8,128)S(1)} %collective-permute-done.4.refs_2_, f32[552,128]{1,0:T(8,128)S(1)} %collective-permute-done.5.refs_3_, ...), custom_call_target="tpu_custom_call" | custom-call | tf_op jit(solution)/shard_map/pallas_call | solution.py:531
  (8 shorter events, 0.2 us)
Async XLA Ops:
  15.7 38.4 %collective-permute-start = (f32[736,128]{1,0:T(8,128)S(1)}, f32[736,128]{1,0:T(8,128)S(1)}, u32[]{:S(2)}, u32[]{:S(2)}) collective-permute-start(f32[736,128]{1,0:T(8,128)S(1)} %get-tuple-element.69), channel_id=1, source_target_pairs={{0,16},{1,17},{2,18},{3,19},{4,20},{5,21},{6,22},{7,23},{8,24},{9,... | collective-permute-start | bytes 1130504 | tf_op jit(solution)/shard_map/ppermute | solution.py:499
  27.6 26.5 %collective-permute-start.1 = (f32[736,128]{1,0:T(8,128)S(1)}, f32[736,128]{1,0:T(8,128)S(1)}, u32[]{:S(2)}, u32[]{:S(2)}) collective-permute-start(f32[736,128]{1,0:T(8,128)S(1)} %get-tuple-element.70), channel_id=1, source_target_pairs={{0,8},{1,9},{2,10},{3,11},{4,12},{5,13},{6,14},{7,15},{8,0},{9,1},... | collective-permute-start | bytes 1130504 | tf_op jit(solution)/shard_map/ppermute | solution.py:499
  37.4 19.5 %collective-permute-start.2 = (f32[736,128]{1,0:T(8,128)S(1)}, f32[736,128]{1,0:T(8,128)S(1)}, u32[]{:S(2)}, u32[]{:S(2)}) collective-permute-start(f32[736,128]{1,0:T(8,128)S(1)} %get-tuple-element.73), channel_id=1, source_target_pairs={{0,17},{1,16},{2,19},{3,18},{4,21},{5,20},{6,23},{7,22},{8,25},{9,... | collective-permute-start | bytes 1130504 | tf_op jit(solution)/shard_map/ppermute | solution.py:499
  48.3 43.1 %all-to-all-start = ((f32[16,184,128]{2,1,0:T(8,128)}), f32[16,184,128]{2,1,0:T(8,128)}, u32[]{:S(2)}, u32[]{:S(2)}) async-start(f32[16,184,128]{2,1,0:T(8,128)} %bitcast.1), calls=%async_computation | async-start | bytes 3014656 | tf_op jit(solution)/shard_map/all_to_all | solution.py:503
  56.9 30.3 %collective-permute-start.3 = (f32[552,128]{1,0:T(8,128)S(1)}, f32[552,128]{1,0:T(8,128)S(1)}, u32[]{:S(2)}, u32[]{:S(2)}) collective-permute-start(f32[552,128]{1,0:T(8,128)S(1)} %get-tuple-element.84), channel_id=1, source_target_pairs={{0,2},{1,3},{2,0},{3,1},{4,6},{5,7},{6,4},{7,5},{8,10},{9,11},{10,... | collective-permute-start | bytes 847880 | tf_op jit(solution)/shard_map/ppermute | solution.py:499
  58.4 28.7 %collective-permute-start.4 = (f32[552,128]{1,0:T(8,128)S(1)}, f32[552,128]{1,0:T(8,128)S(1)}, u32[]{:S(2)}, u32[]{:S(2)}) collective-permute-start(f32[552,128]{1,0:T(8,128)S(1)} %get-tuple-element.85), channel_id=1, source_target_pairs={{0,4},{1,5},{2,6},{3,7},{4,0},{5,1},{6,2},{7,3},{8,12},{9,13},{10,... | collective-permute-start | bytes 847880 | tf_op jit(solution)/shard_map/ppermute | solution.py:499
  60.0 31.4 %collective-permute-start.5 = (f32[552,128]{1,0:T(8,128)S(1)}, f32[552,128]{1,0:T(8,128)S(1)}, u32[]{:S(2)}, u32[]{:S(2)}) collective-permute-start(f32[552,128]{1,0:T(8,128)S(1)} %get-tuple-element.86), channel_id=1, source_target_pairs={{0,6},{1,7},{2,4},{3,5},{4,2},{5,3},{6,0},{7,1},{8,14},{9,15},{10,... | collective-permute-start | bytes 847880 | tf_op jit(solution)/shard_map/ppermute | solution.py:499
  60.4 16.9 %collective-permute-start.6 = (f32[184,128]{1,0:T(8,128)S(1)}, f32[184,128]{1,0:T(8,128)S(1)}, u32[]{:S(2)}, u32[]{:S(2)}) collective-permute-start(f32[184,128]{1,0:T(8,128)S(1)} %get-tuple-element.87), channel_id=1, source_target_pairs={{0,9},{1,8},{2,11},{3,10},{4,13},{5,12},{6,15},{7,14},{8,1},{9,0},... | collective-permute-start | bytes 282632 | tf_op jit(solution)/shard_map/ppermute | solution.py:499
  60.4 19.9 %collective-permute-start.7 = (f32[184,128]{1,0:T(8,128)S(1)}, f32[184,128]{1,0:T(8,128)S(1)}, u32[]{:S(2)}, u32[]{:S(2)}) collective-permute-start(f32[184,128]{1,0:T(8,128)S(1)} %get-tuple-element.88), channel_id=1, source_target_pairs={{0,11},{1,10},{2,9},{3,8},{4,15},{5,14},{6,13},{7,12},{8,3},{9,2},... | collective-permute-start | bytes 282632 | tf_op jit(solution)/shard_map/ppermute | solution.py:499
  77.4 6.2 %collective-permute-start.8 = (f32[184,128]{1,0:T(8,128)S(1)}, f32[184,128]{1,0:T(8,128)S(1)}, u32[]{:S(2)}, u32[]{:S(2)}) collective-permute-start(f32[184,128]{1,0:T(8,128)S(1)} %get-tuple-element.89), channel_id=1, source_target_pairs={{0,13},{1,12},{2,15},{3,14},{4,9},{5,8},{6,11},{7,10},{8,5},{9,4},... | collective-permute-start | bytes 282632 | tf_op jit(solution)/shard_map/ppermute | solution.py:499
  80.3 6.8 %collective-permute-start.9 = (f32[184,128]{1,0:T(8,128)S(1)}, f32[184,128]{1,0:T(8,128)S(1)}, u32[]{:S(2)}, u32[]{:S(2)}) collective-permute-start(f32[184,128]{1,0:T(8,128)S(1)} %get-tuple-element.90), channel_id=1, source_target_pairs={{0,15},{1,14},{2,13},{3,12},{4,11},{5,10},{6,9},{7,8},{8,7},{9,6},... | collective-permute-start | bytes 282632 | tf_op jit(solution)/shard_map/ppermute | solution.py:499

commit v4 on v3

--- a/solution.py
+++ b/solution.py
@@ -66,13 +66,13 @@
     kfull, pad, stack, sem = refs[18:]
     khi, klo, hist_s, weight_s, strain_s, place_s, qp_s, cstack, loads, pdir = outs
     small, stiff, hist, flag = local
-    pairs = [(sources[0].at[pl.ds(0, small.shape[0]), :], small), (sources[2], hist), (sources[3], flag)]
-    pairs += [(sources[1].at[a], stiff.at[a]) for a in range(stiff.shape[0])]
     copies = [
         pltpu.make_async_copy(source, target, sem.at[i])
-        for i, (source, target) in enumerate(pairs)
+        for i, (source, target) in enumerate(
+            zip((sources[0].at[pl.ds(0, local[0].shape[0]), :], *sources[1:]), local)
+        )
     ]
-    for copy in copies[:1] + copies[3:] + copies[1:3]:
+    for copy in copies:
         copy.start()
     nodes, columns = hist.shape
     nb, blk = stiff.shape[0], stiff.shape[2]
@@ -122,8 +122,8 @@
     strain_s[...] = dot(hi, serves, NT) + dot(lo, serves, NT)
 
     kfull[...] = jnp.zeros_like(kfull)
+    copies[1].wait()
     for a in range(nb):
-        copies[3 + a].wait()
         for b in range(nb):
             kfull[a * blk:(a + 1) * blk, b * blk:(b + 1) * blk] = (
                 stiff[a, b] * small[PATTERN + a * nb + b:PATTERN + a * nb + b + 1, 0:blk]
@@ -133,8 +133,8 @@
     khi[...] = kh
     klo[...] = (k - kh.astype(jnp.float32)).astype(jnp.bfloat16)
 
-    copies[1].wait()
     copies[2].wait()
+    copies[3].wait()
     hi, lo = halves(hist[...])
     hist_s[...] = jnp.zeros_like(hist_s)
     hist_s[0:nodes, :] = dot(hi, order, NT) + dot(lo, order, NT)
@@ -367,16 +367,24 @@
 
 
 def land_kernel(devices, cap, pair, *refs):
-    blocks, (out, stage, sem, gather) = refs[:-4], refs[-4:]
+    blocks, (out, stage, sem, gather, fetched, arrival) = refs[:-6], refs[-6:]
     me, plane, lane, lanes = whereabouts(devices)
     nodes, tall = out.shape[0], height(cap, out.shape[0])
-    tiles = lanes * cap // LANES
+    tiles, span = lanes * cap // LANES, lanes * tall
+    fetches = [
+        pltpu.make_async_copy(pair.at[pl.ds(i * span, span), :], fetched.at[i], arrival.at[i])
+        for i in range(2)
+    ]
+    for fetch in fetches:
+        fetch.start()
     copies = []
-    for i in range(4):
+    for i in (2, 3, 0, 1):
+        if i < 2:
+            fetches[i].wait()
         target = gather.at[i]
         for k in range(lanes):
             if i < 2:
-                take(pair, (i * lanes + k) * tall, target, k * cap, cap, nodes)
+                take(fetched.at[i], k * tall, target, k * cap, cap, nodes)
                 continue
             at = pl.multiple_of((lane ^ k) * cap, cap)
             if i == 3 and k % 2 == 1:
@@ -439,7 +447,7 @@
         scratch_shapes=[pltpu.VMEM((small_rows, nodes), f32)]
         + [pltpu.VMEM(x.shape, x.dtype) for x in inputs[1:]]
         + [pltpu.VMEM((rows, deep), f32), pltpu.VMEM((8, columns), f32),
-           pltpu.VMEM((32, rows), f32), pltpu.SemaphoreType.DMA((3 + stiffness.shape[0],))],
+           pltpu.VMEM((32, rows), f32), pltpu.SemaphoreType.DMA((4,))],
         compiler_params=params(46),
     )(*inputs)
 
@@ -531,10 +539,11 @@
     new_history = pl.pallas_call(
         functools.partial(land_kernel, devices, per_peer),
         out_shape=jax.ShapeDtypeStruct((nodes, devices * per_peer), f32),
-        in_specs=[vmem] * (1 + 2 * half),
+        in_specs=[pl.BlockSpec(memory_space=pltpu.HBM)] + [vmem] * (2 * half),
         out_specs=pl.BlockSpec(memory_space=pl.ANY),
         scratch_shapes=[pltpu.VMEM((8, nodes, LANES), f32), pltpu.SemaphoreType.DMA((8,)),
-                        pltpu.VMEM((4, group, deep), f32)],
+                        pltpu.VMEM((4, group, deep), f32),
+                        pltpu.VMEM((2, lanes * tall, LANES), f32), pltpu.SemaphoreType.DMA((2,))],
         compiler_params=params(),
     )(pair, *joined, *direct)
     return (new_history, stress_out)

time: 95.4 us -> 94.5 us (level)
  no operation moved by 1% of the time
where the time goes in v4:
time: 94.5 us; the launch traced here: 94.2 us
  Pallas kernels  45.5 us (48%)
  waiting for transfers between devices  27.5 us (29%)
  starting transfers between devices  20.3 us (21%)
    pallas_call x4, Pallas kernels, shards(): pl.pallas_call(functools.partial(solve_kernel, 1.0 / math.sqrt(comps * no...  31.5 us
    ppermute x10, waiting for transfers between devices, hop(): return lax.ppermute(sent, axes, [(s, s ^ mask) for s in range(devices)])  27.5 us
    ppermute x10, starting transfers between devices, hop(): return lax.ppermute(sent, axes, [(s, s ^ mask) for s in range(devices)])  14.5 us
    all_to_all x1, starting transfers between devices, shards(): lax.all_to_all(pair.reshape(2 * lanes, tall, LANES), axes, split_axis=0,...  5.78 us
    pallas_call x1, Pallas kernels, shards(): pl.pallas_call(functools.partial(prep_kernel, devices, per_peer, comps, v...  4.68 us
    pallas_call x1, Pallas kernels, shards(): pl.pallas_call(functools.partial(land_kernel, devices, per_peer), out_sha...  3.53 us
    pallas_call x1, Pallas kernels, shards(): pl.pallas_call(functools.partial(ship_kernel, devices, per_peer, nodes, 2...  3.02 us
  transfers between devices with their start and end apart: 11, of which 6 were waited for; matrix products, arithmetic and copies ran while one was open for 0% of the time, Pallas kernels for 29%

profile of v4, /device:TPU:0, one launch (start us, length us, event | category | flops | bytes accessed | tf_op | source)
XLA Modules:
  0.0 94.2 jit_solution(6216100779756308959)
XLA Ops:
  0.6 1.7 %shard_map.104.refs_0_ = f32[8192,729]{1,0:T(8,128)} custom-call(f32[3,6,729]{2,1,0:T(8,128)} %coupling.1, f32[3,729]{1,0:T(4,128)} %plastic.1, f32[6,512]{1,0:T(8,128)} %strain.1, s32[1,512]{1,0:T(1,128)} %bitcast.3, s32[1,512]{1,0:T(1,128)} %qp.1, s32[9,9]{1,0:T(8,128)} %pattern.1), custom_call_target="tpu_custom_call" | custom-call | tf_op jit(solution)/shard_map/pallas_call | solution.py:422
  2.4 4.7 %shard_map.105 = (bf16[736,768]{1,0:T(8,128)(2,1)S(1)}, bf16[736,768]{1,0:T(8,128)(2,1)S(1)}, f32[736,512]{1,0:T(8,128)S(1)}, f32[736,512]{1,0:T(8,128)S(1)}, f3...) custom-call(f32[8192,729]{1,0:T(8,128)} %shard_map.104.refs_0_, ...), custom_call_target="tpu_custom_call" | custom-call | tf_op jit(solution)/shard_map/pallas_call | solution.py:431
  7.1 7.8 %shard_map.106 = (f32[736,128]{1,0:T(8,128)S(1)}, f32[8,128]{1,0:T(8,128)S(1)}, f32[736,128]{1,0:T(8,128)S(1)}) custom-call(bf16[736,768]{1,0:T(8,128)(2,1)S(1)} %get-tuple-element.48.khi, bf16[736,768]{1,0:T(8,128)(2,1)S(1)} %get-tuple-element.49.klo, f32[736,512]{1,0:T(8,128)S(1)} %get-tuple-element.50.hist, f32[736,512]{1,0:T(8,128)S(1)} %get-tuple-element.51.weight, ...), custom_call_target="tpu_custom_call" | custom-call | flops 3906994176 | bytes 1048576 | tf_op jit(solution)/shard_map/pallas_call | solution.py:466
  14.8 4.1 %collective-permute-start = (f32[736,128]{1,0:T(8,128)S(1)}, f32[736,128]{1,0:T(8,128)S(1)}, u32[]{:S(2)}, u32[]{:S(2)}) collective-permute-start(f32[736,128]{1,0:T(8,128)S(1)} %get-tuple-element.69), channel_id=1, source_target_pairs={{0,16},{1,17},{2,18},{3,19},{4,20},{5,21},{6,22},{7,23},{8,24},{9,... | collective-permute-start | bytes 1130504 | tf_op jit(solution)/shard_map/ppermute | solution.py:507
  19.0 7.8 %shard_map.107 = (f32[736,128]{1,0:T(8,128)S(1)}, f32[8,128]{1,0:T(8,128)S(1)}, f32[736,128]{1,0:T(8,128)S(1)}) custom-call(bf16[736,768]{1,0:T(8,128)(2,1)S(1)} %get-tuple-element.48.khi, bf16[736,768]{1,0:T(8,128)(2,1)S(1)} %get-tuple-element.49.klo, f32[736,512]{1,0:T(8,128)S(1)} %get-tuple-element.50.hist, f32[736,512]{1,0:T(8,128)S(1)} %get-tuple-element.51.weight, ...), custom_call_target="tpu_custom_call" | custom-call | flops 3906994176 | bytes 1048576 | tf_op jit(solution)/shard_map/pallas_call | solution.py:466
  26.8 1.6 %collective-permute-start.1 = (f32[736,128]{1,0:T(8,128)S(1)}, f32[736,128]{1,0:T(8,128)S(1)}, u32[]{:S(2)}, u32[]{:S(2)}) collective-permute-start(f32[736,128]{1,0:T(8,128)S(1)} %get-tuple-element.70), channel_id=1, source_target_pairs={{0,8},{1,9},{2,10},{3,11},{4,12},{5,13},{6,14},{7,15},{8,0},{9,1},... | collective-permute-start | bytes 1130504 | tf_op jit(solution)/shard_map/ppermute | solution.py:507
  28.4 8.1 %shard_map.108 = (f32[736,128]{1,0:T(8,128)S(1)}, f32[8,128]{1,0:T(8,128)S(1)}, f32[736,128]{1,0:T(8,128)S(1)}) custom-call(bf16[736,768]{1,0:T(8,128)(2,1)S(1)} %get-tuple-element.48.khi, bf16[736,768]{1,0:T(8,128)(2,1)S(1)} %get-tuple-element.49.klo, f32[736,512]{1,0:T(8,128)S(1)} %get-tuple-element.50.hist, f32[736,512]{1,0:T(8,128)S(1)} %get-tuple-element.51.weight, ...), custom_call_target="tpu_custom_call" | custom-call | flops 3906994176 | bytes 1048576 | tf_op jit(solution)/shard_map/pallas_call | solution.py:466
  36.6 7.9 %shard_map.109 = (f32[736,128]{1,0:T(8,128)S(1)}, f32[8,128]{1,0:T(8,128)S(1)}, f32[184,128]{1,0:T(8,128)S(1)}, f32[184,128]{1,0:T(8,128)S(1)}, f32[184,128]{1,0:T(8,128)S(1)}, /*index=5*/f32[184,128]{1,0:T(8,128)S(1)}) custom-call(bf16[736,768]{1,0:T(8,128)(2,1)S(1)} %get-tuple-element.48.khi, bf16[736,768]{1,0:T(8,128)(2,1)S(1)} %get-tuple-element.49.klo, ...), custom_call_target="tpu_custom_call" | custom-call | flops 3906994176 | bytes 1048576 | tf_op jit(solution)/shard_map/pallas_call | solution.py:466
  44.4 3.0 %shard_map.110 = f32[2944,128]{1,0:T(8,128)} custom-call(s32[8,512]{1,0:T(8,128)S(1)} %get-tuple-element.47.place, f32[736,128]{1,0:T(8,128)S(1)} %get-tuple-element.56.refs_0_, f32[736,128]{1,0:T(8,128)S(1)} %get-tuple-element.57.refs_1_, f32[736,128]{1,0:T(8,128)S(1)} %get-tuple-element.58.refs_2_, f32[736,128]{1,0:T(8,128)S(1)} %get-tuple-element.59.refs_3_), custom_call_target="tpu_custom_call" | custom-call | flops 771751936 | bytes 1048576 | tf_op jit(solution)/shard_map/pallas_call | solution.py:493
  47.5 5.8 %all-to-all-start = ((f32[16,184,128]{2,1,0:T(8,128)}), f32[16,184,128]{2,1,0:T(8,128)}, u32[]{:S(2)}, u32[]{:S(2)}) async-start(f32[16,184,128]{2,1,0:T(8,128)} %bitcast.1), calls=%async_computation | async-start | bytes 3014656 | tf_op jit(solution)/shard_map/all_to_all | solution.py:511
  53.3 2.6 %collective-permute-done.2.refs_2_ = f32[736,128]{1,0:T(8,128)S(1)} collective-permute-done((f32[736,128]{1,0:T(8,128)S(1)}, f32[736,128]{1,0:T(8,128)S(1)}, u32[]{:S(2)}, u32[]{:S(2)}) %collective-permute-start.2) | collective-permute-done | bytes 376864 | tf_op jit(solution)/shard_map/ppermute | solution.py:507
  56.0 1.6 %collective-permute-start.3 = (f32[552,128]{1,0:T(8,128)S(1)}, f32[552,128]{1,0:T(8,128)S(1)}, u32[]{:S(2)}, u32[]{:S(2)}) collective-permute-start(f32[552,128]{1,0:T(8,128)S(1)} %get-tuple-element.84), channel_id=1, source_target_pairs={{0,2},{1,3},{2,0},{3,1},{4,6},{5,7},{6,4},{7,5},{8,10},{9,11},{10,... | collective-permute-start | bytes 847880 | tf_op jit(solution)/shard_map/ppermute | solution.py:507
  57.6 1.5 %collective-permute-start.4 = (f32[552,128]{1,0:T(8,128)S(1)}, f32[552,128]{1,0:T(8,128)S(1)}, u32[]{:S(2)}, u32[]{:S(2)}) collective-permute-start(f32[552,128]{1,0:T(8,128)S(1)} %get-tuple-element.85), channel_id=1, source_target_pairs={{0,4},{1,5},{2,6},{3,7},{4,0},{5,1},{6,2},{7,3},{8,12},{9,13},{10,... | collective-permute-start | bytes 847880 | tf_op jit(solution)/shard_map/ppermute | solution.py:507
  59.1 0.5 collective-permute-start.5
  59.6 2.7 %collective-permute-start.7 = (f32[184,128]{1,0:T(8,128)S(1)}, f32[184,128]{1,0:T(8,128)S(1)}, u32[]{:S(2)}, u32[]{:S(2)}) collective-permute-start(f32[184,128]{1,0:T(8,128)S(1)} %get-tuple-element.88), channel_id=1, source_target_pairs={{0,11},{1,10},{2,9},{3,8},{4,15},{5,14},{6,13},{7,12},{8,3},{9,2},... | collective-permute-start | bytes 282632 | tf_op jit(solution)/shard_map/ppermute | solution.py:507
  62.2 14.3 %collective-permute-done.6.refs_4_ = f32[184,128]{1,0:T(8,128)S(1)} collective-permute-done((f32[184,128]{1,0:T(8,128)S(1)}, f32[184,128]{1,0:T(8,128)S(1)}, u32[]{:S(2)}, u32[]{:S(2)}) %collective-permute-start.6) | collective-permute-done | bytes 94240 | tf_op jit(solution)/shard_map/ppermute | solution.py:507
  76.5 1.2 %collective-permute-start.8 = (f32[184,128]{1,0:T(8,128)S(1)}, f32[184,128]{1,0:T(8,128)S(1)}, u32[]{:S(2)}, u32[]{:S(2)}) collective-permute-start(f32[184,128]{1,0:T(8,128)S(1)} %get-tuple-element.89), channel_id=1, source_target_pairs={{0,13},{1,12},{2,15},{3,14},{4,9},{5,8},{6,11},{7,10},{8,5},{9,4},... | collective-permute-start | bytes 282632 | tf_op jit(solution)/shard_map/ppermute | solution.py:507
  77.7 1.7 %collective-permute-done.7.refs_5_ = f32[184,128]{1,0:T(8,128)S(1)} collective-permute-done((f32[184,128]{1,0:T(8,128)S(1)}, f32[184,128]{1,0:T(8,128)S(1)}, u32[]{:S(2)}, u32[]{:S(2)}) %collective-permute-start.7) | collective-permute-done | bytes 94240 | tf_op jit(solution)/shard_map/ppermute | solution.py:507
  79.4 1.3 %collective-permute-start.9 = (f32[184,128]{1,0:T(8,128)S(1)}, f32[184,128]{1,0:T(8,128)S(1)}, u32[]{:S(2)}, u32[]{:S(2)}) collective-permute-start(f32[184,128]{1,0:T(8,128)S(1)} %get-tuple-element.90), channel_id=1, source_target_pairs={{0,15},{1,14},{2,13},{3,12},{4,11},{5,10},{6,9},{7,8},{8,7},{9,6},... | collective-permute-start | bytes 282632 | tf_op jit(solution)/shard_map/ppermute | solution.py:507
  80.7 0.9 shard_map.112
  81.6 1.1 %collective-permute-done.8.refs_6_ = f32[184,128]{1,0:T(8,128)S(1)} collective-permute-done((f32[184,128]{1,0:T(8,128)S(1)}, f32[184,128]{1,0:T(8,128)S(1)}, u32[]{:S(2)}, u32[]{:S(2)}) %collective-permute-start.8) | collective-permute-done | bytes 94240 | tf_op jit(solution)/shard_map/ppermute | solution.py:507
  82.7 3.5 %collective-permute-done.9.refs_7_ = f32[184,128]{1,0:T(8,128)S(1)} collective-permute-done((f32[184,128]{1,0:T(8,128)S(1)}, f32[184,128]{1,0:T(8,128)S(1)}, u32[]{:S(2)}, u32[]{:S(2)}) %collective-permute-start.9) | collective-permute-done | bytes 94240 | tf_op jit(solution)/shard_map/ppermute | solution.py:507
  86.3 4.2 %collective-permute-done.5.refs_3_ = f32[552,128]{1,0:T(8,128)S(1)} collective-permute-done((f32[552,128]{1,0:T(8,128)S(1)}, f32[552,128]{1,0:T(8,128)S(1)}, u32[]{:S(2)}, u32[]{:S(2)}) %collective-permute-start.5) | collective-permute-done | bytes 282656 | tf_op jit(solution)/shard_map/ppermute | solution.py:507
  90.5 3.5 %shard_map.113 = f32[729,1024]{1,0:T(8,128)} custom-call(f32[2944,128]{1,0:T(8,128)} %bitcast.2.pair, f32[552,128]{1,0:T(8,128)S(1)} %get-tuple-element.83.refs_0_, f32[552,128]{1,0:T(8,128)S(1)} %collective-permute-done.3.refs_1_, f32[552,128]{1,0:T(8,128)S(1)} %collective-permute-done.4.refs_2_, f32[552,128]{1,0:T(8,128)S(1)} %collective-permute-done.5.refs_3_, ...), custom_call_target="tpu_custom_call" | custom-call | tf_op jit(solution)/shard_map/pallas_call | solution.py:539
  (8 shorter events, 0.2 us)
Async XLA Ops:
  14.8 38.4 %collective-permute-start = (f32[736,128]{1,0:T(8,128)S(1)}, f32[736,128]{1,0:T(8,128)S(1)}, u32[]{:S(2)}, u32[]{:S(2)}) collective-permute-start(f32[736,128]{1,0:T(8,128)S(1)} %get-tuple-element.69), channel_id=1, source_target_pairs={{0,16},{1,17},{2,18},{3,19},{4,20},{5,21},{6,22},{7,23},{8,24},{9,... | collective-permute-start | bytes 1130504 | tf_op jit(solution)/shard_map/ppermute | solution.py:507
  26.8 26.5 %collective-permute-start.1 = (f32[736,128]{1,0:T(8,128)S(1)}, f32[736,128]{1,0:T(8,128)S(1)}, u32[]{:S(2)}, u32[]{:S(2)}) collective-permute-start(f32[736,128]{1,0:T(8,128)S(1)} %get-tuple-element.70), channel_id=1, source_target_pairs={{0,8},{1,9},{2,10},{3,11},{4,12},{5,13},{6,14},{7,15},{8,0},{9,1},... | collective-permute-start | bytes 1130504 | tf_op jit(solution)/shard_map/ppermute | solution.py:507
  36.5 19.4 %collective-permute-start.2 = (f32[736,128]{1,0:T(8,128)S(1)}, f32[736,128]{1,0:T(8,128)S(1)}, u32[]{:S(2)}, u32[]{:S(2)}) collective-permute-start(f32[736,128]{1,0:T(8,128)S(1)} %get-tuple-element.73), channel_id=1, source_target_pairs={{0,17},{1,16},{2,19},{3,18},{4,21},{5,20},{6,23},{7,22},{8,25},{9,... | collective-permute-start | bytes 1130504 | tf_op jit(solution)/shard_map/ppermute | solution.py:507
  47.5 43.0 %all-to-all-start = ((f32[16,184,128]{2,1,0:T(8,128)}), f32[16,184,128]{2,1,0:T(8,128)}, u32[]{:S(2)}, u32[]{:S(2)}) async-start(f32[16,184,128]{2,1,0:T(8,128)} %bitcast.1), calls=%async_computation | async-start | bytes 3014656 | tf_op jit(solution)/shard_map/all_to_all | solution.py:511
  56.0 30.3 %collective-permute-start.3 = (f32[552,128]{1,0:T(8,128)S(1)}, f32[552,128]{1,0:T(8,128)S(1)}, u32[]{:S(2)}, u32[]{:S(2)}) collective-permute-start(f32[552,128]{1,0:T(8,128)S(1)} %get-tuple-element.84), channel_id=1, source_target_pairs={{0,2},{1,3},{2,0},{3,1},{4,6},{5,7},{6,4},{7,5},{8,10},{9,11},{10,... | collective-permute-start | bytes 847880 | tf_op jit(solution)/shard_map/ppermute | solution.py:507
  57.6 28.7 %collective-permute-start.4 = (f32[552,128]{1,0:T(8,128)S(1)}, f32[552,128]{1,0:T(8,128)S(1)}, u32[]{:S(2)}, u32[]{:S(2)}) collective-permute-start(f32[552,128]{1,0:T(8,128)S(1)} %get-tuple-element.85), channel_id=1, source_target_pairs={{0,4},{1,5},{2,6},{3,7},{4,0},{5,1},{6,2},{7,3},{8,12},{9,13},{10,... | collective-permute-start | bytes 847880 | tf_op jit(solution)/shard_map/ppermute | solution.py:507
  59.1 31.4 %collective-permute-start.5 = (f32[552,128]{1,0:T(8,128)S(1)}, f32[552,128]{1,0:T(8,128)S(1)}, u32[]{:S(2)}, u32[]{:S(2)}) collective-permute-start(f32[552,128]{1,0:T(8,128)S(1)} %get-tuple-element.86), channel_id=1, source_target_pairs={{0,6},{1,7},{2,4},{3,5},{4,2},{5,3},{6,0},{7,1},{8,14},{9,15},{10,... | collective-permute-start | bytes 847880 | tf_op jit(solution)/shard_map/ppermute | solution.py:507
  59.6 16.9 %collective-permute-start.6 = (f32[184,128]{1,0:T(8,128)S(1)}, f32[184,128]{1,0:T(8,128)S(1)}, u32[]{:S(2)}, u32[]{:S(2)}) collective-permute-start(f32[184,128]{1,0:T(8,128)S(1)} %get-tuple-element.87), channel_id=1, source_target_pairs={{0,9},{1,8},{2,11},{3,10},{4,13},{5,12},{6,15},{7,14},{8,1},{9,0},... | collective-permute-start | bytes 282632 | tf_op jit(solution)/shard_map/ppermute | solution.py:507
  59.6 19.9 %collective-permute-start.7 = (f32[184,128]{1,0:T(8,128)S(1)}, f32[184,128]{1,0:T(8,128)S(1)}, u32[]{:S(2)}, u32[]{:S(2)}) collective-permute-start(f32[184,128]{1,0:T(8,128)S(1)} %get-tuple-element.88), channel_id=1, source_target_pairs={{0,11},{1,10},{2,9},{3,8},{4,15},{5,14},{6,13},{7,12},{8,3},{9,2},... | collective-permute-start | bytes 282632 | tf_op jit(solution)/shard_map/ppermute | solution.py:507
  76.5 6.2 %collective-permute-start.8 = (f32[184,128]{1,0:T(8,128)S(1)}, f32[184,128]{1,0:T(8,128)S(1)}, u32[]{:S(2)}, u32[]{:S(2)}) collective-permute-start(f32[184,128]{1,0:T(8,128)S(1)} %get-tuple-element.89), channel_id=1, source_target_pairs={{0,13},{1,12},{2,15},{3,14},{4,9},{5,8},{6,11},{7,10},{8,5},{9,4},... | collective-permute-start | bytes 282632 | tf_op jit(solution)/shard_map/ppermute | solution.py:507
  79.4 6.8 %collective-permute-start.9 = (f32[184,128]{1,0:T(8,128)S(1)}, f32[184,128]{1,0:T(8,128)S(1)}, u32[]{:S(2)}, u32[]{:S(2)}) collective-permute-start(f32[184,128]{1,0:T(8,128)S(1)} %get-tuple-element.90), channel_id=1, source_target_pairs={{0,15},{1,14},{2,13},{3,12},{4,11},{5,10},{6,9},{7,8},{8,7},{9,6},... | collective-permute-start | bytes 282632 | tf_op jit(solution)/shard_map/ppermute | solution.py:507

commit v5 on v4

--- a/solution.py
+++ b/solution.py
@@ -366,35 +366,36 @@
     return copy
 
 
-def land_kernel(devices, cap, pair, *refs):
-    blocks, (out, stage, sem, gather, fetched, arrival) = refs[:-6], refs[-6:]
+def land_pair(devices, cap, pair, out, stage, sem, gather):
     me, plane, lane, lanes = whereabouts(devices)
     nodes, tall = out.shape[0], height(cap, out.shape[0])
-    tiles, span = lanes * cap // LANES, lanes * tall
-    fetches = [
-        pltpu.make_async_copy(pair.at[pl.ds(i * span, span), :], fetched.at[i], arrival.at[i])
-        for i in range(2)
-    ]
-    for fetch in fetches:
-        fetch.start()
+    tiles = lanes * cap // LANES
     copies = []
-    for i in (2, 3, 0, 1):
-        if i < 2:
-            fetches[i].wait()
-        target = gather.at[i]
+    for i in range(2):
         for k in range(lanes):
-            if i < 2:
-                take(fetched.at[i], k * tall, target, k * cap, cap, nodes)
-                continue
+            take(pair, (i * lanes + k) * tall, gather.at[i], k * cap, cap, nodes)
+        source = jnp.where(plane // 2 == i, plane, plane ^ 3)
+        for part in range(tiles):
+            tile = gather[i, part * LANES:(part + 1) * LANES, :]
+            copies.append(land(tile, out, stage, sem, i * tiles + part, source * tiles + part))
+    for copy in copies:
+        copy.wait()
+
+
+def land_hops(devices, cap, *refs):
+    blocks, (out, stage, sem, gather) = refs[:-5], refs[-4:]
+    me, plane, lane, lanes = whereabouts(devices)
+    nodes, tall = out.shape[0], height(cap, out.shape[0])
+    tiles = lanes * cap // LANES
+    copies = []
+    for i in range(2):
+        for k in range(lanes):
             at = pl.multiple_of((lane ^ k) * cap, cap)
-            if i == 3 and k % 2 == 1:
-                take(blocks[lanes // 2 + k // 2], 0, target, at, cap, nodes)
+            if i == 1 and k % 2 == 1:
+                take(blocks[lanes // 2 + k // 2], 0, gather.at[i], at, cap, nodes)
             else:
-                take(blocks[k // 2], (2 * (k % 2) + i - 2) * tall, target, at, cap, nodes)
-        if i < 2:
-            source = jnp.where(plane // 2 == i, plane, plane ^ 3)
-        else:
-            source = plane ^ (4 - i)
+                take(blocks[k // 2], (2 * (k % 2) + i) * tall, gather.at[i], at, cap, nodes)
+        source = plane ^ (2 - i)
         for part in range(tiles):
             tile = gather[i, part * LANES:(part + 1) * LANES, :]
             copies.append(land(tile, out, stage, sem, i * tiles + part, source * tiles + part))
@@ -536,16 +537,27 @@
         compiler_params=params(),
     )(qp_s, *stress_s)
     joined[0], stress_out = lax.optimization_barrier((joined[0], stress_out))
+    hbm = pl.BlockSpec(memory_space=pl.ANY)
+    history_shape = jax.ShapeDtypeStruct((nodes, devices * per_peer), f32)
+    staging = [pltpu.VMEM((4, nodes, LANES), f32), pltpu.SemaphoreType.DMA((4,)),
+               pltpu.VMEM((2, group, deep), f32)]
     new_history = pl.pallas_call(
-        functools.partial(land_kernel, devices, per_peer),
-        out_shape=jax.ShapeDtypeStruct((nodes, devices * per_peer), f32),
-        in_specs=[pl.BlockSpec(memory_space=pltpu.HBM)] + [vmem] * (2 * half),
-        out_specs=pl.BlockSpec(memory_space=pl.ANY),
-        scratch_shapes=[pltpu.VMEM((8, nodes, LANES), f32), pltpu.SemaphoreType.DMA((8,)),
-                        pltpu.VMEM((4, group, deep), f32),
-                        pltpu.VMEM((2, lanes * tall, LANES), f32), pltpu.SemaphoreType.DMA((2,))],
+        functools.partial(land_pair, devices, per_peer),
+        out_shape=history_shape,
+        in_specs=[vmem],
+        out_specs=hbm,
+        scratch_shapes=staging,
         compiler_params=params(),
-    )(pair, *joined, *direct)
+    )(pair)
+    new_history = pl.pallas_call(
+        functools.partial(land_hops, devices, per_peer),
+        out_shape=history_shape,
+        in_specs=[vmem] * (2 * half) + [hbm],
+        out_specs=hbm,
+        scratch_shapes=staging,
+        input_output_aliases={2 * half: 0},
+        compiler_params=params(),
+    )(*joined, *direct, new_history)
     return (new_history, stress_out)
 
 

time: 94.5 us -> 94.5 us (level)
  the two profiles are of different devices: /device:TPU:0 before, /device:TPU:8 now
where the time goes in v5:
time: 94.5 us; the launch traced here: 94.3 us
  Pallas kernels  46.3 us (49%)
  waiting for transfers between devices  24.3 us (26%)
  starting transfers between devices  22.8 us (24%)
  between operations  0.95 us (1%)
    pallas_call x4, Pallas kernels, shards(): pl.pallas_call(functools.partial(solve_kernel, 1.0 / math.sqrt(comps * no...  31.6 us
    ppermute x10, starting transfers between devices, hop(): return lax.ppermute(sent, axes, [(s, s ^ mask) for s in range(devices)])  16.8 us
    ppermute x10, waiting for transfers between devices, hop(): return lax.ppermute(sent, axes, [(s, s ^ mask) for s in range(devices)])  14.6 us
    all_to_all x1, waiting for transfers between devices, shards(): lax.all_to_all(pair.reshape(2 * lanes, tall, LANES), axes, split_axis=0,...  9.65 us
    all_to_all x1, starting transfers between devices, shards(): lax.all_to_all(pair.reshape(2 * lanes, tall, LANES), axes, split_axis=0,...  6.02 us
    pallas_call x1, Pallas kernels, shards(): pl.pallas_call(functools.partial(prep_kernel, devices, per_peer, comps, v...  4.68 us
    pallas_call x1, Pallas kernels, shards(): pl.pallas_call(functools.partial(ship_kernel, devices, per_peer, nodes, 2...  3.02 us
    pallas_call x1, Pallas kernels, shards(): pl.pallas_call(functools.partial(land_pair, devices, per_peer), out_shape...  2.8 us
  transfers between devices with their start and end apart: 11, of which 2 were waited for; matrix products, arithmetic and copies ran while one was open for 0% of the time, Pallas kernels for 32%

profile of v5, /device:TPU:8, one launch (start us, length us, event | category | flops | bytes accessed | tf_op | source)
XLA Modules:
  0.0 94.3 jit_solution(14706447021161401165)
XLA Ops:
  0.6 1.7 %shard_map.104.refs_0_ = f32[8192,729]{1,0:T(8,128)} custom-call(f32[3,6,729]{2,1,0:T(8,128)} %coupling.1, f32[3,729]{1,0:T(4,128)} %plastic.1, f32[6,512]{1,0:T(8,128)} %strain.1, s32[1,512]{1,0:T(1,128)} %bitcast.3, s32[1,512]{1,0:T(1,128)} %qp.1, s32[9,9]{1,0:T(8,128)} %pattern.1), custom_call_target="tpu_custom_call" | custom-call | tf_op jit(solution)/shard_map/pallas_call | solution.py:423
  2.4 4.7 %shard_map.105 = (bf16[736,768]{1,0:T(8,128)(2,1)S(1)}, bf16[736,768]{1,0:T(8,128)(2,1)S(1)}, f32[736,512]{1,0:T(8,128)S(1)}, f32[736,512]{1,0:T(8,128)S(1)}, f3...) custom-call(f32[8192,729]{1,0:T(8,128)} %shard_map.104.refs_0_, ...), custom_call_target="tpu_custom_call" | custom-call | tf_op jit(solution)/shard_map/pallas_call | solution.py:432
  7.1 7.8 %shard_map.106 = (f32[736,128]{1,0:T(8,128)S(1)}, f32[8,128]{1,0:T(8,128)S(1)}, f32[736,128]{1,0:T(8,128)S(1)}) custom-call(bf16[736,768]{1,0:T(8,128)(2,1)S(1)} %get-tuple-element.47.khi, bf16[736,768]{1,0:T(8,128)(2,1)S(1)} %get-tuple-element.48.klo, f32[736,512]{1,0:T(8,128)S(1)} %get-tuple-element.49.hist, f32[736,512]{1,0:T(8,128)S(1)} %get-tuple-element.50.weight, ...), custom_call_target="tpu_custom_call" | custom-call | flops 3906994176 | bytes 1048576 | tf_op jit(solution)/shard_map/pallas_call | solution.py:467
  14.8 2.7 %collective-permute-start = (f32[736,128]{1,0:T(8,128)S(1)}, f32[736,128]{1,0:T(8,128)S(1)}, u32[]{:S(2)}, u32[]{:S(2)}) collective-permute-start(f32[736,128]{1,0:T(8,128)S(1)} %get-tuple-element.63), channel_id=1, source_target_pairs={{0,16},{1,17},{2,18},{3,19},{4,20},{5,21},{6,22},{7,23},{8,24},{9,... | collective-permute-start | bytes 1130504 | tf_op jit(solution)/shard_map/ppermute | solution.py:508
  17.5 7.8 %shard_map.107 = (f32[736,128]{1,0:T(8,128)S(1)}, f32[8,128]{1,0:T(8,128)S(1)}, f32[736,128]{1,0:T(8,128)S(1)}) custom-call(bf16[736,768]{1,0:T(8,128)(2,1)S(1)} %get-tuple-element.47.khi, bf16[736,768]{1,0:T(8,128)(2,1)S(1)} %get-tuple-element.48.klo, f32[736,512]{1,0:T(8,128)S(1)} %get-tuple-element.49.hist, f32[736,512]{1,0:T(8,128)S(1)} %get-tuple-element.50.weight, ...), custom_call_target="tpu_custom_call" | custom-call | flops 3906994176 | bytes 1048576 | tf_op jit(solution)/shard_map/pallas_call | solution.py:467
  25.3 0.5 collective-permute-start.1
  25.8 8.1 %shard_map.108 = (f32[736,128]{1,0:T(8,128)S(1)}, f32[8,128]{1,0:T(8,128)S(1)}, f32[736,128]{1,0:T(8,128)S(1)}) custom-call(bf16[736,768]{1,0:T(8,128)(2,1)S(1)} %get-tuple-element.47.khi, bf16[736,768]{1,0:T(8,128)(2,1)S(1)} %get-tuple-element.48.klo, f32[736,512]{1,0:T(8,128)S(1)} %get-tuple-element.49.hist, f32[736,512]{1,0:T(8,128)S(1)} %get-tuple-element.50.weight, ...), custom_call_target="tpu_custom_call" | custom-call | flops 3906994176 | bytes 1048576 | tf_op jit(solution)/shard_map/pallas_call | solution.py:467
  33.9 0.1 collective-permute-start.2
  34.0 7.9 %shard_map.109 = (f32[736,128]{1,0:T(8,128)S(1)}, f32[8,128]{1,0:T(8,128)S(1)}, f32[184,128]{1,0:T(8,128)S(1)}, f32[184,128]{1,0:T(8,128)S(1)}, f32[184,128]{1,0:T(8,128)S(1)}, /*index=5*/f32[184,128]{1,0:T(8,128)S(1)}) custom-call(bf16[736,768]{1,0:T(8,128)(2,1)S(1)} %get-tuple-element.47.khi, bf16[736,768]{1,0:T(8,128)(2,1)S(1)} %get-tuple-element.48.klo, ...), custom_call_target="tpu_custom_call" | custom-call | flops 3906994176 | bytes 1048576 | tf_op jit(solution)/shard_map/pallas_call | solution.py:467
  41.9 3.0 %shard_map.112 = f32[2944,128]{1,0:T(8,128)} custom-call(s32[8,512]{1,0:T(8,128)S(1)} %get-tuple-element.55.place, f32[736,128]{1,0:T(8,128)S(1)} %get-tuple-element.57.refs_0_, f32[736,128]{1,0:T(8,128)S(1)} %get-tuple-element.59.refs_1_, f32[736,128]{1,0:T(8,128)S(1)} %get-tuple-element.61.refs_2_, f32[736,128]{1,0:T(8,128)S(1)} %get-tuple-element.81.refs_3_), custom_call_target="tpu_custom_call" | custom-call | flops 771751936 | bytes 1048576 | tf_op jit(solution)/shard_map/pallas_call | solution.py:494
  44.9 6.0 %all-to-all-start = ((f32[16,184,128]{2,1,0:T(8,128)}), f32[16,184,128]{2,1,0:T(8,128)}, u32[]{:S(2)}, u32[]{:S(2)}) async-start(f32[16,184,128]{2,1,0:T(8,128)} %bitcast.1), calls=%async_computation | async-start | bytes 3014656 | tf_op jit(solution)/shard_map/all_to_all | solution.py:512
  51.0 0.1 shard_map.110
  51.0 1.9 %collective-permute-start.3 = (f32[552,128]{1,0:T(8,128)S(1)}, f32[552,128]{1,0:T(8,128)S(1)}, u32[]{:S(2)}, u32[]{:S(2)}) collective-permute-start(f32[552,128]{1,0:T(8,128)S(1)} %get-tuple-element.78), channel_id=1, source_target_pairs={{0,2},{1,3},{2,0},{3,1},{4,6},{5,7},{6,4},{7,5},{8,10},{9,11},{10,... | collective-permute-start | bytes 847880 | tf_op jit(solution)/shard_map/ppermute | solution.py:508
  53.0 1.5 %collective-permute-start.4 = (f32[552,128]{1,0:T(8,128)S(1)}, f32[552,128]{1,0:T(8,128)S(1)}, u32[]{:S(2)}, u32[]{:S(2)}) collective-permute-start(f32[552,128]{1,0:T(8,128)S(1)} %get-tuple-element.79), channel_id=1, source_target_pairs={{0,4},{1,5},{2,6},{3,7},{4,0},{5,1},{6,2},{7,3},{8,12},{9,13},{10,... | collective-permute-start | bytes 847880 | tf_op jit(solution)/shard_map/ppermute | solution.py:508
  54.4 0.2 collective-permute-start.5
  54.6 2.8 %collective-permute-start.6 = (f32[184,128]{1,0:T(8,128)S(1)}, f32[184,128]{1,0:T(8,128)S(1)}, u32[]{:S(2)}, u32[]{:S(2)}) collective-permute-start(f32[184,128]{1,0:T(8,128)S(1)} %get-tuple-element.86), channel_id=1, source_target_pairs={{0,9},{1,8},{2,11},{3,10},{4,13},{5,12},{6,15},{7,14},{8,1},{9,0},... | collective-permute-start | bytes 282632 | tf_op jit(solution)/shard_map/ppermute | solution.py:508
  57.4 0.9 %collective-permute-start.7 = (f32[184,128]{1,0:T(8,128)S(1)}, f32[184,128]{1,0:T(8,128)S(1)}, u32[]{:S(2)}, u32[]{:S(2)}) collective-permute-start(f32[184,128]{1,0:T(8,128)S(1)} %get-tuple-element.87), channel_id=1, source_target_pairs={{0,11},{1,10},{2,9},{3,8},{4,15},{5,14},{6,13},{7,12},{8,3},{9,2},... | collective-permute-start | bytes 282632 | tf_op jit(solution)/shard_map/ppermute | solution.py:508
  58.3 14.6 %collective-permute-done.6.refs_4_ = f32[184,128]{1,0:T(8,128)S(1)} collective-permute-done((f32[184,128]{1,0:T(8,128)S(1)}, f32[184,128]{1,0:T(8,128)S(1)}, u32[]{:S(2)}, u32[]{:S(2)}) %collective-permute-start.6) | collective-permute-done | bytes 94240 | tf_op jit(solution)/shard_map/ppermute | solution.py:508
  72.9 3.3 %collective-permute-start.8 = (f32[184,128]{1,0:T(8,128)S(1)}, f32[184,128]{1,0:T(8,128)S(1)}, u32[]{:S(2)}, u32[]{:S(2)}) collective-permute-start(f32[184,128]{1,0:T(8,128)S(1)} %get-tuple-element.88), channel_id=1, source_target_pairs={{0,13},{1,12},{2,15},{3,14},{4,9},{5,8},{6,11},{7,10},{8,5},{9,4},... | collective-permute-start | bytes 282632 | tf_op jit(solution)/shard_map/ppermute | solution.py:508
  76.2 3.0 %collective-permute-start.9 = (f32[184,128]{1,0:T(8,128)S(1)}, f32[184,128]{1,0:T(8,128)S(1)}, u32[]{:S(2)}, u32[]{:S(2)}) collective-permute-start(f32[184,128]{1,0:T(8,128)S(1)} %get-tuple-element.89), channel_id=1, source_target_pairs={{0,15},{1,14},{2,13},{3,12},{4,11},{5,10},{6,9},{7,8},{8,7},{9,6},... | collective-permute-start | bytes 282632 | tf_op jit(solution)/shard_map/ppermute | solution.py:508
  79.2 0.9 shard_map.111
  80.1 9.7 %all-to-all-done = f32[16,184,128]{2,1,0:T(8,128)} async-done(((f32[16,184,128]{2,1,0:T(8,128)}), f32[16,184,128]{2,1,0:T(8,128)}, u32[]{:S(2)}, u32[]{:S(2)}) %all-to-all-start) | async-done | bytes 1507360 | tf_op jit(solution)/shard_map/all_to_all | solution.py:512
  89.7 2.8 %shard_map.113.refs_8_ = f32[729,1024]{1,0:T(8,128)} custom-call(f32[2944,128]{1,0:T(8,128)} %bitcast.2.pair), custom_call_target="tpu_custom_call" | custom-call | tf_op jit(solution)/shard_map/pallas_call | solution.py:544
  92.6 1.5 %shard_map.114 = f32[729,1024]{1,0:T(8,128)} custom-call(f32[552,128]{1,0:T(8,128)S(1)} %get-tuple-element.77.refs_0_, f32[552,128]{1,0:T(8,128)S(1)} %collective-permute-done.3.refs_1_, f32[552,128]{1,0:T(8,128)S(1)} %collective-permute-done.4.refs_2_, f32[552,128]{1,0:T(8,128)S(1)} %collective-permute-done.5.refs_3_, ...), custom_call_target="tpu_custom_call", output_to_operand_aliasing={{}: (8, {})} | custom-call | tf_op jit(solution)/shard_map/pallas_call | solution.py:552
  (9 shorter events, 0.0 us)
Async XLA Ops:
  14.8 36.1 %collective-permute-start = (f32[736,128]{1,0:T(8,128)S(1)}, f32[736,128]{1,0:T(8,128)S(1)}, u32[]{:S(2)}, u32[]{:S(2)}) collective-permute-start(f32[736,128]{1,0:T(8,128)S(1)} %get-tuple-element.63), channel_id=1, source_target_pairs={{0,16},{1,17},{2,18},{3,19},{4,20},{5,21},{6,22},{7,23},{8,24},{9,... | collective-permute-start | bytes 1130504 | tf_op jit(solution)/shard_map/ppermute | solution.py:508
  25.3 25.6 %collective-permute-start.1 = (f32[736,128]{1,0:T(8,128)S(1)}, f32[736,128]{1,0:T(8,128)S(1)}, u32[]{:S(2)}, u32[]{:S(2)}) collective-permute-start(f32[736,128]{1,0:T(8,128)S(1)} %get-tuple-element.64), channel_id=1, source_target_pairs={{0,8},{1,9},{2,10},{3,11},{4,12},{5,13},{6,14},{7,15},{8,0},{9,1},... | collective-permute-start | bytes 1130504 | tf_op jit(solution)/shard_map/ppermute | solution.py:508
  33.9 17.0 %collective-permute-start.2 = (f32[736,128]{1,0:T(8,128)S(1)}, f32[736,128]{1,0:T(8,128)S(1)}, u32[]{:S(2)}, u32[]{:S(2)}) collective-permute-start(f32[736,128]{1,0:T(8,128)S(1)} %get-tuple-element.67), channel_id=1, source_target_pairs={{0,17},{1,16},{2,19},{3,18},{4,21},{5,20},{6,23},{7,22},{8,25},{9,... | collective-permute-start | bytes 1130504 | tf_op jit(solution)/shard_map/ppermute | solution.py:508
  44.9 44.8 %all-to-all-start = ((f32[16,184,128]{2,1,0:T(8,128)}), f32[16,184,128]{2,1,0:T(8,128)}, u32[]{:S(2)}, u32[]{:S(2)}) async-start(f32[16,184,128]{2,1,0:T(8,128)} %bitcast.1), calls=%async_computation | async-start | bytes 3014656 | tf_op jit(solution)/shard_map/all_to_all | solution.py:512
  51.0 41.5 %collective-permute-start.3 = (f32[552,128]{1,0:T(8,128)S(1)}, f32[552,128]{1,0:T(8,128)S(1)}, u32[]{:S(2)}, u32[]{:S(2)}) collective-permute-start(f32[552,128]{1,0:T(8,128)S(1)} %get-tuple-element.78), channel_id=1, source_target_pairs={{0,2},{1,3},{2,0},{3,1},{4,6},{5,7},{6,4},{7,5},{8,10},{9,11},{10,... | collective-permute-start | bytes 847880 | tf_op jit(solution)/shard_map/ppermute | solution.py:508
  53.0 39.6 %collective-permute-start.4 = (f32[552,128]{1,0:T(8,128)S(1)}, f32[552,128]{1,0:T(8,128)S(1)}, u32[]{:S(2)}, u32[]{:S(2)}) collective-permute-start(f32[552,128]{1,0:T(8,128)S(1)} %get-tuple-element.79), channel_id=1, source_target_pairs={{0,4},{1,5},{2,6},{3,7},{4,0},{5,1},{6,2},{7,3},{8,12},{9,13},{10,... | collective-permute-start | bytes 847880 | tf_op jit(solution)/shard_map/ppermute | solution.py:508
  54.4 38.1 %collective-permute-start.5 = (f32[552,128]{1,0:T(8,128)S(1)}, f32[552,128]{1,0:T(8,128)S(1)}, u32[]{:S(2)}, u32[]{:S(2)}) collective-permute-start(f32[552,128]{1,0:T(8,128)S(1)} %get-tuple-element.80), channel_id=1, source_target_pairs={{0,6},{1,7},{2,4},{3,5},{4,2},{5,3},{6,0},{7,1},{8,14},{9,15},{10,... | collective-permute-start | bytes 847880 | tf_op jit(solution)/shard_map/ppermute | solution.py:508
  54.6 18.3 %collective-permute-start.6 = (f32[184,128]{1,0:T(8,128)S(1)}, f32[184,128]{1,0:T(8,128)S(1)}, u32[]{:S(2)}, u32[]{:S(2)}) collective-permute-start(f32[184,128]{1,0:T(8,128)S(1)} %get-tuple-element.86), channel_id=1, source_target_pairs={{0,9},{1,8},{2,11},{3,10},{4,13},{5,12},{6,15},{7,14},{8,1},{9,0},... | collective-permute-start | bytes 282632 | tf_op jit(solution)/shard_map/ppermute | solution.py:508
  57.4 18.8 %collective-permute-start.7 = (f32[184,128]{1,0:T(8,128)S(1)}, f32[184,128]{1,0:T(8,128)S(1)}, u32[]{:S(2)}, u32[]{:S(2)}) collective-permute-start(f32[184,128]{1,0:T(8,128)S(1)} %get-tuple-element.87), channel_id=1, source_target_pairs={{0,11},{1,10},{2,9},{3,8},{4,15},{5,14},{6,13},{7,12},{8,3},{9,2},... | collective-permute-start | bytes 282632 | tf_op jit(solution)/shard_map/ppermute | solution.py:508
  72.9 19.6 %collective-permute-start.8 = (f32[184,128]{1,0:T(8,128)S(1)}, f32[184,128]{1,0:T(8,128)S(1)}, u32[]{:S(2)}, u32[]{:S(2)}) collective-permute-start(f32[184,128]{1,0:T(8,128)S(1)} %get-tuple-element.88), channel_id=1, source_target_pairs={{0,13},{1,12},{2,15},{3,14},{4,9},{5,8},{6,11},{7,10},{8,5},{9,4},... | collective-permute-start | bytes 282632 | tf_op jit(solution)/shard_map/ppermute | solution.py:508
  76.2 16.3 %collective-permute-start.9 = (f32[184,128]{1,0:T(8,128)S(1)}, f32[184,128]{1,0:T(8,128)S(1)}, u32[]{:S(2)}, u32[]{:S(2)}) collective-permute-start(f32[184,128]{1,0:T(8,128)S(1)} %get-tuple-element.89), channel_id=1, source_target_pairs={{0,15},{1,14},{2,13},{3,12},{4,11},{5,10},{6,9},{7,8},{8,7},{9,6},... | collective-permute-start | bytes 282632 | tf_op jit(solution)/shard_map/ppermute | solution.py:508

commit v6 on v5

--- a/solution.py
+++ b/solution.py
@@ -366,7 +366,7 @@
     return copy
 
 
-def land_pair(devices, cap, pair, out, stage, sem, gather):
+def land_pair(devices, cap, pair, history, out, stage, sem, gather):
     me, plane, lane, lanes = whereabouts(devices)
     nodes, tall = out.shape[0], height(cap, out.shape[0])
     tiles = lanes * cap // LANES
@@ -383,7 +383,7 @@
 
 
 def land_hops(devices, cap, *refs):
-    blocks, (out, stage, sem, gather) = refs[:-5], refs[-4:]
+    blocks, (out, stage, sem, gather) = refs[:-4], refs[-4:]
     me, plane, lane, lanes = whereabouts(devices)
     nodes, tall = out.shape[0], height(cap, out.shape[0])
     tiles = lanes * cap // LANES
@@ -542,22 +542,22 @@
     staging = [pltpu.VMEM((4, nodes, LANES), f32), pltpu.SemaphoreType.DMA((4,)),
                pltpu.VMEM((2, group, deep), f32)]
     new_history = pl.pallas_call(
-        functools.partial(land_pair, devices, per_peer),
+        functools.partial(land_hops, devices, per_peer),
         out_shape=history_shape,
-        in_specs=[vmem],
+        in_specs=[vmem] * (2 * half),
         out_specs=hbm,
         scratch_shapes=staging,
         compiler_params=params(),
-    )(pair)
+    )(*joined, *direct)
     new_history = pl.pallas_call(
-        functools.partial(land_hops, devices, per_peer),
+        functools.partial(land_pair, devices, per_peer),
         out_shape=history_shape,
-        in_specs=[vmem] * (2 * half) + [hbm],
+        in_specs=[vmem, hbm],
         out_specs=hbm,
         scratch_shapes=staging,
-        input_output_aliases={2 * half: 0},
+        input_output_aliases={1: 0},
         compiler_params=params(),
-    )(*joined, *direct, new_history)
+    )(pair, new_history)
     return (new_history, stress_out)
 
 

time: 94.5 us -> 95.3 us (level)
  the two profiles are of different devices: /device:TPU:8 before, /device:TPU:0 now
where the time goes in v6:
time: 95.3 us; the launch traced here: 95 us
  Pallas kernels  46.3 us (49%)
  waiting for transfers between devices  27.5 us (29%)
  starting transfers between devices  20.3 us (21%)
    pallas_call x4, Pallas kernels, shards(): pl.pallas_call(functools.partial(solve_kernel, 1.0 / math.sqrt(comps * no...  31.5 us
    ppermute x10, waiting for transfers between devices, hop(): return lax.ppermute(sent, axes, [(s, s ^ mask) for s in range(devices)])  27.5 us
    ppermute x10, starting transfers between devices, hop(): return lax.ppermute(sent, axes, [(s, s ^ mask) for s in range(devices)])  14.5 us
    all_to_all x1, starting transfers between devices, shards(): lax.all_to_all(pair.reshape(2 * lanes, tall, LANES), axes, split_axis=0,...  5.78 us
    pallas_call x1, Pallas kernels, shards(): pl.pallas_call(functools.partial(prep_kernel, devices, per_peer, comps, v...  4.68 us
    pallas_call x1, Pallas kernels, shards(): pl.pallas_call(functools.partial(ship_kernel, devices, per_peer, nodes, 2...  3.02 us
    pallas_call x1, Pallas kernels, shards(): pl.pallas_call(functools.partial(land_pair, devices, per_peer), out_shape...  2.8 us
  transfers between devices with their start and end apart: 11, of which 6 were waited for; matrix products, arithmetic and copies ran while one was open for 0% of the time, Pallas kernels for 31%

profile of v6, /device:TPU:0, one launch (start us, length us, event | category | flops | bytes accessed | tf_op | source)
XLA Modules:
  0.0 95.0 jit_solution(9446387054788447861)
XLA Ops:
  0.6 1.7 %shard_map.104.refs_0_ = f32[8192,729]{1,0:T(8,128)} custom-call(f32[3,6,729]{2,1,0:T(8,128)} %coupling.1, f32[3,729]{1,0:T(4,128)} %plastic.1, f32[6,512]{1,0:T(8,128)} %strain.1, s32[1,512]{1,0:T(1,128)} %bitcast.3, s32[1,512]{1,0:T(1,128)} %qp.1, s32[9,9]{1,0:T(8,128)} %pattern.1), custom_call_target="tpu_custom_call" | custom-call | tf_op jit(solution)/shard_map/pallas_call | solution.py:423
  2.4 4.7 %shard_map.105 = (bf16[736,768]{1,0:T(8,128)(2,1)S(1)}, bf16[736,768]{1,0:T(8,128)(2,1)S(1)}, f32[736,512]{1,0:T(8,128)S(1)}, f32[736,512]{1,0:T(8,128)S(1)}, f3...) custom-call(f32[8192,729]{1,0:T(8,128)} %shard_map.104.refs_0_, ...), custom_call_target="tpu_custom_call" | custom-call | tf_op jit(solution)/shard_map/pallas_call | solution.py:432
  7.1 7.8 %shard_map.106 = (f32[736,128]{1,0:T(8,128)S(1)}, f32[8,128]{1,0:T(8,128)S(1)}, f32[736,128]{1,0:T(8,128)S(1)}) custom-call(bf16[736,768]{1,0:T(8,128)(2,1)S(1)} %get-tuple-element.48.khi, bf16[736,768]{1,0:T(8,128)(2,1)S(1)} %get-tuple-element.49.klo, f32[736,512]{1,0:T(8,128)S(1)} %get-tuple-element.50.hist, f32[736,512]{1,0:T(8,128)S(1)} %get-tuple-element.51.weight, ...), custom_call_target="tpu_custom_call" | custom-call | flops 3906994176 | bytes 1048576 | tf_op jit(solution)/shard_map/pallas_call | solution.py:467
  14.8 4.1 %collective-permute-start = (f32[736,128]{1,0:T(8,128)S(1)}, f32[736,128]{1,0:T(8,128)S(1)}, u32[]{:S(2)}, u32[]{:S(2)}) collective-permute-start(f32[736,128]{1,0:T(8,128)S(1)} %get-tuple-element.69), channel_id=1, source_target_pairs={{0,16},{1,17},{2,18},{3,19},{4,20},{5,21},{6,22},{7,23},{8,24},{9,... | collective-permute-start | bytes 1130504 | tf_op jit(solution)/shard_map/ppermute | solution.py:508
  19.0 7.8 %shard_map.107 = (f32[736,128]{1,0:T(8,128)S(1)}, f32[8,128]{1,0:T(8,128)S(1)}, f32[736,128]{1,0:T(8,128)S(1)}) custom-call(bf16[736,768]{1,0:T(8,128)(2,1)S(1)} %get-tuple-element.48.khi, bf16[736,768]{1,0:T(8,128)(2,1)S(1)} %get-tuple-element.49.klo, f32[736,512]{1,0:T(8,128)S(1)} %get-tuple-element.50.hist, f32[736,512]{1,0:T(8,128)S(1)} %get-tuple-element.51.weight, ...), custom_call_target="tpu_custom_call" | custom-call | flops 3906994176 | bytes 1048576 | tf_op jit(solution)/shard_map/pallas_call | solution.py:467
  26.8 1.6 %collective-permute-start.1 = (f32[736,128]{1,0:T(8,128)S(1)}, f32[736,128]{1,0:T(8,128)S(1)}, u32[]{:S(2)}, u32[]{:S(2)}) collective-permute-start(f32[736,128]{1,0:T(8,128)S(1)} %get-tuple-element.70), channel_id=1, source_target_pairs={{0,8},{1,9},{2,10},{3,11},{4,12},{5,13},{6,14},{7,15},{8,0},{9,1},... | collective-permute-start | bytes 1130504 | tf_op jit(solution)/shard_map/ppermute | solution.py:508
  28.4 8.1 %shard_map.108 = (f32[736,128]{1,0:T(8,128)S(1)}, f32[8,128]{1,0:T(8,128)S(1)}, f32[736,128]{1,0:T(8,128)S(1)}) custom-call(bf16[736,768]{1,0:T(8,128)(2,1)S(1)} %get-tuple-element.48.khi, bf16[736,768]{1,0:T(8,128)(2,1)S(1)} %get-tuple-element.49.klo, f32[736,512]{1,0:T(8,128)S(1)} %get-tuple-element.50.hist, f32[736,512]{1,0:T(8,128)S(1)} %get-tuple-element.51.weight, ...), custom_call_target="tpu_custom_call" | custom-call | flops 3906994176 | bytes 1048576 | tf_op jit(solution)/shard_map/pallas_call | solution.py:467
  36.6 7.9 %shard_map.109 = (f32[736,128]{1,0:T(8,128)S(1)}, f32[8,128]{1,0:T(8,128)S(1)}, f32[184,128]{1,0:T(8,128)S(1)}, f32[184,128]{1,0:T(8,128)S(1)}, f32[184,128]{1,0:T(8,128)S(1)}, /*index=5*/f32[184,128]{1,0:T(8,128)S(1)}) custom-call(bf16[736,768]{1,0:T(8,128)(2,1)S(1)} %get-tuple-element.48.khi, bf16[736,768]{1,0:T(8,128)(2,1)S(1)} %get-tuple-element.49.klo, ...), custom_call_target="tpu_custom_call" | custom-call | flops 3906994176 | bytes 1048576 | tf_op jit(solution)/shard_map/pallas_call | solution.py:467
  44.4 3.0 %shard_map.110 = f32[2944,128]{1,0:T(8,128)} custom-call(s32[8,512]{1,0:T(8,128)S(1)} %get-tuple-element.47.place, f32[736,128]{1,0:T(8,128)S(1)} %get-tuple-element.56.refs_0_, f32[736,128]{1,0:T(8,128)S(1)} %get-tuple-element.57.refs_1_, f32[736,128]{1,0:T(8,128)S(1)} %get-tuple-element.58.refs_2_, f32[736,128]{1,0:T(8,128)S(1)} %get-tuple-element.59.refs_3_), custom_call_target="tpu_custom_call" | custom-call | flops 771751936 | bytes 1048576 | tf_op jit(solution)/shard_map/pallas_call | solution.py:494
  47.5 5.8 %all-to-all-start = ((f32[16,184,128]{2,1,0:T(8,128)}), f32[16,184,128]{2,1,0:T(8,128)}, u32[]{:S(2)}, u32[]{:S(2)}) async-start(f32[16,184,128]{2,1,0:T(8,128)} %bitcast.1), calls=%async_computation | async-start | bytes 3014656 | tf_op jit(solution)/shard_map/all_to_all | solution.py:512
  53.3 2.6 %collective-permute-done.2.refs_2_ = f32[736,128]{1,0:T(8,128)S(1)} collective-permute-done((f32[736,128]{1,0:T(8,128)S(1)}, f32[736,128]{1,0:T(8,128)S(1)}, u32[]{:S(2)}, u32[]{:S(2)}) %collective-permute-start.2) | collective-permute-done | bytes 376864 | tf_op jit(solution)/shard_map/ppermute | solution.py:508
  56.0 1.6 %collective-permute-start.3 = (f32[552,128]{1,0:T(8,128)S(1)}, f32[552,128]{1,0:T(8,128)S(1)}, u32[]{:S(2)}, u32[]{:S(2)}) collective-permute-start(f32[552,128]{1,0:T(8,128)S(1)} %get-tuple-element.84), channel_id=1, source_target_pairs={{0,2},{1,3},{2,0},{3,1},{4,6},{5,7},{6,4},{7,5},{8,10},{9,11},{10,... | collective-permute-start | bytes 847880 | tf_op jit(solution)/shard_map/ppermute | solution.py:508
  57.6 1.5 %collective-permute-start.4 = (f32[552,128]{1,0:T(8,128)S(1)}, f32[552,128]{1,0:T(8,128)S(1)}, u32[]{:S(2)}, u32[]{:S(2)}) collective-permute-start(f32[552,128]{1,0:T(8,128)S(1)} %get-tuple-element.85), channel_id=1, source_target_pairs={{0,4},{1,5},{2,6},{3,7},{4,0},{5,1},{6,2},{7,3},{8,12},{9,13},{10,... | collective-permute-start | bytes 847880 | tf_op jit(solution)/shard_map/ppermute | solution.py:508
  59.6 2.7 %collective-permute-start.7 = (f32[184,128]{1,0:T(8,128)S(1)}, f32[184,128]{1,0:T(8,128)S(1)}, u32[]{:S(2)}, u32[]{:S(2)}) collective-permute-start(f32[184,128]{1,0:T(8,128)S(1)} %get-tuple-element.88), channel_id=1, source_target_pairs={{0,11},{1,10},{2,9},{3,8},{4,15},{5,14},{6,13},{7,12},{8,3},{9,2},... | collective-permute-start | bytes 282632 | tf_op jit(solution)/shard_map/ppermute | solution.py:508
  62.2 14.3 %collective-permute-done.6.refs_4_ = f32[184,128]{1,0:T(8,128)S(1)} collective-permute-done((f32[184,128]{1,0:T(8,128)S(1)}, f32[184,128]{1,0:T(8,128)S(1)}, u32[]{:S(2)}, u32[]{:S(2)}) %collective-permute-start.6) | collective-permute-done | bytes 94240 | tf_op jit(solution)/shard_map/ppermute | solution.py:508
  76.5 1.2 %collective-permute-start.8 = (f32[184,128]{1,0:T(8,128)S(1)}, f32[184,128]{1,0:T(8,128)S(1)}, u32[]{:S(2)}, u32[]{:S(2)}) collective-permute-start(f32[184,128]{1,0:T(8,128)S(1)} %get-tuple-element.89), channel_id=1, source_target_pairs={{0,13},{1,12},{2,15},{3,14},{4,9},{5,8},{6,11},{7,10},{8,5},{9,4},... | collective-permute-start | bytes 282632 | tf_op jit(solution)/shard_map/ppermute | solution.py:508
  77.7 1.7 %collective-permute-done.7.refs_5_ = f32[184,128]{1,0:T(8,128)S(1)} collective-permute-done((f32[184,128]{1,0:T(8,128)S(1)}, f32[184,128]{1,0:T(8,128)S(1)}, u32[]{:S(2)}, u32[]{:S(2)}) %collective-permute-start.7) | collective-permute-done | bytes 94240 | tf_op jit(solution)/shard_map/ppermute | solution.py:508
  79.4 1.3 %collective-permute-start.9 = (f32[184,128]{1,0:T(8,128)S(1)}, f32[184,128]{1,0:T(8,128)S(1)}, u32[]{:S(2)}, u32[]{:S(2)}) collective-permute-start(f32[184,128]{1,0:T(8,128)S(1)} %get-tuple-element.90), channel_id=1, source_target_pairs={{0,15},{1,14},{2,13},{3,12},{4,11},{5,10},{6,9},{7,8},{8,7},{9,6},... | collective-permute-start | bytes 282632 | tf_op jit(solution)/shard_map/ppermute | solution.py:508
  80.7 0.9 shard_map.112
  81.6 1.1 %collective-permute-done.8.refs_6_ = f32[184,128]{1,0:T(8,128)S(1)} collective-permute-done((f32[184,128]{1,0:T(8,128)S(1)}, f32[184,128]{1,0:T(8,128)S(1)}, u32[]{:S(2)}, u32[]{:S(2)}) %collective-permute-start.8) | collective-permute-done | bytes 94240 | tf_op jit(solution)/shard_map/ppermute | solution.py:508
  82.7 3.5 %collective-permute-done.9.refs_7_ = f32[184,128]{1,0:T(8,128)S(1)} collective-permute-done((f32[184,128]{1,0:T(8,128)S(1)}, f32[184,128]{1,0:T(8,128)S(1)}, u32[]{:S(2)}, u32[]{:S(2)}) %collective-permute-start.9) | collective-permute-done | bytes 94240 | tf_op jit(solution)/shard_map/ppermute | solution.py:508
  86.3 4.2 %collective-permute-done.5.refs_3_ = f32[552,128]{1,0:T(8,128)S(1)} collective-permute-done((f32[552,128]{1,0:T(8,128)S(1)}, f32[552,128]{1,0:T(8,128)S(1)}, u32[]{:S(2)}, u32[]{:S(2)}) %collective-permute-start.5) | collective-permute-done | bytes 282656 | tf_op jit(solution)/shard_map/ppermute | solution.py:508
  90.5 1.5 %shard_map.113.history = f32[729,1024]{1,0:T(8,128)} custom-call(f32[552,128]{1,0:T(8,128)S(1)} %get-tuple-element.83.refs_0_, f32[552,128]{1,0:T(8,128)S(1)} %collective-permute-done.3.refs_1_, f32[552,128]{1,0:T(8,128)S(1)} %collective-permute-done.4.refs_2_, f32[552,128]{1,0:T(8,128)S(1)} %collective-permute-done.5.refs_3_, ...), custom_call_target="tpu_custom_call" | custom-call | tf_op jit(solution)/shard_map/pallas_call | solution.py:544
  92.0 2.8 %shard_map.114 = f32[729,1024]{1,0:T(8,128)} custom-call(f32[2944,128]{1,0:T(8,128)} %bitcast.2.pair, f32[729,1024]{1,0:T(8,128)} %shard_map.113.history), custom_call_target="tpu_custom_call", output_to_operand_aliasing={{}: (1, {})} | custom-call | tf_op jit(solution)/shard_map/pallas_call | solution.py:552
  (9 shorter events, 0.6 us)
Async XLA Ops:
  14.8 38.4 %collective-permute-start = (f32[736,128]{1,0:T(8,128)S(1)}, f32[736,128]{1,0:T(8,128)S(1)}, u32[]{:S(2)}, u32[]{:S(2)}) collective-permute-start(f32[736,128]{1,0:T(8,128)S(1)} %get-tuple-element.69), channel_id=1, source_target_pairs={{0,16},{1,17},{2,18},{3,19},{4,20},{5,21},{6,22},{7,23},{8,24},{9,... | collective-permute-start | bytes 1130504 | tf_op jit(solution)/shard_map/ppermute | solution.py:508
  26.8 26.5 %collective-permute-start.1 = (f32[736,128]{1,0:T(8,128)S(1)}, f32[736,128]{1,0:T(8,128)S(1)}, u32[]{:S(2)}, u32[]{:S(2)}) collective-permute-start(f32[736,128]{1,0:T(8,128)S(1)} %get-tuple-element.70), channel_id=1, source_target_pairs={{0,8},{1,9},{2,10},{3,11},{4,12},{5,13},{6,14},{7,15},{8,0},{9,1},... | collective-permute-start | bytes 1130504 | tf_op jit(solution)/shard_map/ppermute | solution.py:508
  36.5 19.4 %collective-permute-start.2 = (f32[736,128]{1,0:T(8,128)S(1)}, f32[736,128]{1,0:T(8,128)S(1)}, u32[]{:S(2)}, u32[]{:S(2)}) collective-permute-start(f32[736,128]{1,0:T(8,128)S(1)} %get-tuple-element.73), channel_id=1, source_target_pairs={{0,17},{1,16},{2,19},{3,18},{4,21},{5,20},{6,23},{7,22},{8,25},{9,... | collective-permute-start | bytes 1130504 | tf_op jit(solution)/shard_map/ppermute | solution.py:508
  47.5 44.5 %all-to-all-start = ((f32[16,184,128]{2,1,0:T(8,128)}), f32[16,184,128]{2,1,0:T(8,128)}, u32[]{:S(2)}, u32[]{:S(2)}) async-start(f32[16,184,128]{2,1,0:T(8,128)} %bitcast.1), calls=%async_computation | async-start | bytes 3014656 | tf_op jit(solution)/shard_map/all_to_all | solution.py:512
  56.0 30.3 %collective-permute-start.3 = (f32[552,128]{1,0:T(8,128)S(1)}, f32[552,128]{1,0:T(8,128)S(1)}, u32[]{:S(2)}, u32[]{:S(2)}) collective-permute-start(f32[552,128]{1,0:T(8,128)S(1)} %get-tuple-element.84), channel_id=1, source_target_pairs={{0,2},{1,3},{2,0},{3,1},{4,6},{5,7},{6,4},{7,5},{8,10},{9,11},{10,... | collective-permute-start | bytes 847880 | tf_op jit(solution)/shard_map/ppermute | solution.py:508
  57.6 28.7 %collective-permute-start.4 = (f32[552,128]{1,0:T(8,128)S(1)}, f32[552,128]{1,0:T(8,128)S(1)}, u32[]{:S(2)}, u32[]{:S(2)}) collective-permute-start(f32[552,128]{1,0:T(8,128)S(1)} %get-tuple-element.85), channel_id=1, source_target_pairs={{0,4},{1,5},{2,6},{3,7},{4,0},{5,1},{6,2},{7,3},{8,12},{9,13},{10,... | collective-permute-start | bytes 847880 | tf_op jit(solution)/shard_map/ppermute | solution.py:508
  59.1 31.4 %collective-permute-start.5 = (f32[552,128]{1,0:T(8,128)S(1)}, f32[552,128]{1,0:T(8,128)S(1)}, u32[]{:S(2)}, u32[]{:S(2)}) collective-permute-start(f32[552,128]{1,0:T(8,128)S(1)} %get-tuple-element.86), channel_id=1, source_target_pairs={{0,6},{1,7},{2,4},{3,5},{4,2},{5,3},{6,0},{7,1},{8,14},{9,15},{10,... | collective-permute-start | bytes 847880 | tf_op jit(solution)/shard_map/ppermute | solution.py:508
  59.6 16.9 %collective-permute-start.6 = (f32[184,128]{1,0:T(8,128)S(1)}, f32[184,128]{1,0:T(8,128)S(1)}, u32[]{:S(2)}, u32[]{:S(2)}) collective-permute-start(f32[184,128]{1,0:T(8,128)S(1)} %get-tuple-element.87), channel_id=1, source_target_pairs={{0,9},{1,8},{2,11},{3,10},{4,13},{5,12},{6,15},{7,14},{8,1},{9,0},... | collective-permute-start | bytes 282632 | tf_op jit(solution)/shard_map/ppermute | solution.py:508
  59.6 19.9 %collective-permute-start.7 = (f32[184,128]{1,0:T(8,128)S(1)}, f32[184,128]{1,0:T(8,128)S(1)}, u32[]{:S(2)}, u32[]{:S(2)}) collective-permute-start(f32[184,128]{1,0:T(8,128)S(1)} %get-tuple-element.88), channel_id=1, source_target_pairs={{0,11},{1,10},{2,9},{3,8},{4,15},{5,14},{6,13},{7,12},{8,3},{9,2},... | collective-permute-start | bytes 282632 | tf_op jit(solution)/shard_map/ppermute | solution.py:508
  76.5 6.2 %collective-permute-start.8 = (f32[184,128]{1,0:T(8,128)S(1)}, f32[184,128]{1,0:T(8,128)S(1)}, u32[]{:S(2)}, u32[]{:S(2)}) collective-permute-start(f32[184,128]{1,0:T(8,128)S(1)} %get-tuple-element.89), channel_id=1, source_target_pairs={{0,13},{1,12},{2,15},{3,14},{4,9},{5,8},{6,11},{7,10},{8,5},{9,4},... | collective-permute-start | bytes 282632 | tf_op jit(solution)/shard_map/ppermute | solution.py:508
  79.4 6.8 %collective-permute-start.9 = (f32[184,128]{1,0:T(8,128)S(1)}, f32[184,128]{1,0:T(8,128)S(1)}, u32[]{:S(2)}, u32[]{:S(2)}) collective-permute-start(f32[184,128]{1,0:T(8,128)S(1)} %get-tuple-element.90), channel_id=1, source_target_pairs={{0,15},{1,14},{2,13},{3,12},{4,11},{5,10},{6,9},{7,8},{8,7},{9,6},... | collective-permute-start | bytes 282632 | tf_op jit(solution)/shard_map/ppermute | solution.py:508

commit v7 on v5

--- a/solution.py
+++ b/solution.py
@@ -159,7 +159,7 @@
 
 
 def row_blocks(rows, span):
-    pieces = 4 * span // LANES
+    pieces = 2 * span // LANES
     cuts = [rows // 16 * i // pieces * 16 for i in range(pieces + 1)]
     return [slice(top, end) for top, end in zip(cuts, cuts[1:])]
 

time: 94.5 us -> 96 us (1.016)
  Pallas kernels: 46.3 us -> 47.8 us
    pallas_call x4, Pallas kernels: 31.6 us -> 33.1 us  [shards(): pl.pallas_call(functools.partial(solve_kernel, 1.0 / math.sqrt(comps * no...]
  transfers between devices with their start and end apart: 11 -> 11, of which waited for: 2 -> 2; matrix products, arithmetic and copies ran while one was open for 0% -> 0% of each run, Pallas kernels for 32% -> 33%
where the time goes in v7:
time: 96 us; the launch traced here: 95.7 us
  Pallas kernels  47.8 us (50%)
  waiting for transfers between devices  24.8 us (26%)
  starting transfers between devices  22.2 us (23%)
    pallas_call x4, Pallas kernels, shards(): pl.pallas_call(functools.partial(solve_kernel, 1.0 / math.sqrt(comps * no...  33.1 us
    ppermute x10, starting transfers between devices, hop(): return lax.ppermute(sent, axes, [(s, s ^ mask) for s in range(devices)])  16.2 us
    ppermute x10, waiting for transfers between devices, hop(): return lax.ppermute(sent, axes, [(s, s ^ mask) for s in range(devices)])  14.9 us
    all_to_all x1, waiting for transfers between devices, shards(): lax.all_to_all(pair.reshape(2 * lanes, tall, LANES), axes, split_axis=0,...  9.91 us
    all_to_all x1, starting transfers between devices, shards(): lax.all_to_all(pair.reshape(2 * lanes, tall, LANES), axes, split_axis=0,...  6.04 us
    pallas_call x1, Pallas kernels, shards(): pl.pallas_call(functools.partial(prep_kernel, devices, per_peer, comps, v...  4.68 us
    pallas_call x1, Pallas kernels, shards(): pl.pallas_call(functools.partial(ship_kernel, devices, per_peer, nodes, 2...  3.02 us
    pallas_call x1, Pallas kernels, shards(): pl.pallas_call(functools.partial(land_pair, devices, per_peer), out_shape...  2.8 us
  transfers between devices with their start and end apart: 11, of which 2 were waited for; matrix products, arithmetic and copies ran while one was open for 0% of the time, Pallas kernels for 33%

profile of v7, /device:TPU:8, one launch (start us, length us, event | category | flops | bytes accessed | tf_op | source)
XLA Modules:
  0.0 95.7 jit_solution(13482467460052997197)
XLA Ops:
  0.6 1.7 %shard_map.104.refs_0_ = f32[8192,729]{1,0:T(8,128)} custom-call(f32[3,6,729]{2,1,0:T(8,128)} %coupling.1, f32[3,729]{1,0:T(4,128)} %plastic.1, f32[6,512]{1,0:T(8,128)} %strain.1, s32[1,512]{1,0:T(1,128)} %bitcast.3, s32[1,512]{1,0:T(1,128)} %qp.1, s32[9,9]{1,0:T(8,128)} %pattern.1), custom_call_target="tpu_custom_call" | custom-call | tf_op jit(solution)/shard_map/pallas_call | solution.py:423
  2.4 4.7 %shard_map.105 = (bf16[736,768]{1,0:T(8,128)(2,1)S(1)}, bf16[736,768]{1,0:T(8,128)(2,1)S(1)}, f32[736,512]{1,0:T(8,128)S(1)}, f32[736,512]{1,0:T(8,128)S(1)}, f3...) custom-call(f32[8192,729]{1,0:T(8,128)} %shard_map.104.refs_0_, ...), custom_call_target="tpu_custom_call" | custom-call | tf_op jit(solution)/shard_map/pallas_call | solution.py:432
  7.1 8.3 %shard_map.106 = (f32[736,128]{1,0:T(8,128)S(1)}, f32[8,128]{1,0:T(8,128)S(1)}, f32[736,128]{1,0:T(8,128)S(1)}) custom-call(bf16[736,768]{1,0:T(8,128)(2,1)S(1)} %get-tuple-element.47.khi, bf16[736,768]{1,0:T(8,128)(2,1)S(1)} %get-tuple-element.48.klo, f32[736,512]{1,0:T(8,128)S(1)} %get-tuple-element.49.hist, f32[736,512]{1,0:T(8,128)S(1)} %get-tuple-element.50.weight, ...), custom_call_target="tpu_custom_call" | custom-call | flops 3906994176 | bytes 1048576 | tf_op jit(solution)/shard_map/pallas_call | solution.py:467
  15.3 2.7 %collective-permute-start = (f32[736,128]{1,0:T(8,128)S(1)}, f32[736,128]{1,0:T(8,128)S(1)}, u32[]{:S(2)}, u32[]{:S(2)}) collective-permute-start(f32[736,128]{1,0:T(8,128)S(1)} %get-tuple-element.63), channel_id=1, source_target_pairs={{0,16},{1,17},{2,18},{3,19},{4,20},{5,21},{6,22},{7,23},{8,24},{9,... | collective-permute-start | bytes 1130504 | tf_op jit(solution)/shard_map/ppermute | solution.py:508
  18.0 8.2 %shard_map.107 = (f32[736,128]{1,0:T(8,128)S(1)}, f32[8,128]{1,0:T(8,128)S(1)}, f32[736,128]{1,0:T(8,128)S(1)}) custom-call(bf16[736,768]{1,0:T(8,128)(2,1)S(1)} %get-tuple-element.47.khi, bf16[736,768]{1,0:T(8,128)(2,1)S(1)} %get-tuple-element.48.klo, f32[736,512]{1,0:T(8,128)S(1)} %get-tuple-element.49.hist, f32[736,512]{1,0:T(8,128)S(1)} %get-tuple-element.50.weight, ...), custom_call_target="tpu_custom_call" | custom-call | flops 3906994176 | bytes 1048576 | tf_op jit(solution)/shard_map/pallas_call | solution.py:467
  26.2 0.5 collective-permute-start.1
  26.7 8.4 %shard_map.108 = (f32[736,128]{1,0:T(8,128)S(1)}, f32[8,128]{1,0:T(8,128)S(1)}, f32[736,128]{1,0:T(8,128)S(1)}) custom-call(bf16[736,768]{1,0:T(8,128)(2,1)S(1)} %get-tuple-element.47.khi, bf16[736,768]{1,0:T(8,128)(2,1)S(1)} %get-tuple-element.48.klo, f32[736,512]{1,0:T(8,128)S(1)} %get-tuple-element.49.hist, f32[736,512]{1,0:T(8,128)S(1)} %get-tuple-element.50.weight, ...), custom_call_target="tpu_custom_call" | custom-call | flops 3906994176 | bytes 1048576 | tf_op jit(solution)/shard_map/pallas_call | solution.py:467
  35.0 0.1 collective-permute-start.2
  35.1 8.3 %shard_map.109 = (f32[736,128]{1,0:T(8,128)S(1)}, f32[8,128]{1,0:T(8,128)S(1)}, f32[184,128]{1,0:T(8,128)S(1)}, f32[184,128]{1,0:T(8,128)S(1)}, f32[184,128]{1,0:T(8,128)S(1)}, /*index=5*/f32[184,128]{1,0:T(8,128)S(1)}) custom-call(bf16[736,768]{1,0:T(8,128)(2,1)S(1)} %get-tuple-element.47.khi, bf16[736,768]{1,0:T(8,128)(2,1)S(1)} %get-tuple-element.48.klo, ...), custom_call_target="tpu_custom_call" | custom-call | flops 3906994176 | bytes 1048576 | tf_op jit(solution)/shard_map/pallas_call | solution.py:467
  43.4 3.0 %shard_map.112 = f32[2944,128]{1,0:T(8,128)} custom-call(s32[8,512]{1,0:T(8,128)S(1)} %get-tuple-element.55.place, f32[736,128]{1,0:T(8,128)S(1)} %get-tuple-element.57.refs_0_, f32[736,128]{1,0:T(8,128)S(1)} %get-tuple-element.59.refs_1_, f32[736,128]{1,0:T(8,128)S(1)} %get-tuple-element.61.refs_2_, f32[736,128]{1,0:T(8,128)S(1)} %get-tuple-element.81.refs_3_), custom_call_target="tpu_custom_call" | custom-call | flops 771751936 | bytes 1048576 | tf_op jit(solution)/shard_map/pallas_call | solution.py:494
  46.4 6.0 %all-to-all-start = ((f32[16,184,128]{2,1,0:T(8,128)}), f32[16,184,128]{2,1,0:T(8,128)}, u32[]{:S(2)}, u32[]{:S(2)}) async-start(f32[16,184,128]{2,1,0:T(8,128)} %bitcast.1), calls=%async_computation | async-start | bytes 3014656 | tf_op jit(solution)/shard_map/all_to_all | solution.py:512
  52.5 0.1 shard_map.110
  52.5 1.9 %collective-permute-start.3 = (f32[552,128]{1,0:T(8,128)S(1)}, f32[552,128]{1,0:T(8,128)S(1)}, u32[]{:S(2)}, u32[]{:S(2)}) collective-permute-start(f32[552,128]{1,0:T(8,128)S(1)} %get-tuple-element.78), channel_id=1, source_target_pairs={{0,2},{1,3},{2,0},{3,1},{4,6},{5,7},{6,4},{7,5},{8,10},{9,11},{10,... | collective-permute-start | bytes 847880 | tf_op jit(solution)/shard_map/ppermute | solution.py:508
  54.5 1.5 %collective-permute-start.4 = (f32[552,128]{1,0:T(8,128)S(1)}, f32[552,128]{1,0:T(8,128)S(1)}, u32[]{:S(2)}, u32[]{:S(2)}) collective-permute-start(f32[552,128]{1,0:T(8,128)S(1)} %get-tuple-element.79), channel_id=1, source_target_pairs={{0,4},{1,5},{2,6},{3,7},{4,0},{5,1},{6,2},{7,3},{8,12},{9,13},{10,... | collective-permute-start | bytes 847880 | tf_op jit(solution)/shard_map/ppermute | solution.py:508
  56.0 0.2 collective-permute-start.5
  56.1 2.4 %collective-permute-start.6 = (f32[184,128]{1,0:T(8,128)S(1)}, f32[184,128]{1,0:T(8,128)S(1)}, u32[]{:S(2)}, u32[]{:S(2)}) collective-permute-start(f32[184,128]{1,0:T(8,128)S(1)} %get-tuple-element.86), channel_id=1, source_target_pairs={{0,9},{1,8},{2,11},{3,10},{4,13},{5,12},{6,15},{7,14},{8,1},{9,0},... | collective-permute-start | bytes 282632 | tf_op jit(solution)/shard_map/ppermute | solution.py:508
  58.5 1.0 %collective-permute-start.7 = (f32[184,128]{1,0:T(8,128)S(1)}, f32[184,128]{1,0:T(8,128)S(1)}, u32[]{:S(2)}, u32[]{:S(2)}) collective-permute-start(f32[184,128]{1,0:T(8,128)S(1)} %get-tuple-element.87), channel_id=1, source_target_pairs={{0,11},{1,10},{2,9},{3,8},{4,15},{5,14},{6,13},{7,12},{8,3},{9,2},... | collective-permute-start | bytes 282632 | tf_op jit(solution)/shard_map/ppermute | solution.py:508
  59.5 14.9 %collective-permute-done.6.refs_4_ = f32[184,128]{1,0:T(8,128)S(1)} collective-permute-done((f32[184,128]{1,0:T(8,128)S(1)}, f32[184,128]{1,0:T(8,128)S(1)}, u32[]{:S(2)}, u32[]{:S(2)}) %collective-permute-start.6) | collective-permute-done | bytes 94240 | tf_op jit(solution)/shard_map/ppermute | solution.py:508
  74.4 3.1 %collective-permute-start.8 = (f32[184,128]{1,0:T(8,128)S(1)}, f32[184,128]{1,0:T(8,128)S(1)}, u32[]{:S(2)}, u32[]{:S(2)}) collective-permute-start(f32[184,128]{1,0:T(8,128)S(1)} %get-tuple-element.88), channel_id=1, source_target_pairs={{0,13},{1,12},{2,15},{3,14},{4,9},{5,8},{6,11},{7,10},{8,5},{9,4},... | collective-permute-start | bytes 282632 | tf_op jit(solution)/shard_map/ppermute | solution.py:508
  77.4 3.0 %collective-permute-start.9 = (f32[184,128]{1,0:T(8,128)S(1)}, f32[184,128]{1,0:T(8,128)S(1)}, u32[]{:S(2)}, u32[]{:S(2)}) collective-permute-start(f32[184,128]{1,0:T(8,128)S(1)} %get-tuple-element.89), channel_id=1, source_target_pairs={{0,15},{1,14},{2,13},{3,12},{4,11},{5,10},{6,9},{7,8},{8,7},{9,6},... | collective-permute-start | bytes 282632 | tf_op jit(solution)/shard_map/ppermute | solution.py:508
  80.4 0.9 shard_map.111
  81.3 9.9 %all-to-all-done = f32[16,184,128]{2,1,0:T(8,128)} async-done(((f32[16,184,128]{2,1,0:T(8,128)}), f32[16,184,128]{2,1,0:T(8,128)}, u32[]{:S(2)}, u32[]{:S(2)}) %all-to-all-start) | async-done | bytes 1507360 | tf_op jit(solution)/shard_map/all_to_all | solution.py:512
  91.2 2.8 %shard_map.113.refs_8_ = f32[729,1024]{1,0:T(8,128)} custom-call(f32[2944,128]{1,0:T(8,128)} %bitcast.2.pair), custom_call_target="tpu_custom_call" | custom-call | tf_op jit(solution)/shard_map/pallas_call | solution.py:544
  94.1 1.5 %shard_map.114 = f32[729,1024]{1,0:T(8,128)} custom-call(f32[552,128]{1,0:T(8,128)S(1)} %get-tuple-element.77.refs_0_, f32[552,128]{1,0:T(8,128)S(1)} %collective-permute-done.3.refs_1_, f32[552,128]{1,0:T(8,128)S(1)} %collective-permute-done.4.refs_2_, f32[552,128]{1,0:T(8,128)S(1)} %collective-permute-done.5.refs_3_, ...), custom_call_target="tpu_custom_call", output_to_operand_aliasing={{}: (8, {})} | custom-call | tf_op jit(solution)/shard_map/pallas_call | solution.py:552
  (9 shorter events, 0.0 us)
Async XLA Ops:
  15.3 37.1 %collective-permute-start = (f32[736,128]{1,0:T(8,128)S(1)}, f32[736,128]{1,0:T(8,128)S(1)}, u32[]{:S(2)}, u32[]{:S(2)}) collective-permute-start(f32[736,128]{1,0:T(8,128)S(1)} %get-tuple-element.63), channel_id=1, source_target_pairs={{0,16},{1,17},{2,18},{3,19},{4,20},{5,21},{6,22},{7,23},{8,24},{9,... | collective-permute-start | bytes 1130504 | tf_op jit(solution)/shard_map/ppermute | solution.py:508
  26.2 26.3 %collective-permute-start.1 = (f32[736,128]{1,0:T(8,128)S(1)}, f32[736,128]{1,0:T(8,128)S(1)}, u32[]{:S(2)}, u32[]{:S(2)}) collective-permute-start(f32[736,128]{1,0:T(8,128)S(1)} %get-tuple-element.64), channel_id=1, source_target_pairs={{0,8},{1,9},{2,10},{3,11},{4,12},{5,13},{6,14},{7,15},{8,0},{9,1},... | collective-permute-start | bytes 1130504 | tf_op jit(solution)/shard_map/ppermute | solution.py:508
  35.0 17.4 %collective-permute-start.2 = (f32[736,128]{1,0:T(8,128)S(1)}, f32[736,128]{1,0:T(8,128)S(1)}, u32[]{:S(2)}, u32[]{:S(2)}) collective-permute-start(f32[736,128]{1,0:T(8,128)S(1)} %get-tuple-element.67), channel_id=1, source_target_pairs={{0,17},{1,16},{2,19},{3,18},{4,21},{5,20},{6,23},{7,22},{8,25},{9,... | collective-permute-start | bytes 1130504 | tf_op jit(solution)/shard_map/ppermute | solution.py:508
  46.4 44.8 %all-to-all-start = ((f32[16,184,128]{2,1,0:T(8,128)}), f32[16,184,128]{2,1,0:T(8,128)}, u32[]{:S(2)}, u32[]{:S(2)}) async-start(f32[16,184,128]{2,1,0:T(8,128)} %bitcast.1), calls=%async_computation | async-start | bytes 3014656 | tf_op jit(solution)/shard_map/all_to_all | solution.py:512
  52.5 41.5 %collective-permute-start.3 = (f32[552,128]{1,0:T(8,128)S(1)}, f32[552,128]{1,0:T(8,128)S(1)}, u32[]{:S(2)}, u32[]{:S(2)}) collective-permute-start(f32[552,128]{1,0:T(8,128)S(1)} %get-tuple-element.78), channel_id=1, source_target_pairs={{0,2},{1,3},{2,0},{3,1},{4,6},{5,7},{6,4},{7,5},{8,10},{9,11},{10,... | collective-permute-start | bytes 847880 | tf_op jit(solution)/shard_map/ppermute | solution.py:508
  54.5 39.5 %collective-permute-start.4 = (f32[552,128]{1,0:T(8,128)S(1)}, f32[552,128]{1,0:T(8,128)S(1)}, u32[]{:S(2)}, u32[]{:S(2)}) collective-permute-start(f32[552,128]{1,0:T(8,128)S(1)} %get-tuple-element.79), channel_id=1, source_target_pairs={{0,4},{1,5},{2,6},{3,7},{4,0},{5,1},{6,2},{7,3},{8,12},{9,13},{10,... | collective-permute-start | bytes 847880 | tf_op jit(solution)/shard_map/ppermute | solution.py:508
  56.0 38.1 %collective-permute-start.5 = (f32[552,128]{1,0:T(8,128)S(1)}, f32[552,128]{1,0:T(8,128)S(1)}, u32[]{:S(2)}, u32[]{:S(2)}) collective-permute-start(f32[552,128]{1,0:T(8,128)S(1)} %get-tuple-element.80), channel_id=1, source_target_pairs={{0,6},{1,7},{2,4},{3,5},{4,2},{5,3},{6,0},{7,1},{8,14},{9,15},{10,... | collective-permute-start | bytes 847880 | tf_op jit(solution)/shard_map/ppermute | solution.py:508
  56.1 18.2 %collective-permute-start.6 = (f32[184,128]{1,0:T(8,128)S(1)}, f32[184,128]{1,0:T(8,128)S(1)}, u32[]{:S(2)}, u32[]{:S(2)}) collective-permute-start(f32[184,128]{1,0:T(8,128)S(1)} %get-tuple-element.86), channel_id=1, source_target_pairs={{0,9},{1,8},{2,11},{3,10},{4,13},{5,12},{6,15},{7,14},{8,1},{9,0},... | collective-permute-start | bytes 282632 | tf_op jit(solution)/shard_map/ppermute | solution.py:508
  58.5 18.9 %collective-permute-start.7 = (f32[184,128]{1,0:T(8,128)S(1)}, f32[184,128]{1,0:T(8,128)S(1)}, u32[]{:S(2)}, u32[]{:S(2)}) collective-permute-start(f32[184,128]{1,0:T(8,128)S(1)} %get-tuple-element.87), channel_id=1, source_target_pairs={{0,11},{1,10},{2,9},{3,8},{4,15},{5,14},{6,13},{7,12},{8,3},{9,2},... | collective-permute-start | bytes 282632 | tf_op jit(solution)/shard_map/ppermute | solution.py:508
  74.4 19.6 %collective-permute-start.8 = (f32[184,128]{1,0:T(8,128)S(1)}, f32[184,128]{1,0:T(8,128)S(1)}, u32[]{:S(2)}, u32[]{:S(2)}) collective-permute-start(f32[184,128]{1,0:T(8,128)S(1)} %get-tuple-element.88), channel_id=1, source_target_pairs={{0,13},{1,12},{2,15},{3,14},{4,9},{5,8},{6,11},{7,10},{8,5},{9,4},... | collective-permute-start | bytes 282632 | tf_op jit(solution)/shard_map/ppermute | solution.py:508
  77.4 16.6 %collective-permute-start.9 = (f32[184,128]{1,0:T(8,128)S(1)}, f32[184,128]{1,0:T(8,128)S(1)}, u32[]{:S(2)}, u32[]{:S(2)}) collective-permute-start(f32[184,128]{1,0:T(8,128)S(1)} %get-tuple-element.89), channel_id=1, source_target_pairs={{0,15},{1,14},{2,13},{3,12},{4,11},{5,10},{6,9},{7,8},{8,7},{9,6},... | collective-permute-start | bytes 282632 | tf_op jit(solution)/shard_map/ppermute | solution.py:508
